TPU v7x, 256 devices: a whole 4x4x8 slice. The times are simulated.
256 devices in a mesh: section: 4 (over x), expert: 64 (over y, z, core).
Axes of the slice: x: 4, y: 4, z: 8, core: 2. Of those that a mesh axis runs over, the one named last changes fastest.
Arguments:
- tokens: bfloat16 [8, 1024, 2048], P('section', 'expert'), may hold values from -6 to 6
- norm_gain: float32 [4, 2048], P('section'), may hold values from 0.1 to 1.9
- gate_proj: bfloat16 [4, 64, 2048, 768], P('section', 'expert'), may hold values from -0.125 to 0.125
- up_proj: bfloat16 [4, 64, 2048, 768], P('section', 'expert'), may hold values from -0.125 to 0.125
- down_proj: bfloat16 [4, 64, 768, 2048], P('section', 'expert'), may hold values from -0.21875 to 0.21875
- expert_ids: int32 [4, 8, 1024, 8], P('section', None, 'expert'), may hold values from 0 to 63, all different within a row; in each aligned block of 16 rows (0 to 15, 16 to 31, ..., all dimensions but the last counted through in order) at most 2 rows name the same one
- gate_weights: float32 [4, 8, 1024, 8], P('section', None, 'expert'), may hold values from 0.05 to 1
Outputs:
- finished: bfloat16 [8, 1024, 2048], P('section', 'expert')
Inputs may be any that keep to these rules, and one draw needn't show every extreme that they name: `expert_ids`: each row names 8 different experts. In each aligned block of 16 rows (one device's rows of one layer and micro-batch) no expert is named by more than 2 rows, and in some block one expert is named by exactly 2 rows.
All inputs are finite; a program needn't handle non-finite values.
Results may differ from a plain program's by a relative error of at most 0.015.
Values may be sent and summed in bfloat16 or wider, within the bound.
No kernel may reach another device: no remote copies, remote signals or barrier semaphores. Data moves between devices by JAX's collectives and lax.ppermute only.
A program may use at most 64 MiB of HBM per device.

v0:
```python
import jax
import jax.numpy as jnp
from jax import lax
from jax.sharding import PartitionSpec as P

TOP = 8


EPSILON = 1e-06


def shifted(block, axis, distance):
    devices = range(lax.axis_size(axis))
    route = [((i - distance) % len(devices), i) for i in devices]
    return lax.ppermute(block, axis, route)


def rms_normed(hidden, norm_scale):
    values = hidden.astype(jnp.float32)
    inverse_rms = lax.rsqrt(jnp.mean(values * values, axis=-1, keepdims=True) + EPSILON)
    return (values * inverse_rms * norm_scale).astype(jnp.bfloat16)


def slot_tables(routed, expert_count, capacity):
    row_count, pick_count = routed.shape
    expert_hot = (routed[:, :, None] == jnp.arange(expert_count, dtype=jnp.int32)).astype(jnp.int32)
    flattened = expert_hot.reshape(row_count * pick_count, expert_count)
    earlier = jnp.cumsum(flattened, axis=0) - flattened
    position = jnp.sum(earlier * flattened, axis=1).reshape(row_count, pick_count)
    slot_hot = (position[:, :, None] == jnp.arange(capacity, dtype=jnp.int32)).astype(jnp.bfloat16)
    placing = jnp.einsum(
        "rke,rkc->ecr",
        expert_hot.astype(jnp.bfloat16),
        slot_hot,
        preferred_element_type=jnp.float32,
    )
    return (placing.astype(jnp.bfloat16), position)


def expert_ffn(received, w_gate, w_up, w_down):
    sources, slot_count, feature_count = received.shape
    flattened = received.reshape(sources * slot_count, feature_count)
    gate_part = jnp.dot(flattened, w_gate, preferred_element_type=jnp.float32)
    upward = jnp.dot(flattened, w_up, preferred_element_type=jnp.float32)
    activated = (jax.nn.silu(gate_part) * upward).astype(jnp.bfloat16)
    projected = jnp.dot(activated, w_down, preferred_element_type=jnp.float32).astype(jnp.bfloat16)
    return projected.reshape(sources, slot_count, feature_count)


def combine_rows(returned, routed, position, weights):
    expert_count, slot_count, feature_count = returned.shape
    flattened = returned.reshape(expert_count * slot_count, feature_count)
    slot_index = (routed * slot_count + position).reshape(-1)
    picked = jnp.take(flattened, slot_index, axis=0).reshape(
        routed.shape[0], routed.shape[1], feature_count
    )
    return jnp.sum(picked.astype(jnp.float32) * weights[:, :, None], axis=1)


def on_device(tokens, norm_gain, gate_proj, up_proj, down_proj, expert_ids, gate_weights):
    sections = lax.axis_size("section")
    peer_count = lax.axis_size("expert")
    row_count = tokens.shape[1]
    micro_count = expert_ids.shape[1]
    expert_count = peer_count * gate_proj.shape[1]
    capacity = max(2, (row_count * TOP + expert_count - 1) // expert_count)
    section_index = lax.axis_index("section")
    w_gate = gate_proj[0, 0]
    w_up = up_proj[0, 0]
    w_down = down_proj[0, 0]
    norm_scale = norm_gain[0]

    def advance_moment(moment, streams):
        hidden, waiting = streams
        at_entry = jnp.logical_and(
            section_index == 0, jnp.logical_and(moment >= sections, moment < micro_count)
        )
        hidden, waiting = (
            jnp.where(at_entry, waiting, hidden),
            jnp.where(at_entry, hidden, waiting),
        )
        offset = moment - section_index
        micro_index = jnp.clip(offset, 0, micro_count - 1)
        active = jnp.logical_and(offset >= 0, offset < micro_count)
        routed = lax.dynamic_index_in_dim(expert_ids[0], micro_index, 0, keepdims=False)
        raw_weights = lax.dynamic_index_in_dim(gate_weights[0], micro_index, 0, keepdims=False)
        weights = raw_weights / jnp.sum(raw_weights, axis=-1, keepdims=True)
        normed = rms_normed(hidden, norm_scale)
        placing, position = slot_tables(routed, expert_count, capacity)
        outgoing = jnp.einsum(
            "ecr,rd->ecd", placing, normed, preferred_element_type=jnp.float32
        ).astype(jnp.bfloat16)

        def compute_rows(received_rows):
            return expert_ffn(received_rows, w_gate, w_up, w_down)

        received = lax.all_to_all(outgoing, "expert", split_axis=0, concat_axis=0, tiled=True)
        returned = lax.all_to_all(
            lax.cond(active, compute_rows, jnp.zeros_like, received),
            "expert",
            split_axis=0,
            concat_axis=0,
            tiled=True,
        )
        mixed_rows = hidden.astype(jnp.float32) + combine_rows(returned, routed, position, weights)
        updated = jnp.where(active, mixed_rows.astype(jnp.bfloat16), hidden)
        return shifted((updated, waiting), "section", 1)

    hidden, waiting = lax.fori_loop(
        0, micro_count + sections - 1, advance_moment, (tokens[0], tokens[1])
    )
    return jnp.stack([hidden, waiting])


def solution(mesh):
    return jax.shard_map(
        on_device,
        mesh=mesh,
        in_specs=(
            P("section", "expert", None),
            P("section", None),
            P("section", "expert", None, None),
            P("section", "expert", None, None),
            P("section", "expert", None, None),
            P("section", None, "expert", None),
            P("section", None, "expert", None),
        ),
        out_specs=P("section", "expert", None),
        check_vma=False,
    )
```

profile of v0, /device:TPU:1, one launch (start us, length us, event | category | flops | bytes accessed | tf_op | source)
XLA Modules:
  0.0 764.4 jit_solution(18231443014789289442)
XLA Ops:
  0.9 762.8 %while.16 = (s32[]{:T(128)}, bf16[16,2048]{1,0:T(8,128)(2,1)S(1)}, bf16[16,2048]{1,0:T(8,128)(2,1)S(1)}, s32[]{:T(128)}, pred[]{:T(512)}, /*index=5*/s32[1,8,16,...) while((s32[]{:T(128)}, bf16[16,2048]{1,0:T(8,128)(2,1)S(1)}, ...), condition=%wide.region_8.9_spmd, body=%wide.region_0.8_spmd.sunk | while | flops 1220064256 | bytes 37460844 | solution.py:109
  5.3 13.3 %all-to-all-start = ((bf16[64,2,2048]{2,1,0:T(2,128)(2,1)}), bf16[64,2,2048]{2,1,0:T(2,128)(2,1)}, u32[]{:S(2)}, u32[]{:S(2)}) async-start(bf16[64,2,2048]{2,1,0:T(2,128)(2,1)} %copy.43), calls=%async_computation | async-start | bytes 1048576 | tf_op jit(solution)/shard_map/while/body/eval_jaxpr/all_to_all | solution.py:97
  18.7 17.2 %all-to-all-done = bf16[64,2,2048]{2,1,0:T(2,128)(2,1)} async-done(((bf16[64,2,2048]{2,1,0:T(2,128)(2,1)}), bf16[64,2,2048]{2,1,0:T(2,128)(2,1)}, u32[]{:S(2)}, u32[]{:S(2)}) %all-to-all-start) | async-done | bytes 524320 | tf_op jit(solution)/shard_map/while/body/eval_jaxpr/all_to_all | solution.py:97
  54.1 15.4 %all-to-all-done.1 = bf16[64,2,2048]{2,1,0:T(2,128)(2,1)S(1)} async-done(((bf16[64,2,2048]{2,1,0:T(2,128)(2,1)}), bf16[64,2,2048]{2,1,0:T(2,128)(2,1)S(1)}, u32[]{:S(2)}, u32[]{:S(2)}) %all-to-all-start.1) | async-done | bytes 524320 | tf_op jit(solution)/shard_map/while/body/eval_jaxpr/all_to_all | solution.py:98
  88.0 17.2 %all-to-all-done = bf16[64,2,2048]{2,1,0:T(2,128)(2,1)} async-done(((bf16[64,2,2048]{2,1,0:T(2,128)(2,1)}), bf16[64,2,2048]{2,1,0:T(2,128)(2,1)}, u32[]{:S(2)}, u32[]{:S(2)}) %all-to-all-start) | async-done | bytes 524320 | tf_op jit(solution)/shard_map/while/body/eval_jaxpr/all_to_all | solution.py:97
  123.4 15.4 %all-to-all-done.1 = bf16[64,2,2048]{2,1,0:T(2,128)(2,1)S(1)} async-done(((bf16[64,2,2048]{2,1,0:T(2,128)(2,1)}), bf16[64,2,2048]{2,1,0:T(2,128)(2,1)S(1)}, u32[]{:S(2)}, u32[]{:S(2)}) %all-to-all-start.1) | async-done | bytes 524320 | tf_op jit(solution)/shard_map/while/body/eval_jaxpr/all_to_all | solution.py:98
  157.2 17.2 %all-to-all-done = bf16[64,2,2048]{2,1,0:T(2,128)(2,1)} async-done(((bf16[64,2,2048]{2,1,0:T(2,128)(2,1)}), bf16[64,2,2048]{2,1,0:T(2,128)(2,1)}, u32[]{:S(2)}, u32[]{:S(2)}) %all-to-all-start) | async-done | bytes 524320 | tf_op jit(solution)/shard_map/while/body/eval_jaxpr/all_to_all | solution.py:97
  192.6 15.4 %all-to-all-done.1 = bf16[64,2,2048]{2,1,0:T(2,128)(2,1)S(1)} async-done(((bf16[64,2,2048]{2,1,0:T(2,128)(2,1)}), bf16[64,2,2048]{2,1,0:T(2,128)(2,1)S(1)}, u32[]{:S(2)}, u32[]{:S(2)}) %all-to-all-start.1) | async-done | bytes 524320 | tf_op jit(solution)/shard_map/while/body/eval_jaxpr/all_to_all | solution.py:98
  226.5 17.2 %all-to-all-done = bf16[64,2,2048]{2,1,0:T(2,128)(2,1)} async-done(((bf16[64,2,2048]{2,1,0:T(2,128)(2,1)}), bf16[64,2,2048]{2,1,0:T(2,128)(2,1)}, u32[]{:S(2)}, u32[]{:S(2)}) %all-to-all-start) | async-done | bytes 524320 | tf_op jit(solution)/shard_map/while/body/eval_jaxpr/all_to_all | solution.py:97
  261.9 15.4 %all-to-all-done.1 = bf16[64,2,2048]{2,1,0:T(2,128)(2,1)S(1)} async-done(((bf16[64,2,2048]{2,1,0:T(2,128)(2,1)}), bf16[64,2,2048]{2,1,0:T(2,128)(2,1)S(1)}, u32[]{:S(2)}, u32[]{:S(2)}) %all-to-all-start.1) | async-done | bytes 524320 | tf_op jit(solution)/shard_map/while/body/eval_jaxpr/all_to_all | solution.py:98
  295.8 17.2 %all-to-all-done = bf16[64,2,2048]{2,1,0:T(2,128)(2,1)} async-done(((bf16[64,2,2048]{2,1,0:T(2,128)(2,1)}), bf16[64,2,2048]{2,1,0:T(2,128)(2,1)}, u32[]{:S(2)}, u32[]{:S(2)}) %all-to-all-start) | async-done | bytes 524320 | tf_op jit(solution)/shard_map/while/body/eval_jaxpr/all_to_all | solution.py:97
  331.2 15.4 %all-to-all-done.1 = bf16[64,2,2048]{2,1,0:T(2,128)(2,1)S(1)} async-done(((bf16[64,2,2048]{2,1,0:T(2,128)(2,1)}), bf16[64,2,2048]{2,1,0:T(2,128)(2,1)S(1)}, u32[]{:S(2)}, u32[]{:S(2)}) %all-to-all-start.1) | async-done | bytes 524320 | tf_op jit(solution)/shard_map/while/body/eval_jaxpr/all_to_all | solution.py:98
  365.1 17.2 %all-to-all-done = bf16[64,2,2048]{2,1,0:T(2,128)(2,1)} async-done(((bf16[64,2,2048]{2,1,0:T(2,128)(2,1)}), bf16[64,2,2048]{2,1,0:T(2,128)(2,1)}, u32[]{:S(2)}, u32[]{:S(2)}) %all-to-all-start) | async-done | bytes 524320 | tf_op jit(solution)/shard_map/while/body/eval_jaxpr/all_to_all | solution.py:97
  400.5 15.4 %all-to-all-done.1 = bf16[64,2,2048]{2,1,0:T(2,128)(2,1)S(1)} async-done(((bf16[64,2,2048]{2,1,0:T(2,128)(2,1)}), bf16[64,2,2048]{2,1,0:T(2,128)(2,1)S(1)}, u32[]{:S(2)}, u32[]{:S(2)}) %all-to-all-start.1) | async-done | bytes 524320 | tf_op jit(solution)/shard_map/while/body/eval_jaxpr/all_to_all | solution.py:98
  434.4 17.2 %all-to-all-done = bf16[64,2,2048]{2,1,0:T(2,128)(2,1)} async-done(((bf16[64,2,2048]{2,1,0:T(2,128)(2,1)}), bf16[64,2,2048]{2,1,0:T(2,128)(2,1)}, u32[]{:S(2)}, u32[]{:S(2)}) %all-to-all-start) | async-done | bytes 524320 | tf_op jit(solution)/shard_map/while/body/eval_jaxpr/all_to_all | solution.py:97
  469.8 15.4 %all-to-all-done.1 = bf16[64,2,2048]{2,1,0:T(2,128)(2,1)S(1)} async-done(((bf16[64,2,2048]{2,1,0:T(2,128)(2,1)}), bf16[64,2,2048]{2,1,0:T(2,128)(2,1)S(1)}, u32[]{:S(2)}, u32[]{:S(2)}) %all-to-all-start.1) | async-done | bytes 524320 | tf_op jit(solution)/shard_map/while/body/eval_jaxpr/all_to_all | solution.py:98
  503.7 17.2 %all-to-all-done = bf16[64,2,2048]{2,1,0:T(2,128)(2,1)} async-done(((bf16[64,2,2048]{2,1,0:T(2,128)(2,1)}), bf16[64,2,2048]{2,1,0:T(2,128)(2,1)}, u32[]{:S(2)}, u32[]{:S(2)}) %all-to-all-start) | async-done | bytes 524320 | tf_op jit(solution)/shard_map/while/body/eval_jaxpr/all_to_all | solution.py:97
  539.1 15.4 %all-to-all-done.1 = bf16[64,2,2048]{2,1,0:T(2,128)(2,1)S(1)} async-done(((bf16[64,2,2048]{2,1,0:T(2,128)(2,1)}), bf16[64,2,2048]{2,1,0:T(2,128)(2,1)S(1)}, u32[]{:S(2)}, u32[]{:S(2)}) %all-to-all-start.1) | async-done | bytes 524320 | tf_op jit(solution)/shard_map/while/body/eval_jaxpr/all_to_all | solution.py:98
  573.0 17.2 %all-to-all-done = bf16[64,2,2048]{2,1,0:T(2,128)(2,1)} async-done(((bf16[64,2,2048]{2,1,0:T(2,128)(2,1)}), bf16[64,2,2048]{2,1,0:T(2,128)(2,1)}, u32[]{:S(2)}, u32[]{:S(2)}) %all-to-all-start) | async-done | bytes 524320 | tf_op jit(solution)/shard_map/while/body/eval_jaxpr/all_to_all | solution.py:97
  638.7 17.2 %all-to-all-done = bf16[64,2,2048]{2,1,0:T(2,128)(2,1)} async-done(((bf16[64,2,2048]{2,1,0:T(2,128)(2,1)}), bf16[64,2,2048]{2,1,0:T(2,128)(2,1)}, u32[]{:S(2)}, u32[]{:S(2)}) %all-to-all-start) | async-done | bytes 524320 | tf_op jit(solution)/shard_map/while/body/eval_jaxpr/all_to_all | solution.py:97
  666.1 14.5 %all-to-all-done.1 = bf16[64,2,2048]{2,1,0:T(2,128)(2,1)S(1)} async-done(((bf16[64,2,2048]{2,1,0:T(2,128)(2,1)}), bf16[64,2,2048]{2,1,0:T(2,128)(2,1)S(1)}, u32[]{:S(2)}, u32[]{:S(2)}) %all-to-all-start.1) | async-done | bytes 524320 | tf_op jit(solution)/shard_map/while/body/eval_jaxpr/all_to_all | solution.py:98
  706.8 17.2 %all-to-all-done = bf16[64,2,2048]{2,1,0:T(2,128)(2,1)} async-done(((bf16[64,2,2048]{2,1,0:T(2,128)(2,1)}), bf16[64,2,2048]{2,1,0:T(2,128)(2,1)}, u32[]{:S(2)}, u32[]{:S(2)}) %all-to-all-start) | async-done | bytes 524320 | tf_op jit(solution)/shard_map/while/body/eval_jaxpr/all_to_all | solution.py:97
  733.3 15.4 %all-to-all-done.1 = bf16[64,2,2048]{2,1,0:T(2,128)(2,1)S(1)} async-done(((bf16[64,2,2048]{2,1,0:T(2,128)(2,1)}), bf16[64,2,2048]{2,1,0:T(2,128)(2,1)S(1)}, u32[]{:S(2)}, u32[]{:S(2)}) %all-to-all-start.1) | async-done | bytes 524320 | tf_op jit(solution)/shard_map/while/body/eval_jaxpr/all_to_all | solution.py:98
  750.9 12.8 %collective-permute-done = bf16[16,2048]{1,0:T(8,128)(2,1)S(1)} collective-permute-done((bf16[16,2048]{1,0:T(8,128)(2,1)S(1)}, bf16[16,2048]{1,0:T(8,128)(2,1)S(1)}, u32[]{:S(2)}, u32[]{:S(2)}) %collective-permute-start) | collective-permute-done | bytes 65568 | tf_op jit(solution)/shard_map/while/body/eval_jaxpr/ppermute | solution.py:15
  (465 shorter events, 468.1 us)
Async XLA Ops:
  5.3 30.6 %all-to-all-start = ((bf16[64,2,2048]{2,1,0:T(2,128)(2,1)}), bf16[64,2,2048]{2,1,0:T(2,128)(2,1)}, u32[]{:S(2)}, u32[]{:S(2)}) async-start(bf16[64,2,2048]{2,1,0:T(2,128)(2,1)} %copy.43), calls=%async_computation | async-start | bytes 1048576 | tf_op jit(solution)/shard_map/while/body/eval_jaxpr/all_to_all | solution.py:97
  45.8 23.6 %all-to-all-start.1 = ((bf16[64,2,2048]{2,1,0:T(2,128)(2,1)}), bf16[64,2,2048]{2,1,0:T(2,128)(2,1)S(1)}, u32[]{:S(2)}, u32[]{:S(2)}) async-start(bf16[64,2,2048]{2,1,0:T(2,128)(2,1)} %copy-done.1), calls=%async_computation.1 | async-start | bytes 1048576 | tf_op jit(solution)/shard_map/while/body/eval_jaxpr/all_to_all | solution.py:98
  80.3 24.9 %all-to-all-start = ((bf16[64,2,2048]{2,1,0:T(2,128)(2,1)}), bf16[64,2,2048]{2,1,0:T(2,128)(2,1)}, u32[]{:S(2)}, u32[]{:S(2)}) async-start(bf16[64,2,2048]{2,1,0:T(2,128)(2,1)} %copy.43), calls=%async_computation | async-start | bytes 1048576 | tf_op jit(solution)/shard_map/while/body/eval_jaxpr/all_to_all | solution.py:97
  115.1 23.6 %all-to-all-start.1 = ((bf16[64,2,2048]{2,1,0:T(2,128)(2,1)}), bf16[64,2,2048]{2,1,0:T(2,128)(2,1)S(1)}, u32[]{:S(2)}, u32[]{:S(2)}) async-start(bf16[64,2,2048]{2,1,0:T(2,128)(2,1)} %copy-done.1), calls=%async_computation.1 | async-start | bytes 1048576 | tf_op jit(solution)/shard_map/while/body/eval_jaxpr/all_to_all | solution.py:98
  149.6 24.9 %all-to-all-start = ((bf16[64,2,2048]{2,1,0:T(2,128)(2,1)}), bf16[64,2,2048]{2,1,0:T(2,128)(2,1)}, u32[]{:S(2)}, u32[]{:S(2)}) async-start(bf16[64,2,2048]{2,1,0:T(2,128)(2,1)} %copy.43), calls=%async_computation | async-start | bytes 1048576 | tf_op jit(solution)/shard_map/while/body/eval_jaxpr/all_to_all | solution.py:97
  184.4 23.6 %all-to-all-start.1 = ((bf16[64,2,2048]{2,1,0:T(2,128)(2,1)}), bf16[64,2,2048]{2,1,0:T(2,128)(2,1)S(1)}, u32[]{:S(2)}, u32[]{:S(2)}) async-start(bf16[64,2,2048]{2,1,0:T(2,128)(2,1)} %copy-done.1), calls=%async_computation.1 | async-start | bytes 1048576 | tf_op jit(solution)/shard_map/while/body/eval_jaxpr/all_to_all | solution.py:98
  218.9 24.9 %all-to-all-start = ((bf16[64,2,2048]{2,1,0:T(2,128)(2,1)}), bf16[64,2,2048]{2,1,0:T(2,128)(2,1)}, u32[]{:S(2)}, u32[]{:S(2)}) async-start(bf16[64,2,2048]{2,1,0:T(2,128)(2,1)} %copy.43), calls=%async_computation | async-start | bytes 1048576 | tf_op jit(solution)/shard_map/while/body/eval_jaxpr/all_to_all | solution.py:97
  253.7 23.6 %all-to-all-start.1 = ((bf16[64,2,2048]{2,1,0:T(2,128)(2,1)}), bf16[64,2,2048]{2,1,0:T(2,128)(2,1)S(1)}, u32[]{:S(2)}, u32[]{:S(2)}) async-start(bf16[64,2,2048]{2,1,0:T(2,128)(2,1)} %copy-done.1), calls=%async_computation.1 | async-start | bytes 1048576 | tf_op jit(solution)/shard_map/while/body/eval_jaxpr/all_to_all | solution.py:98
  288.2 24.9 %all-to-all-start = ((bf16[64,2,2048]{2,1,0:T(2,128)(2,1)}), bf16[64,2,2048]{2,1,0:T(2,128)(2,1)}, u32[]{:S(2)}, u32[]{:S(2)}) async-start(bf16[64,2,2048]{2,1,0:T(2,128)(2,1)} %copy.43), calls=%async_computation | async-start | bytes 1048576 | tf_op jit(solution)/shard_map/while/body/eval_jaxpr/all_to_all | solution.py:97
  323.0 23.6 %all-to-all-start.1 = ((bf16[64,2,2048]{2,1,0:T(2,128)(2,1)}), bf16[64,2,2048]{2,1,0:T(2,128)(2,1)S(1)}, u32[]{:S(2)}, u32[]{:S(2)}) async-start(bf16[64,2,2048]{2,1,0:T(2,128)(2,1)} %copy-done.1), calls=%async_computation.1 | async-start | bytes 1048576 | tf_op jit(solution)/shard_map/while/body/eval_jaxpr/all_to_all | solution.py:98
  357.5 24.9 %all-to-all-start = ((bf16[64,2,2048]{2,1,0:T(2,128)(2,1)}), bf16[64,2,2048]{2,1,0:T(2,128)(2,1)}, u32[]{:S(2)}, u32[]{:S(2)}) async-start(bf16[64,2,2048]{2,1,0:T(2,128)(2,1)} %copy.43), calls=%async_computation | async-start | bytes 1048576 | tf_op jit(solution)/shard_map/while/body/eval_jaxpr/all_to_all | solution.py:97
  392.3 23.6 %all-to-all-start.1 = ((bf16[64,2,2048]{2,1,0:T(2,128)(2,1)}), bf16[64,2,2048]{2,1,0:T(2,128)(2,1)S(1)}, u32[]{:S(2)}, u32[]{:S(2)}) async-start(bf16[64,2,2048]{2,1,0:T(2,128)(2,1)} %copy-done.1), calls=%async_computation.1 | async-start | bytes 1048576 | tf_op jit(solution)/shard_map/while/body/eval_jaxpr/all_to_all | solution.py:98
  426.8 24.9 %all-to-all-start = ((bf16[64,2,2048]{2,1,0:T(2,128)(2,1)}), bf16[64,2,2048]{2,1,0:T(2,128)(2,1)}, u32[]{:S(2)}, u32[]{:S(2)}) async-start(bf16[64,2,2048]{2,1,0:T(2,128)(2,1)} %copy.43), calls=%async_computation | async-start | bytes 1048576 | tf_op jit(solution)/shard_map/while/body/eval_jaxpr/all_to_all | solution.py:97
  461.6 23.6 %all-to-all-start.1 = ((bf16[64,2,2048]{2,1,0:T(2,128)(2,1)}), bf16[64,2,2048]{2,1,0:T(2,128)(2,1)S(1)}, u32[]{:S(2)}, u32[]{:S(2)}) async-start(bf16[64,2,2048]{2,1,0:T(2,128)(2,1)} %copy-done.1), calls=%async_computation.1 | async-start | bytes 1048576 | tf_op jit(solution)/shard_map/while/body/eval_jaxpr/all_to_all | solution.py:98
  496.0 24.9 %all-to-all-start = ((bf16[64,2,2048]{2,1,0:T(2,128)(2,1)}), bf16[64,2,2048]{2,1,0:T(2,128)(2,1)}, u32[]{:S(2)}, u32[]{:S(2)}) async-start(bf16[64,2,2048]{2,1,0:T(2,128)(2,1)} %copy.43), calls=%async_computation | async-start | bytes 1048576 | tf_op jit(solution)/shard_map/while/body/eval_jaxpr/all_to_all | solution.py:97
  530.9 23.6 %all-to-all-start.1 = ((bf16[64,2,2048]{2,1,0:T(2,128)(2,1)}), bf16[64,2,2048]{2,1,0:T(2,128)(2,1)S(1)}, u32[]{:S(2)}, u32[]{:S(2)}) async-start(bf16[64,2,2048]{2,1,0:T(2,128)(2,1)} %copy-done.1), calls=%async_computation.1 | async-start | bytes 1048576 | tf_op jit(solution)/shard_map/while/body/eval_jaxpr/all_to_all | solution.py:98
  565.3 24.9 %all-to-all-start = ((bf16[64,2,2048]{2,1,0:T(2,128)(2,1)}), bf16[64,2,2048]{2,1,0:T(2,128)(2,1)}, u32[]{:S(2)}, u32[]{:S(2)}) async-start(bf16[64,2,2048]{2,1,0:T(2,128)(2,1)} %copy.43), calls=%async_computation | async-start | bytes 1048576 | tf_op jit(solution)/shard_map/while/body/eval_jaxpr/all_to_all | solution.py:97
  591.3 23.6 %all-to-all-start.1 = ((bf16[64,2,2048]{2,1,0:T(2,128)(2,1)}), bf16[64,2,2048]{2,1,0:T(2,128)(2,1)S(1)}, u32[]{:S(2)}, u32[]{:S(2)}) async-start(bf16[64,2,2048]{2,1,0:T(2,128)(2,1)} %copy-done.1), calls=%async_computation.1 | async-start | bytes 1048576 | tf_op jit(solution)/shard_map/while/body/eval_jaxpr/all_to_all | solution.py:98
  597.6 26.9 %collective-permute-start.1 = (bf16[16,2048]{1,0:T(8,128)(2,1)S(1)}, bf16[16,2048]{1,0:T(8,128)(2,1)S(1)}, u32[]{:S(2)}, u32[]{:S(2)}) collective-permute-start(bf16[16,2048]{1,0:T(8,128)(2,1)S(1)} %broadcast_select_fusion.4), channel_id=1, source_target_pairs={{192,0},{0,64},{64,128},{128,192},{193,1},{1,65},{65,129},{129,193... | collective-permute-start | bytes 196616 | tf_op jit(solution)/shard_map/while/body/eval_jaxpr/ppermute | solution.py:15
  631.9 24.0 %all-to-all-start = ((bf16[64,2,2048]{2,1,0:T(2,128)(2,1)}), bf16[64,2,2048]{2,1,0:T(2,128)(2,1)}, u32[]{:S(2)}, u32[]{:S(2)}) async-start(bf16[64,2,2048]{2,1,0:T(2,128)(2,1)} %copy.43), calls=%async_computation | async-start | bytes 1048576 | tf_op jit(solution)/shard_map/while/body/eval_jaxpr/all_to_all | solution.py:97
  657.0 23.6 %all-to-all-start.1 = ((bf16[64,2,2048]{2,1,0:T(2,128)(2,1)}), bf16[64,2,2048]{2,1,0:T(2,128)(2,1)S(1)}, u32[]{:S(2)}, u32[]{:S(2)}) async-start(bf16[64,2,2048]{2,1,0:T(2,128)(2,1)} %copy-done.1), calls=%async_computation.1 | async-start | bytes 1048576 | tf_op jit(solution)/shard_map/while/body/eval_jaxpr/all_to_all | solution.py:98
  663.3 20.3 %collective-permute-start.1 = (bf16[16,2048]{1,0:T(8,128)(2,1)S(1)}, bf16[16,2048]{1,0:T(8,128)(2,1)S(1)}, u32[]{:S(2)}, u32[]{:S(2)}) collective-permute-start(bf16[16,2048]{1,0:T(8,128)(2,1)S(1)} %broadcast_select_fusion.4), channel_id=1, source_target_pairs={{192,0},{0,64},{64,128},{128,192},{193,1},{1,65},{65,129},{129,193... | collective-permute-start | bytes 196616 | tf_op jit(solution)/shard_map/while/body/eval_jaxpr/ppermute | solution.py:15
  700.0 24.0 %all-to-all-start = ((bf16[64,2,2048]{2,1,0:T(2,128)(2,1)}), bf16[64,2,2048]{2,1,0:T(2,128)(2,1)}, u32[]{:S(2)}, u32[]{:S(2)}) async-start(bf16[64,2,2048]{2,1,0:T(2,128)(2,1)} %copy.43), calls=%async_computation | async-start | bytes 1048576 | tf_op jit(solution)/shard_map/while/body/eval_jaxpr/all_to_all | solution.py:97
  725.1 23.6 %all-to-all-start.1 = ((bf16[64,2,2048]{2,1,0:T(2,128)(2,1)}), bf16[64,2,2048]{2,1,0:T(2,128)(2,1)S(1)}, u32[]{:S(2)}, u32[]{:S(2)}) async-start(bf16[64,2,2048]{2,1,0:T(2,128)(2,1)} %copy-done.1), calls=%async_computation.1 | async-start | bytes 1048576 | tf_op jit(solution)/shard_map/while/body/eval_jaxpr/all_to_all | solution.py:98
  (42 other events, 581.4 us)
where the time goes:
time: 769 us; the launch traced here: 764 us
  waiting for transfers between devices  413 us (54%)
  starting transfers between devices  175 us (23%)
  matrix products  67.7 us (9%)
  local copies, waits for them, and re-layouts  64.4 us (8%)
  other arithmetic  42.6 us (6%)
    all_to_all x11, waiting for transfers between devices, advance_moment(): lax.all_to_all(outgoing, 'expert', split_axis=0, concat_axis=0, tiled=True)  190 us
    all_to_all x11, waiting for transfers between devices, advance_moment(): lax.all_to_all(lax.cond(active, compute_rows, jnp.zeros_like, received),...  161 us
    all_to_all x11, starting transfers between devices, advance_moment(): lax.all_to_all(outgoing, 'expert', split_axis=0, concat_axis=0, tiled=True)  87.9 us
    all_to_all x11, starting transfers between devices, advance_moment(): lax.all_to_all(lax.cond(active, compute_rows, jnp.zeros_like, received),...  69 us
    ppermute x22, waiting for transfers between devices, shifted(): return lax.ppermute(block, axis, route)  62.3 us
    dot_general x8, matrix products, expert_ffn(): jnp.dot(activated, w_down, preferred_element_type=jnp.float32)  35.1 us
    dot_general x8, matrix products, expert_ffn(): gate_part = jnp.dot(flattened, w_gate, preferred_element_type=jnp.float32)  18.9 us
    ppermute x22, starting transfers between devices, shifted(): return lax.ppermute(block, axis, route)  18.3 us
  transfers between devices with their start and end apart: 44, of which 33 were waited for; matrix products, arithmetic and copies ran while one was open for 6% of the time, Pallas kernels for 0%

commit v1 on v0

v1 whole, which is shorter than its diff:
```python
import functools

import jax
import jax.numpy as jnp
from jax import lax
from jax.experimental import pallas as pl
from jax.experimental.pallas import tpu as pltpu
from jax.sharding import PartitionSpec as P

EPSILON = 1e-06
SLOTS = 2

PAIR = (
    (3, 3, 3, 3),
    (2, 3, 3, 3),
    (0, 2, 3, 1),
    (1, 0, 2, 3),
    (1, 1, 0, 2),
    (1, 1, 1, 0),
)
RECEIVED = (
    (0, 0, 0, 0),
    (0, 0, 0, 0),
    (0, 0, 0, 1),
    (1, 0, 0, 0),
    (0, 1, 0, 0),
    (0, 0, 1, 0),
)


def normed_rows_kernel(experts, take_ref, first_ref, second_ref, gain_ref, ids_ref, hidden_ref, out_ref):
    rows = first_ref.shape[0]
    block = rows // 2
    hidden = jnp.where(take_ref[0] == 0, first_ref[...], second_ref[...])
    hidden_ref[...] = hidden
    values = hidden.astype(jnp.float32)
    inverse = lax.rsqrt(jnp.mean(values * values, axis=-1, keepdims=True) + EPSILON)
    normed = (values * inverse * gain_ref[...]).astype(jnp.bfloat16)
    height = experts * 2 * SLOTS
    place = lax.broadcasted_iota(jnp.int32, (height, rows), 0)
    source = lax.broadcasted_iota(jnp.int32, (height, rows), 1)
    expert = place // (2 * SLOTS)
    member = (place // SLOTS) % 2
    slot = place % SLOTS
    named = jnp.zeros((height, rows), jnp.bool_)
    for choice in range(ids_ref.shape[0]):
        named = jnp.logical_or(named, ids_ref[choice : choice + 1, :] == expert)
    named = jnp.logical_and(named, source // block == member)
    hot = jnp.where(named, 1.0, 0.0).astype(jnp.bfloat16)
    row = lax.broadcasted_iota(jnp.int32, (rows, rows), 0)
    column = lax.broadcasted_iota(jnp.int32, (rows, rows), 1)
    before = jnp.where(row < column, 1.0, 0.0).astype(jnp.bfloat16)
    earlier = jnp.dot(hot, before, preferred_element_type=jnp.float32)
    chosen = jnp.logical_and(named, earlier == slot.astype(jnp.float32))
    placing = jnp.where(chosen, 1.0, 0.0).astype(jnp.bfloat16)
    sent = jnp.dot(placing, normed, preferred_element_type=jnp.float32)
    out_ref[...] = sent.reshape(out_ref.shape).astype(jnp.bfloat16)


def ffn_kernel(rows_ref, gate_ref, up_ref, down_ref, out_ref, flat, total):
    step = pl.program_id(0)

    @pl.when(step == 0)
    def _():
        flat[...] = rows_ref[...].reshape(flat.shape)

    rows = flat[...]
    gate = jnp.dot(rows, gate_ref[...], preferred_element_type=jnp.float32)
    up = jnp.dot(rows, up_ref[...], preferred_element_type=jnp.float32)
    activated = (gate / (1.0 + jnp.exp(-gate)) * up).astype(jnp.bfloat16)
    part = jnp.dot(activated, down_ref[...], preferred_element_type=jnp.float32)

    @pl.when(step == 0)
    def _():
        total[...] = part

    @pl.when(jnp.logical_and(step > 0, step < pl.num_programs(0) - 1))
    def _():
        total[...] += part

    @pl.when(step == pl.num_programs(0) - 1)
    def _():
        out_ref[...] = (total[...] + part).reshape(out_ref.shape).astype(jnp.bfloat16)


def combine_kernel(experts, back_ref, hidden_ref, ids_ref, weights_ref, out_ref):
    rows = hidden_ref.shape[0]
    block = rows // 2
    width = experts * 2 * SLOTS
    raw = weights_ref[...]
    weights = raw / jnp.sum(raw, axis=-1, keepdims=True)
    source = lax.broadcasted_iota(jnp.int32, (rows, width), 0)
    place = lax.broadcasted_iota(jnp.int32, (rows, width), 1)
    expert = place // (2 * SLOTS)
    member = (place // SLOTS) % 2
    slot = place % SLOTS
    mine = source // block == member
    scale = jnp.zeros((rows, width), jnp.float32)
    named = jnp.zeros((rows, width), jnp.bool_)
    for choice in range(ids_ref.shape[1]):
        same = jnp.logical_and(ids_ref[:, choice : choice + 1] == expert, mine)
        named = jnp.logical_or(named, same)
        scale = jnp.where(same, weights[:, choice : choice + 1], scale)
    hot = jnp.where(named, 1.0, 0.0).astype(jnp.bfloat16)
    row = lax.broadcasted_iota(jnp.int32, (rows, rows), 0)
    column = lax.broadcasted_iota(jnp.int32, (rows, rows), 1)
    before = jnp.where(column < row, 1.0, 0.0).astype(jnp.bfloat16)
    earlier = jnp.dot(before, hot, preferred_element_type=jnp.float32)
    chosen = jnp.logical_and(named, earlier == slot.astype(jnp.float32))
    scale = jnp.where(chosen, scale, 0.0)
    high = scale.astype(jnp.bfloat16)
    low = (scale - high.astype(jnp.float32)).astype(jnp.bfloat16)
    back = back_ref[...].reshape(width, back_ref.shape[-1])
    mixed = jnp.dot(high, back, preferred_element_type=jnp.float32)
    mixed += jnp.dot(low, back, preferred_element_type=jnp.float32)
    out_ref[...] = (hidden_ref[...].astype(jnp.float32) + mixed).astype(jnp.bfloat16)


VMEM = pl.BlockSpec(memory_space=pltpu.VMEM)
SMEM = pl.BlockSpec(memory_space=pltpu.SMEM)
PARAMS = pltpu.CompilerParams(vmem_limit_bytes=40 * 1024 * 1024)


def normed_rows(experts, take, first, second, gain, ids):
    rows, features = first.shape
    return pl.pallas_call(
        functools.partial(normed_rows_kernel, experts),
        out_shape=(
            jax.ShapeDtypeStruct((rows, features), jnp.bfloat16),
            jax.ShapeDtypeStruct((experts, 2 * SLOTS, features), jnp.bfloat16),
        ),
        in_specs=[SMEM, VMEM, VMEM, VMEM, VMEM],
        out_specs=(VMEM, VMEM),
        compiler_params=PARAMS,
    )(take, first, second, gain, ids)


def ffn(rows, gate, up, down):
    sources, slots, features = rows.shape
    hidden_units = gate.shape[1]
    cut = 256 if hidden_units % 256 == 0 else hidden_units
    whole = pl.BlockSpec(rows.shape, lambda i: (0, 0, 0))
    return pl.pallas_call(
        ffn_kernel,
        out_shape=jax.ShapeDtypeStruct(rows.shape, jnp.bfloat16),
        grid=(hidden_units // cut,),
        in_specs=[
            whole,
            pl.BlockSpec((features, cut), lambda i: (0, i)),
            pl.BlockSpec((features, cut), lambda i: (0, i)),
            pl.BlockSpec((cut, features), lambda i: (i, 0)),
        ],
        out_specs=whole,
        scratch_shapes=[
            pltpu.VMEM((sources * slots, features), jnp.bfloat16),
            pltpu.VMEM((sources * slots, features), jnp.float32),
        ],
        compiler_params=PARAMS,
    )(rows, gate, up, down)


def combine(experts, back, hidden, ids, weights):
    return pl.pallas_call(
        functools.partial(combine_kernel, experts),
        out_shape=jax.ShapeDtypeStruct(hidden.shape, jnp.bfloat16),
        in_specs=[VMEM] * 4,
        out_specs=VMEM,
        compiler_params=PARAMS,
    )(back, hidden, ids, weights)


def on_device(tokens, norm_gain, gate_proj, up_proj, down_proj, expert_ids, gate_weights):
    section = lax.axis_index("section")
    experts = lax.axis_size("expert")
    block, features = tokens.shape[1:]
    rows = 2 * block
    own = tokens.reshape(rows, features)

    def move(value, route):
        return lax.ppermute(value, "section", route)

    def exchange(value):
        return lax.all_to_all(value, "expert", split_axis=0, concat_axis=0, tiled=True)

    back_one = [(i, (i - 1) % 4) for i in range(4)]
    on_one = [(i, (i + 1) % 4) for i in range(4)]
    arrived = move(own, [(1, 0)])
    second_in = move(own, [(2, 0)])
    ids = (expert_ids[0], move(expert_ids[0], back_one))
    raw = (gate_weights[0], move(gate_weights[0], back_one))
    gains = (norm_gain, move(norm_gain, back_one))
    own_layer = (gate_proj[0, 0], up_proj[0, 0], down_proj[0, 0])
    next_layer = tuple(move(part, back_one) for part in own_layer)

    def choice(table):
        return jnp.array(table, jnp.int32)[section]

    def of_pair(value, pair):
        low = lax.dynamic_index_in_dim(value, pair, 0, keepdims=False)
        high = lax.dynamic_index_in_dim(value, pair + 4, 0, keepdims=False)
        return jnp.concatenate([low, high], axis=0)

    def step(number, take, first, second):
        pair = choice(PAIR[number])
        received = choice(RECEIVED[number]) == 1
        if any(RECEIVED[number]):
            step_ids = of_pair(jnp.where(received, ids[1], ids[0]), pair)
            step_raw = of_pair(jnp.where(received, raw[1], raw[0]), pair)
            gain = jnp.where(received, gains[1], gains[0])
        else:
            step_ids, step_raw, gain = of_pair(ids[0], pair), of_pair(raw[0], pair), gains[0]
        hidden, sent = normed_rows(experts, take.reshape(1), first, second, gain, step_ids.T)
        gathered = exchange(sent)
        if any(RECEIVED[number]):
            made = lax.cond(
                received,
                lambda value: ffn(value, *next_layer),
                lambda value: ffn(value, *own_layer),
                gathered,
            )
        else:
            made = ffn(gathered, *own_layer)
        return combine(experts, exchange(made), hidden, step_ids, step_raw)

    keep = jnp.zeros((), jnp.int32)
    state = step(0, keep, arrived, arrived)
    state = move(state, [(0, 1)])
    state = step(1, choice((1, 0, 0, 0)), state, second_in)
    state = move(state, [(0, 1), (1, 2)])
    state = step(2, choice((1, 0, 0, 1)), state, own)
    state = move(state, on_one)
    state = step(3, keep, state, state)
    state = move(state, on_one)
    finished_first = state
    state = step(4, keep, state, state)
    finished_second = move(state, [(3, 1)])
    state = move(state, [(1, 2), (2, 3)])
    state = step(5, keep, state, state)
    state = jnp.where(section == 0, finished_first, jnp.where(section == 1, finished_second, state))
    return state.reshape(2, block, features)[::-1]


def solution(mesh):
    return jax.shard_map(
        on_device,
        mesh=mesh,
        in_specs=(
            P("section", "expert", None),
            P("section", None),
            P("section", "expert", None, None),
            P("section", "expert", None, None),
            P("section", "expert", None, None),
            P("section", None, "expert", None),
            P("section", None, "expert", None),
        ),
        out_specs=P("section", "expert", None),
        check_vma=False,
    )
```

time: 769 us -> 715 us (0.930); the launches traced: 764 us -> 701 us
  starting transfers between devices: 175 us -> 87.3 us
  blocking collectives: 0 us -> 77.1 us
  matrix products: 67.7 us -> 0 us
  Pallas kernels: 0 us -> 58.1 us
  local copies, waits for them, and re-layouts: 64.4 us -> 9.85 us
  other arithmetic: 42.6 us -> 1.42 us
  waiting for transfers between devices: 413 us -> 448 us
  between operations: 0.01 us -> 19.4 us
    ppermute x22 -> x14, waiting for transfers between devices: 62.3 us -> 202 us  [move(): return lax.ppermute(value, 'section', route)]
    all_to_all x22 -> x10, waiting for transfers between devices: 351 us -> 246 us  [exchange(): lax.all_to_all(value, 'expert', split_axis=0, concat_axis=0, tiled=True)]
    all_to_all x22 -> x10, starting transfers between devices: 157 us -> 68.4 us  [exchange(): lax.all_to_all(value, 'expert', split_axis=0, concat_axis=0, tiled=True)]
    all_to_all x0 -> x2, blocking collectives: none -> 77.1 us  [exchange(): lax.all_to_all(value, 'expert', split_axis=0, concat_axis=0, tiled=True)]
    dot_general x38 -> x0, matrix products: 67.7 us -> none  [the longest x8 35.1 us: expert_ffn(): jnp.dot(activated, w_down, preferred_element_type=jnp.float32)]
    pallas_call x0 -> x18, Pallas kernels: none -> 58.1 us  [the longest x6 44.8 us: ffn(): pl.pallas_call(ffn_kernel, out_shape=jax.ShapeDtypeStruct(rows.shape, jnp...]
    reduce_sum x44 -> x0, other arithmetic: 21.5 us -> none  [the longest x11 10.1 us: combine_rows(): return jnp.sum(picked.astype(jnp.float32) * weights[:, :, None], axis=1)]
    reshape x27 -> x0, local copies, waits for them, and re-layouts: 21.3 us -> none  [the longest x8 16.4 us: expert_ffn(): flattened = received.reshape(sources * slot_count, feature_count)]
  transfers between devices with their start and end apart: 44 -> 24, of which waited for: 33 -> 14; matrix products, arithmetic and copies ran while one was open for 6% -> 1% of each run, Pallas kernels for 0% -> 1%
where the time goes in v1:
time: 715 us; the launch traced here: 701 us
  waiting for transfers between devices  448 us (63%)
  starting transfers between devices  87.3 us (12%)
  blocking collectives  77.1 us (11%)
  Pallas kernels  58.1 us (8%)
  between operations  19.4 us (3%)
  local copies, waits for them, and re-layouts  9.85 us (1%)
    all_to_all x10, waiting for transfers between devices, exchange(): lax.all_to_all(value, 'expert', split_axis=0, concat_axis=0, tiled=True)  246 us
    ppermute x14, waiting for transfers between devices, move(): return lax.ppermute(value, 'section', route)  202 us
    all_to_all x2, blocking collectives, exchange(): lax.all_to_all(value, 'expert', split_axis=0, concat_axis=0, tiled=True)  77.1 us
    all_to_all x10, starting transfers between devices, exchange(): lax.all_to_all(value, 'expert', split_axis=0, concat_axis=0, tiled=True)  68.4 us
    pallas_call x6, Pallas kernels, ffn(): pl.pallas_call(ffn_kernel, out_shape=jax.ShapeDtypeStruct(rows.shape, jnp...  44.8 us
    ppermute x14, starting transfers between devices, move(): return lax.ppermute(value, 'section', route)  19 us
  transfers between devices with their start and end apart: 24, of which 14 were waited for; matrix products, arithmetic and copies ran while one was open for 1% of the time, Pallas kernels for 1%

profile of v1, /device:TPU:1, one launch (start us, length us, event | category | flops | bytes accessed | tf_op | source)
XLA Modules:
  0.0 701.3 jit_solution(4601332580924055003)
XLA Ops:
  8.0 42.2 %all_to_all.60.rows_ref = bf16[64,4,2048]{2,1,0:T(4,128)(2,1)S(1)} all-to-all(bf16[64,4,2048]{2,1,0:T(4,128)(2,1)S(1)} %get-tuple-element.125), channel_id=1, replica_groups=mesh['section'=4,'expert'=64] {'expert'}, dimensions={0} | all-to-all | bytes 2097152 | tf_op jit(solution)/shard_map/all_to_all | solution.py:183
  50.2 7.6 %shard_map.182 = bf16[64,4,2048]{2,1,0:T(4,128)(2,1)} custom-call(bf16[64,4,2048]{2,1,0:T(4,128)(2,1)S(1)} %all_to_all.60.rows_ref, bf16[2048,768]{1,0:T(8,128)(2,1)} %bitcast.87, bf16[2048,768]{1,0:T(8,128)(2,1)} %bitcast.94, bf16[768,2048]{1,0:T(8,128)(2,1)} %bitcast.101), custom_call_target="tpu_custom_call" | custom-call | tf_op jit(solution)/shard_map/pallas_call | solution.py:143
  65.8 26.9 %all-to-all-done.1.back_ref = bf16[64,4,2048]{2,1,0:T(4,128)(2,1)S(1)} async-done(((bf16[64,4,2048]{2,1,0:T(4,128)(2,1)}), bf16[64,4,2048]{2,1,0:T(4,128)(2,1)S(1)}, u32[]{:S(2)}, u32[]{:S(2)}) %all-to-all-start.1) | async-done | bytes 1048608 | tf_op jit(solution)/shard_map/all_to_all | solution.py:183
  101.3 34.8 %all_to_all.61.rows_ref = bf16[64,4,2048]{2,1,0:T(4,128)(2,1)S(1)} all-to-all(bf16[64,4,2048]{2,1,0:T(4,128)(2,1)S(1)} %get-tuple-element.127), channel_id=1, replica_groups=mesh['section'=4,'expert'=64] {'expert'}, dimensions={0} | all-to-all | bytes 2097152 | tf_op jit(solution)/shard_map/all_to_all | solution.py:183
  136.2 7.0 shard_map.185
  167.0 188.9 %collective-permute-done.5 = s32[8,16,8]{1,2,0:T(8,128)S(1)} collective-permute-done((s32[8,16,8]{1,2,0:T(8,128)S(1)}, s32[8,16,8]{1,2,0:T(8,128)S(1)}, u32[]{:S(2)}, u32[]{:S(2)}) %collective-permute-start.5) | collective-permute-done | bytes 4128 | tf_op jit(solution)/shard_map/ppermute | solution.py:180
  364.0 11.9 %all-to-all-start.4 = ((bf16[64,4,2048]{2,1,0:T(4,128)(2,1)}), bf16[64,4,2048]{2,1,0:T(4,128)(2,1)S(1)}, u32[]{:S(2)}, u32[]{:S(2)}) async-start(bf16[64,4,2048]{2,1,0:T(4,128)(2,1)} %get-tuple-element.129), calls=%async_computation.4 | async-start | bytes 2097152 | tf_op jit(solution)/shard_map/all_to_all | solution.py:183
  375.9 28.6 %all-to-all-done.4 = bf16[64,4,2048]{2,1,0:T(4,128)(2,1)S(1)} async-done(((bf16[64,4,2048]{2,1,0:T(4,128)(2,1)}), bf16[64,4,2048]{2,1,0:T(4,128)(2,1)S(1)}, u32[]{:S(2)}, u32[]{:S(2)}) %all-to-all-start.4) | async-done | bytes 1048608 | tf_op jit(solution)/shard_map/all_to_all | solution.py:183
  404.5 7.6 %conditional.4 = (bf16[64,4,2048]{2,1,0:T(4,128)(2,1)}) conditional(s32[]{:T(128)} %convert_element_type.13, (bf16[64,4,2048]{2,1,0:T(4,128)(2,1)S(1)}, bf16[2048,768]{1,0:T(8,128)(2,1)}, bf16[2048,768]{1,0:T(8,128)(2,1)}, bf16[768,2048]{1,0:T(8,128)(2,1)}) %tuple.84, (bf16[64,4,2048]{2,1,0:T(4,128)(2,1)S(1)}, bf16[2048,768]{1,0:T(8,128)(2,1)}, ...), branch_computations={%region_0.1_spmd, %region_1.2_spmd} | conditional | bytes 8 | solution.py:215
  404.5 7.6 %branch_0_fun.4 = bf16[64,4,2048]{2,1,0:T(4,128)(2,1)} custom-call(bf16[64,4,2048]{2,1,0:T(4,128)(2,1)S(1)} %get-tuple-element.74.rows_ref, bf16[2048,768]{1,0:T(8,128)(2,1)} %get-tuple-element.80.gate_ref, bf16[2048,768]{1,0:T(8,128)(2,1)} %get-tuple-element.82.up_ref, bf16[768,2048]{1,0:T(8,128)(2,1)} %get-tuple-element.84.down_ref), custom_call_target="tpu_custom_call" | custom-call | tf_op jit(solution)/shard_map/cond/branch_0_fun/pallas_call | solution.py:143
  426.3 20.5 %all-to-all-done.5.back_ref = bf16[64,4,2048]{2,1,0:T(4,128)(2,1)S(1)} async-done(((bf16[64,4,2048]{2,1,0:T(4,128)(2,1)}), bf16[64,4,2048]{2,1,0:T(4,128)(2,1)S(1)}, u32[]{:S(2)}, u32[]{:S(2)}) %all-to-all-start.5) | async-done | bytes 1048608 | tf_op jit(solution)/shard_map/all_to_all | solution.py:183
  462.0 28.6 %all-to-all-done.6 = bf16[64,4,2048]{2,1,0:T(4,128)(2,1)S(1)} async-done(((bf16[64,4,2048]{2,1,0:T(4,128)(2,1)}), bf16[64,4,2048]{2,1,0:T(4,128)(2,1)S(1)}, u32[]{:S(2)}, u32[]{:S(2)}) %all-to-all-start.6) | async-done | bytes 1048608 | tf_op jit(solution)/shard_map/all_to_all | solution.py:183
  490.5 7.7 %conditional.5 = (bf16[64,4,2048]{2,1,0:T(4,128)(2,1)}) conditional(s32[]{:T(128)} %convert_element_type.12, (bf16[64,4,2048]{2,1,0:T(4,128)(2,1)S(1)}, bf16[2048,768]{1,0:T(8,128)(2,1)}, bf16[2048,768]{1,0:T(8,128)(2,1)}, bf16[768,2048]{1,0:T(8,128)(2,1)}) %tuple.85, (bf16[64,4,2048]{2,1,0:T(4,128)(2,1)S(1)}, bf16[2048,768]{1,0:T(8,128)(2,1)}, ...), branch_computations={%region_2.3_spmd, %region_3.4_spmd} | conditional | bytes 8 | solution.py:215
  490.7 7.5 %branch_1_fun.5 = bf16[64,4,2048]{2,1,0:T(4,128)(2,1)} custom-call(bf16[64,4,2048]{2,1,0:T(4,128)(2,1)S(1)} %get-tuple-element.93.rows_ref, bf16[2048,768]{1,0:T(8,128)(2,1)} %get-tuple-element.94.gate_ref, bf16[2048,768]{1,0:T(8,128)(2,1)} %get-tuple-element.95.up_ref, bf16[768,2048]{1,0:T(8,128)(2,1)} %get-tuple-element.96.down_ref), custom_call_target="tpu_custom_call" | custom-call | tf_op jit(solution)/shard_map/cond/branch_1_fun/pallas_call | solution.py:143
  504.8 28.2 %all-to-all-done.7.back_ref = bf16[64,4,2048]{2,1,0:T(4,128)(2,1)S(1)} async-done(((bf16[64,4,2048]{2,1,0:T(4,128)(2,1)}), bf16[64,4,2048]{2,1,0:T(4,128)(2,1)S(1)}, u32[]{:S(2)}, u32[]{:S(2)}) %all-to-all-start.7) | async-done | bytes 1048608 | tf_op jit(solution)/shard_map/all_to_all | solution.py:183
  541.7 6.5 all-to-all-start.8
  548.2 28.6 %all-to-all-done.8 = bf16[64,4,2048]{2,1,0:T(4,128)(2,1)S(1)} async-done(((bf16[64,4,2048]{2,1,0:T(4,128)(2,1)}), bf16[64,4,2048]{2,1,0:T(4,128)(2,1)S(1)}, u32[]{:S(2)}, u32[]{:S(2)}) %all-to-all-start.8) | async-done | bytes 1048608 | tf_op jit(solution)/shard_map/all_to_all | solution.py:183
  576.7 7.5 %conditional.6 = (bf16[64,4,2048]{2,1,0:T(4,128)(2,1)}) conditional(s32[]{:T(128)} %convert_element_type.14, (bf16[64,4,2048]{2,1,0:T(4,128)(2,1)S(1)}, bf16[2048,768]{1,0:T(8,128)(2,1)}, bf16[2048,768]{1,0:T(8,128)(2,1)}, bf16[768,2048]{1,0:T(8,128)(2,1)}) %tuple.86, (bf16[64,4,2048]{2,1,0:T(4,128)(2,1)S(1)}, bf16[2048,768]{1,0:T(8,128)(2,1)}, ...), branch_computations={%region_4.5_spmd, %region_5.6_spmd} | conditional | bytes 8 | solution.py:215
  576.7 7.5 %branch_0_fun.6 = bf16[64,4,2048]{2,1,0:T(4,128)(2,1)} custom-call(bf16[64,4,2048]{2,1,0:T(4,128)(2,1)S(1)} %get-tuple-element.97.rows_ref, bf16[2048,768]{1,0:T(8,128)(2,1)} %get-tuple-element.98.gate_ref, bf16[2048,768]{1,0:T(8,128)(2,1)} %get-tuple-element.99.up_ref, bf16[768,2048]{1,0:T(8,128)(2,1)} %get-tuple-element.100.down_ref), custom_call_target="tpu_custom_call" | custom-call | tf_op jit(solution)/shard_map/cond/branch_0_fun/pallas_call | solution.py:143
  590.8 28.2 %all-to-all-done.9.back_ref = bf16[64,4,2048]{2,1,0:T(4,128)(2,1)S(1)} async-done(((bf16[64,4,2048]{2,1,0:T(4,128)(2,1)}), bf16[64,4,2048]{2,1,0:T(4,128)(2,1)S(1)}, u32[]{:S(2)}, u32[]{:S(2)}) %all-to-all-start.9) | async-done | bytes 1048608 | tf_op jit(solution)/shard_map/all_to_all | solution.py:183
  628.6 28.6 %all-to-all-done.10 = bf16[64,4,2048]{2,1,0:T(4,128)(2,1)S(1)} async-done(((bf16[64,4,2048]{2,1,0:T(4,128)(2,1)}), bf16[64,4,2048]{2,1,0:T(4,128)(2,1)S(1)}, u32[]{:S(2)}, u32[]{:S(2)}) %all-to-all-start.10) | async-done | bytes 1048608 | tf_op jit(solution)/shard_map/all_to_all | solution.py:183
  657.1 7.5 %conditional.7 = (bf16[64,4,2048]{2,1,0:T(4,128)(2,1)}) conditional(s32[]{:T(128)} %convert_element_type.15, (bf16[64,4,2048]{2,1,0:T(4,128)(2,1)S(1)}, bf16[2048,768]{1,0:T(8,128)(2,1)}, bf16[2048,768]{1,0:T(8,128)(2,1)}, bf16[768,2048]{1,0:T(8,128)(2,1)}) %tuple.87, (bf16[64,4,2048]{2,1,0:T(4,128)(2,1)S(1)}, bf16[2048,768]{1,0:T(8,128)(2,1)}, ...), branch_computations={%region_6.7_spmd, %region_7.8_spmd} | conditional | bytes 8 | solution.py:215
  657.1 7.5 %branch_0_fun.7 = bf16[64,4,2048]{2,1,0:T(4,128)(2,1)} custom-call(bf16[64,4,2048]{2,1,0:T(4,128)(2,1)S(1)} %get-tuple-element.105.rows_ref, bf16[2048,768]{1,0:T(8,128)(2,1)} %get-tuple-element.106.gate_ref, bf16[2048,768]{1,0:T(8,128)(2,1)} %get-tuple-element.107.up_ref, bf16[768,2048]{1,0:T(8,128)(2,1)} %get-tuple-element.108.down_ref), custom_call_target="tpu_custom_call" | custom-call | tf_op jit(solution)/shard_map/cond/branch_0_fun/pallas_call | solution.py:143
  671.9 27.6 %all-to-all-done.11.back_ref = bf16[64,4,2048]{2,1,0:T(4,128)(2,1)S(1)} async-done(((bf16[64,4,2048]{2,1,0:T(4,128)(2,1)}), bf16[64,4,2048]{2,1,0:T(4,128)(2,1)S(1)}, u32[]{:S(2)}, u32[]{:S(2)}) %all-to-all-start.11) | async-done | bytes 1048608 | tf_op jit(solution)/shard_map/all_to_all | solution.py:183
  (129 shorter events, 106.9 us)
Async XLA Ops:
  0.0 6.6 collective-permute-start
  57.8 34.9 %all-to-all-start.1 = ((bf16[64,4,2048]{2,1,0:T(4,128)(2,1)}), bf16[64,4,2048]{2,1,0:T(4,128)(2,1)S(1)}, u32[]{:S(2)}, u32[]{:S(2)}) async-start(bf16[64,4,2048]{2,1,0:T(4,128)(2,1)} %shard_map.182), calls=%async_computation.1 | async-start | bytes 2097152 | tf_op jit(solution)/shard_map/all_to_all | solution.py:183
  64.2 33.6 %collective-permute-start.2 = (bf16[32,2048]{1,0:T(8,128)(2,1)S(1)}, bf16[32,2048]{1,0:T(8,128)(2,1)S(1)}, u32[]{:S(2)}, u32[]{:S(2)}) collective-permute-start(bf16[32,2048]{1,0:T(8,128)(2,1)S(1)} %bitcast.85), channel_id=1, source_target_pairs={{128,0},{129,1},{130,2},{131,3},{132,4},{133,5},{134,6},{135,7},{1... | collective-permute-start | bytes 393224 | tf_op jit(solution)/shard_map/ppermute | solution.py:180
  93.4 6.5 collective-permute-start.1
  143.2 212.8 %all-to-all-start.3 = ((bf16[64,4,2048]{2,1,0:T(4,128)(2,1)}), bf16[64,4,2048]{2,1,0:T(4,128)(2,1)S(1)}, u32[]{:S(2)}, u32[]{:S(2)}) async-start(bf16[64,4,2048]{2,1,0:T(4,128)(2,1)} %shard_map.185), calls=%async_computation.3 | async-start | bytes 2097152 | tf_op jit(solution)/shard_map/all_to_all | solution.py:183
  149.4 210.3 %collective-permute-start.4 = (f32[1,2048]{1,0:T(1,128)S(1)}, f32[1,2048]{1,0:T(1,128)S(1)}, u32[]{:S(2)}, u32[]{:S(2)}) collective-permute-start(f32[1,2048]{1,0:T(1,128)S(1)} %copy-done.2), channel_id=1, source_target_pairs={{0,192},{64,0},{128,64},{192,128},{1,193},{65,1},{129,65},{193,129... | collective-permute-start | bytes 24584 | tf_op jit(solution)/shard_map/ppermute | solution.py:180
  149.5 255.0 %collective-permute-start.6 = (bf16[2048,768]{1,0:T(8,128)(2,1)}, bf16[2048,768]{1,0:T(8,128)(2,1)}, u32[]{:S(2)}, u32[]{:S(2)}) collective-permute-start(bf16[2048,768]{1,0:T(8,128)(2,1)} %bitcast.88), channel_id=1, source_target_pairs={{0,192},{64,0},{128,64},{192,128},{1,193},{65,1},{129,65},{193,129... | collective-permute-start | bytes 9437192 | tf_op jit(solution)/shard_map/ppermute | solution.py:180
  149.6 254.9 %collective-permute-start.7 = (bf16[2048,768]{1,0:T(8,128)(2,1)}, bf16[2048,768]{1,0:T(8,128)(2,1)}, u32[]{:S(2)}, u32[]{:S(2)}) collective-permute-start(bf16[2048,768]{1,0:T(8,128)(2,1)} %bitcast.96), channel_id=1, source_target_pairs={{0,192},{64,0},{128,64},{192,128},{1,193},{65,1},{129,65},{193,129... | collective-permute-start | bytes 9437192 | tf_op jit(solution)/shard_map/ppermute | solution.py:180
  153.8 250.7 %collective-permute-start.8 = (bf16[768,2048]{1,0:T(8,128)(2,1)}, bf16[768,2048]{1,0:T(8,128)(2,1)}, u32[]{:S(2)}, u32[]{:S(2)}) collective-permute-start(bf16[768,2048]{1,0:T(8,128)(2,1)} %bitcast.103), channel_id=1, source_target_pairs={{0,192},{64,0},{128,64},{192,128},{1,193},{65,1},{129,65},{193,129... | collective-permute-start | bytes 9437192 | tf_op jit(solution)/shard_map/ppermute | solution.py:180
  154.0 201.9 %collective-permute-start.5 = (s32[8,16,8]{1,2,0:T(8,128)S(1)}, s32[8,16,8]{1,2,0:T(8,128)S(1)}, u32[]{:S(2)}, u32[]{:S(2)}) collective-permute-start(s32[8,16,8]{1,2,0:T(8,128)S(1)} %bitcast.109), channel_id=1, source_target_pairs={{0,192},{64,0},{128,64},{192,128},{1,193},{65,1},{129,65},{193,129... | collective-permute-start | bytes 12296 | tf_op jit(solution)/shard_map/ppermute | solution.py:180
  356.7 5.0 collective-permute-start.3
  364.0 40.5 %all-to-all-start.4 = ((bf16[64,4,2048]{2,1,0:T(4,128)(2,1)}), bf16[64,4,2048]{2,1,0:T(4,128)(2,1)S(1)}, u32[]{:S(2)}, u32[]{:S(2)}) async-start(bf16[64,4,2048]{2,1,0:T(4,128)(2,1)} %get-tuple-element.129), calls=%async_computation.4 | async-start | bytes 2097152 | tf_op jit(solution)/shard_map/all_to_all | solution.py:183
  412.0 34.8 %all-to-all-start.5 = ((bf16[64,4,2048]{2,1,0:T(4,128)(2,1)}), bf16[64,4,2048]{2,1,0:T(4,128)(2,1)S(1)}, u32[]{:S(2)}, u32[]{:S(2)}) async-start(bf16[64,4,2048]{2,1,0:T(4,128)(2,1)} %get-tuple-element.181), calls=%async_computation.5 | async-start | bytes 2097152 | tf_op jit(solution)/shard_map/all_to_all | solution.py:183
  418.2 7.9 %collective-permute-start.9 = (f32[8,16,8]{1,2,0:T(8,128)S(1)}, f32[8,16,8]{1,2,0:T(8,128)S(1)}, u32[]{:S(2)}, u32[]{:S(2)}) collective-permute-start(f32[8,16,8]{1,2,0:T(8,128)S(1)} %bitcast.110), channel_id=1, source_target_pairs={{0,192},{64,0},{128,64},{192,128},{1,193},{65,1},{129,65},{193,129... | collective-permute-start | bytes 12296 | tf_op jit(solution)/shard_map/ppermute | solution.py:180
  447.5 6.3 collective-permute-start.10
  455.5 35.0 %all-to-all-start.6 = ((bf16[64,4,2048]{2,1,0:T(4,128)(2,1)}), bf16[64,4,2048]{2,1,0:T(4,128)(2,1)S(1)}, u32[]{:S(2)}, u32[]{:S(2)}) async-start(bf16[64,4,2048]{2,1,0:T(4,128)(2,1)} %get-tuple-element.131), calls=%async_computation.6 | async-start | bytes 2097152 | tf_op jit(solution)/shard_map/all_to_all | solution.py:183
  498.3 34.8 %all-to-all-start.7 = ((bf16[64,4,2048]{2,1,0:T(4,128)(2,1)}), bf16[64,4,2048]{2,1,0:T(4,128)(2,1)S(1)}, u32[]{:S(2)}, u32[]{:S(2)}) async-start(bf16[64,4,2048]{2,1,0:T(4,128)(2,1)} %get-tuple-element.182), calls=%async_computation.7 | async-start | bytes 2097152 | tf_op jit(solution)/shard_map/all_to_all | solution.py:183
  533.7 6.3 collective-permute-start.11
  541.7 35.0 %all-to-all-start.8 = ((bf16[64,4,2048]{2,1,0:T(4,128)(2,1)}), bf16[64,4,2048]{2,1,0:T(4,128)(2,1)S(1)}, u32[]{:S(2)}, u32[]{:S(2)}) async-start(bf16[64,4,2048]{2,1,0:T(4,128)(2,1)} %get-tuple-element.133), calls=%async_computation.8 | async-start | bytes 2097152 | tf_op jit(solution)/shard_map/all_to_all | solution.py:183
  584.3 34.8 %all-to-all-start.9 = ((bf16[64,4,2048]{2,1,0:T(4,128)(2,1)}), bf16[64,4,2048]{2,1,0:T(4,128)(2,1)S(1)}, u32[]{:S(2)}, u32[]{:S(2)}) async-start(bf16[64,4,2048]{2,1,0:T(4,128)(2,1)} %get-tuple-element.183), calls=%async_computation.9 | async-start | bytes 2097152 | tf_op jit(solution)/shard_map/all_to_all | solution.py:183
  619.7 1.0 collective-permute-start.13
  622.4 34.8 %all-to-all-start.10 = ((bf16[64,4,2048]{2,1,0:T(4,128)(2,1)}), bf16[64,4,2048]{2,1,0:T(4,128)(2,1)S(1)}, u32[]{:S(2)}, u32[]{:S(2)}) async-start(bf16[64,4,2048]{2,1,0:T(4,128)(2,1)} %get-tuple-element.135), calls=%async_computation.10 | async-start | bytes 2097152 | tf_op jit(solution)/shard_map/all_to_all | solution.py:183
  664.7 34.8 %all-to-all-start.11 = ((bf16[64,4,2048]{2,1,0:T(4,128)(2,1)}), bf16[64,4,2048]{2,1,0:T(4,128)(2,1)S(1)}, u32[]{:S(2)}, u32[]{:S(2)}) async-start(bf16[64,4,2048]{2,1,0:T(4,128)(2,1)} %get-tuple-element.184), calls=%async_computation.11 | async-start | bytes 2097152 | tf_op jit(solution)/shard_map/all_to_all | solution.py:183
  670.9 29.2 %collective-permute-start.12 = (bf16[32,2048]{1,0:T(8,128)(2,1)S(1)}, bf16[32,2048]{1,0:T(8,128)(2,1)S(1)}, u32[]{:S(2)}, u32[]{:S(2)}) collective-permute-start(bf16[32,2048]{1,0:T(8,128)(2,1)S(1)} %shard_map.192), channel_id=1, source_target_pairs={{192,64},{193,65},{194,66},{195,67},{196,68},{197,69},{198,70},{19... | collective-permute-start | bytes 393224 | tf_op jit(solution)/shard_map/ppermute | solution.py:180
  (15 other events, 348.9 us)

commit v2 on v0

v2 whole, which is shorter than its diff:
```python
import functools

import jax
import jax.numpy as jnp
from jax import lax
from jax.experimental import pallas as pl
from jax.experimental.pallas import tpu as pltpu
from jax.sharding import PartitionSpec as P

EPSILON = 1e-06
SLOTS = 2
GROUP = 2 * SLOTS

OWN, UPPER, LOWER = 0, 1, 2

PAIRS = (
    ((2, 0, 0, 1),),
    ((0, 0, 0, 0), (3, 2, 0, 1)),
    ((0, 3, 1, 2),),
    ((2, 3, 1, 0),),
    ((3, 0, 1, 0),),
)
LAYERS = (
    (OWN, OWN, OWN, UPPER),
    (OWN, OWN, OWN, UPPER),
    (UPPER, OWN, LOWER, LOWER),
    (LOWER, UPPER, OWN, LOWER),
    (LOWER, OWN, UPPER, OWN),
)
TAKES = (
    ((1, 0, 0, 0),),
    ((0, 0, 0, 0), (1, 2, 0, 0)),
    ((1, 0, 0, 0),),
    ((0, 1, 1, 0),),
    ((0, 1, 1, 1),),
)


def looked_up(table, section):
    value = jnp.int32(table[0])
    for index in range(1, len(table)):
        value = jnp.where(section == index, jnp.int32(table[index]), value)
    return value


def picked(values, number):
    value = values[0]
    for index in range(1, len(values)):
        value = jnp.where(number == index, values[index], value)
    return value


def of_pair(refs, number, pair):
    both = [jnp.concatenate([ref[pair], ref[pair + 4]], axis=0) for ref in refs]
    return picked(both, number)


def chosen_places(ids, experts, scales=None):
    rows, choices = ids.shape
    block = rows // 2
    width = experts * GROUP
    source = lax.broadcasted_iota(jnp.int32, (rows, width), 0)
    place = lax.broadcasted_iota(jnp.int32, (rows, width), 1)
    expert = place // GROUP
    mine = source // block == (place // SLOTS) % 2
    named = jnp.zeros((rows, width), jnp.float32)
    scale = jnp.zeros((rows, width), jnp.float32)
    for choice in range(choices):
        same = jnp.logical_and(ids[:, choice : choice + 1] == expert, mine)
        named = jnp.where(same, 1.0, named)
        if scales is not None:
            scale = jnp.where(same, scales[:, choice : choice + 1], scale)
    row = lax.broadcasted_iota(jnp.int32, (rows, rows), 0)
    column = lax.broadcasted_iota(jnp.int32, (rows, rows), 1)
    before = jnp.where(column < row, 1.0, 0.0).astype(jnp.bfloat16)
    earlier = jnp.dot(before, named.astype(jnp.bfloat16), preferred_element_type=jnp.float32)
    chosen = jnp.logical_and(named > 0.0, earlier == (place % SLOTS).astype(jnp.float32))
    return jnp.where(chosen, named if scales is None else scale, 0.0)


def dispatch_kernel(step, kinds, counts, experts, section_ref, *refs):
    section = section_ref[0]
    gains, ids, refs = refs[:kinds], refs[kinds : 2 * kinds], refs[2 * kinds :]
    hidden_ref, out_ref = refs[-2:]
    layer = looked_up(LAYERS[step], section)
    gain = picked([ref[...] for ref in gains], layer)
    for lane, count in enumerate(counts):
        candidates, refs = refs[:count], refs[count:]
        hidden = picked([ref[...] for ref in candidates], looked_up(TAKES[step][lane], section))
        hidden_ref[lane] = hidden
        values = hidden.astype(jnp.float32)
        inverse = lax.rsqrt(jnp.mean(values * values, axis=-1, keepdims=True) + EPSILON)
        normed = (values * inverse * gain).astype(jnp.bfloat16)
        pair = looked_up(PAIRS[step][lane], section)
        placing = chosen_places(of_pair(ids, layer, pair), experts).T.astype(jnp.bfloat16)
        sent = jnp.dot(placing, normed, preferred_element_type=jnp.float32)
        out_ref[:, lane] = sent.astype(jnp.bfloat16).reshape(experts, GROUP, sent.shape[-1])


def in_parts(values, parts):
    total, start = None, 0
    for depth, part in parts:
        product = jnp.dot(values[:, start : start + depth], part, preferred_element_type=jnp.float32)
        total = product if total is None else total + product
        start += depth
    return total


def copy_kernel(source_ref, tie_ref, out_ref):
    out_ref[...] = source_ref[...]


def ffn_kernel(given, counts, section_ref, rows_ref, *refs):
    gates, refs = refs[: counts[0]], refs[counts[0] :]
    ups, refs = refs[: counts[1]], refs[counts[1] :]
    downs, refs = refs[: counts[2]], refs[counts[2] :]
    out_ref, activated, flat = refs[-3:]
    features = rows_ref.shape[-1]
    lanes = rows_ref.shape[1]
    units = gates[0].shape[1]
    cut = 256 if units % 256 == 0 else units
    wide = 512 if features % 512 == 0 else features
    for lane in range(lanes):
        flat[...] = rows_ref[:, lane].reshape(flat.shape)
        for start in range(0, units, cut):
            part = slice(start, start + cut)
            gate = in_parts(flat, [(ref.shape[0], ref[:, part]) for ref in gates])
            up = in_parts(flat, [(ref.shape[0], ref[:, part]) for ref in ups])
            activated[:, part] = (gate / (1.0 + jnp.exp(-gate)) * up).astype(jnp.bfloat16)
        for start in range(0, features, wide):
            part = slice(start, start + wide)
            made = in_parts(activated, [(ref.shape[0], ref[:, part]) for ref in downs])
            made = made.astype(jnp.bfloat16).reshape(out_ref.shape[0], GROUP, wide)
            if given is not None and lane == lanes - 1:
                made = jnp.where(section_ref[0] == given, refs[0][:, 0, :, part], made)
            out_ref[:, lane, :, part] = made


def combine_kernel(step, kinds, experts, last, section_ref, back_ref, hidden_ref, *refs):
    section = section_ref[0]
    ids, raw = refs[:kinds], refs[kinds : 2 * kinds]
    layer = looked_up(LAYERS[step], section)
    features = back_ref.shape[-1]
    lanes = back_ref.shape[1]
    outs = refs[-lanes:]
    for lane in range(lanes):
        pair = looked_up(PAIRS[step][lane], section)
        weights = of_pair(raw, layer, pair)
        weights = weights / jnp.sum(weights, axis=-1, keepdims=True)
        scale = chosen_places(of_pair(ids, layer, pair), experts, weights)
        high = scale.astype(jnp.bfloat16)
        low = (scale - high.astype(jnp.float32)).astype(jnp.bfloat16)
        back = back_ref[:, lane].reshape(experts * GROUP, features)
        mixed = jnp.dot(high, back, preferred_element_type=jnp.float32)
        mixed += jnp.dot(low, back, preferred_element_type=jnp.float32)
        made = (hidden_ref[lane].astype(jnp.float32) + mixed).astype(jnp.bfloat16)
        if last is None:
            outs[lane][...] = made
        else:
            made = jnp.where(section == last, refs[2 * kinds][...], made)
            block = made.shape[0] // 2
            outs[lane][0] = made[block:]
            outs[lane][1] = made[:block]


VMEM = pl.BlockSpec(memory_space=pltpu.VMEM)
SMEM = pl.BlockSpec(memory_space=pltpu.SMEM)
WHEREVER = pl.BlockSpec(memory_space=pl.ANY)


def limit(mebibytes):
    return pltpu.CompilerParams(vmem_limit_bytes=mebibytes * 1024 * 1024)


def dispatch(step, experts, section, gains, ids, lanes):
    rows, features = lanes[0][0].shape
    counts = tuple(len(lane) for lane in lanes)
    operands = (*gains, *ids, *(value for lane in lanes for value in lane))
    return pl.pallas_call(
        functools.partial(dispatch_kernel, step, len(gains), counts, experts),
        out_shape=(
            jax.ShapeDtypeStruct((len(lanes), rows, features), jnp.bfloat16),
            jax.ShapeDtypeStruct((experts, len(lanes), GROUP, features), jnp.bfloat16),
        ),
        in_specs=[SMEM] + [VMEM] * len(operands),
        out_specs=(VMEM, VMEM),
        compiler_params=limit(12),
    )(section, *operands)


def copied_after(value, tie):
    return pl.pallas_call(
        copy_kernel,
        out_shape=jax.ShapeDtypeStruct(value.shape, value.dtype),
        in_specs=[VMEM, WHEREVER],
        out_specs=VMEM,
        compiler_params=limit(12),
    )(value, tie)


def ffn(section, rows, weights, given=None, made=(), ties=()):
    sources, lanes, group, features = rows.shape
    units = weights[0][0].shape[1]
    height = sources * group
    counts = tuple(len(parts) for parts in weights)
    weights = [part for parts in weights for part in parts]
    return pl.pallas_call(
        functools.partial(ffn_kernel, given, counts),
        out_shape=jax.ShapeDtypeStruct(rows.shape, jnp.bfloat16),
        in_specs=[SMEM] + [VMEM] * (1 + len(weights) + len(made)) + [WHEREVER] * len(ties),
        out_specs=VMEM,
        scratch_shapes=[
            pltpu.VMEM((height, units), jnp.bfloat16),
            pltpu.VMEM((height, features), jnp.bfloat16),
        ],
        cost_estimate=pl.CostEstimate(
            flops=6 * lanes * height * features * units,
            bytes_accessed=6 * features * units + 4 * lanes * height * features,
            transcendentals=lanes * height * units,
        ),
        compiler_params=limit(20),
    )(section, rows, *weights, *made, *ties)


def combine(step, experts, section, back, hidden, ids, raw, ties=(), last=None, finished=()):
    lanes, rows, features = hidden.shape
    shape = (rows, features) if last is None else (2, rows // 2, features)
    operands = (back, hidden, *ids, *raw, *finished)
    return pl.pallas_call(
        functools.partial(combine_kernel, step, len(ids), experts, last),
        out_shape=tuple(jax.ShapeDtypeStruct(shape, jnp.bfloat16) for _ in range(lanes)),
        in_specs=[SMEM] + [VMEM] * len(operands) + [WHEREVER] * len(ties),
        out_specs=tuple(VMEM for _ in range(lanes)),
        compiler_params=limit(12),
    )(section, *operands, *ties)


def on_device(tokens, norm_gain, gate_proj, up_proj, down_proj, expert_ids, gate_weights):
    section = lax.axis_index("section")
    at = section.reshape(1)
    experts = lax.axis_size("expert")
    block, features = tokens.shape[1:]
    own = tokens.reshape(2 * block, features)

    def move(value, *route):
        return lax.ppermute(value, "section", route)

    def exchange(value):
        return lax.all_to_all(value, "expert", split_axis=0, concat_axis=0, tiled=True)

    downward = ((1, 0), (2, 1), (3, 2), (0, 3))
    upward = ((1, 2), (2, 3), (3, 0), (0, 1))
    small = (norm_gain, expert_ids[0], gate_weights[0])
    small_upper = tuple(move(value, *downward) for value in small)
    small_lower = tuple(move(value, *upward) for value in small)
    gains, ids, raw = zip(small, small_upper, small_lower)

    weights = ((gate_proj[0, 0],), (up_proj[0, 0],), (down_proj[0, 0],))
    gate, up, down = (jnp.split(parts[0], 2) for parts in weights)

    def layer_of(step, rows, held, ties=()):
        layer = looked_up(LAYERS[step], section)
        late = jnp.logical_and(layer == LOWER, section == 0)
        branches = [functools.partial(ffn, at, weights=value, ties=ties) for value in held]
        return lax.switch(jnp.where(late, LOWER + 1, layer), branches, rows)

    first_in = move(own, (2, 0))
    second_in = move(own, (1, 0))
    hidden, sent = dispatch(0, experts, at, gains[:2], ids[:2], [(own, first_in)])
    first = copied_after(weights[0][0], hidden)
    upper = [move(value, *downward[:3]) for value in (first, *up, *down)]
    lower_early = [move(value, *upward[:2]) for value in (first, *up, *down)]
    lower_late = [move(value, upward[2]) for value in (*gate, *up, *down)]
    rows = exchange(sent)
    away = move(rows, (3, 0))
    made = exchange(ffn(at, rows, weights))
    away = move(ffn(at, away, weights), (0, 3))
    ties = (upper[0], lower_early[0])
    (state,) = combine(0, experts, at, made, hidden, ids[:1], raw[:1], ties)
    state = move(state, (0, 1))

    hidden, sent = dispatch(1, experts, at, gains[:1], ids[:1], [(own,), (own, second_in, state)])
    rows = exchange(sent)
    ties = (upper[1], lower_early[1], lower_late[0], *small_lower, *small_upper)
    made = ffn(at, rows, weights, 3, (away,), ties)
    ties = (*upper[2:4], *lower_early[2:4], *lower_late[1:3])
    kept, state = combine(1, experts, at, exchange(made), hidden, ids[:2], raw[:2], ties)
    state = move(state, (0, 1), (1, 3), (3, 2))

    held = [weights]
    held += [(parts[:1], parts[1:3], parts[3:]) for parts in (upper, lower_early)]
    hidden, sent = dispatch(2, experts, at, gains, ids, [(state, kept)])
    rows = exchange(sent)
    made = exchange(layer_of(2, rows, held, (lower_late[3],)))
    (kept,) = combine(2, experts, at, made, hidden, ids, raw, (lower_late[4],))
    state = move(kept, (0, 3), (3, 0))

    held.append((lower_late[:2], lower_late[2:4], lower_late[4:]))
    hidden, sent = dispatch(3, experts, at, gains, ids, [(state, kept)])
    made = exchange(layer_of(3, exchange(sent), held))
    (kept,) = combine(3, experts, at, made, hidden, ids, raw)
    state = move(kept, (1, 0), (0, 1))

    hidden, sent = dispatch(4, experts, at, gains, ids, [(state, kept)])
    made = exchange(layer_of(4, exchange(sent), held))
    (finished,) = combine(4, experts, at, made, hidden, ids, raw, (), 1, (state,))
    return finished


def solution(mesh):
    return jax.shard_map(
        on_device,
        mesh=mesh,
        in_specs=(
            P("section", "expert", None),
            P("section", None),
            P("section", "expert", None, None),
            P("section", "expert", None, None),
            P("section", "expert", None, None),
            P("section", None, "expert", None),
            P("section", None, "expert", None),
        ),
        out_specs=P("section", "expert", None),
        check_vma=False,
    )
```

time: 769 us -> 628 us (0.82)
  waiting for transfers between devices: 413 us -> 335 us
  blocking collectives: 0 us -> 74.6 us
  matrix products: 67.7 us -> 0 us
  Pallas kernels: 0 us -> 58.3 us
  starting transfers between devices: 175 us -> 128 us
  local copies, waits for them, and re-layouts: 64.4 us -> 21.7 us
  other arithmetic: 42.6 us -> 0 us
    all_to_all x22 -> x8, waiting for transfers between devices: 351 us -> 76.8 us  [exchange(): lax.all_to_all(value, 'expert', split_axis=0, concat_axis=0, tiled=True)]
    ppermute x22 -> x30, waiting for transfers between devices: 62.3 us -> 259 us  [move(): return lax.ppermute(value, 'section', route)]
    all_to_all x0 -> x2, blocking collectives: none -> 74.6 us  [exchange(): lax.all_to_all(value, 'expert', split_axis=0, concat_axis=0, tiled=True)]
    dot_general x38 -> x0, matrix products: 67.7 us -> none  [the longest x8 35.1 us: expert_ffn(): jnp.dot(activated, w_down, preferred_element_type=jnp.float32)]
    all_to_all x22 -> x8, starting transfers between devices: 157 us -> 89.3 us  [exchange(): lax.all_to_all(value, 'expert', split_axis=0, concat_axis=0, tiled=True)]
    pallas_call x0 -> x17, Pallas kernels: none -> 58.3 us  [the longest x6 41.8 us: ffn(): pl.pallas_call(functools.partial(ffn_kernel, given, counts), out_shape=ja...]
    reduce_sum x44 -> x0, other arithmetic: 21.5 us -> none  [the longest x11 10.1 us: combine_rows(): return jnp.sum(picked.astype(jnp.float32) * weights[:, :, None], axis=1)]
    reshape x27 -> x0, local copies, waits for them, and re-layouts: 21.3 us -> none  [the longest x8 16.4 us: expert_ffn(): flattened = received.reshape(sources * slot_count, feature_count)]
  transfers between devices with their start and end apart: 44 -> 38, of which waited for: 33 -> 21; matrix products, arithmetic and copies ran while one was open for 6% -> 1% of each run, Pallas kernels for 0% -> 2%
where the time goes in v2:
time: 628 us; the launch traced here: 619 us
  waiting for transfers between devices  335 us (53%)
  starting transfers between devices  128 us (20%)
  blocking collectives  74.6 us (12%)
  Pallas kernels  58.3 us (9%)
  local copies, waits for them, and re-layouts  21.7 us (3%)
    ppermute x30, waiting for transfers between devices, move(): return lax.ppermute(value, 'section', route)  259 us
    all_to_all x8, starting transfers between devices, exchange(): lax.all_to_all(value, 'expert', split_axis=0, concat_axis=0, tiled=True)  89.3 us
    all_to_all x8, waiting for transfers between devices, exchange(): lax.all_to_all(value, 'expert', split_axis=0, concat_axis=0, tiled=True)  76.8 us
    all_to_all x2, blocking collectives, exchange(): lax.all_to_all(value, 'expert', split_axis=0, concat_axis=0, tiled=True)  74.6 us
    pallas_call x6, Pallas kernels, ffn(): pl.pallas_call(functools.partial(ffn_kernel, given, counts), out_shape=ja...  41.8 us
    ppermute x30, starting transfers between devices, move(): return lax.ppermute(value, 'section', route)  39 us
    unnamed x56, local copies, waits for them, and re-layouts  13.4 us
  transfers between devices with their start and end apart: 38, of which 21 were waited for; matrix products, arithmetic and copies ran while one was open for 1% of the time, Pallas kernels for 2%

profile of v2, /device:TPU:1, one launch (start us, length us, event | category | flops | bytes accessed | tf_op | source)
XLA Modules:
  0.0 619.1 jit_solution(4606334819132771279)
XLA Ops:
  11.5 13.9 %all-to-all-start = ((bf16[64,1,4,2048]{3,2,1,0:T(4,128)(2,1)}), bf16[64,1,4,2048]{3,2,1,0:T(4,128)(2,1)S(1)}, u32[]{:S(2)}, u32[]{:S(2)}) async-start(bf16[64,1,4,2048]{3,2,1,0:T(4,128)(2,1)} %get-tuple-element.259), calls=%async_computation | async-start | bytes 2097152 | tf_op jit(solution)/shard_map/all_to_all | solution.py:249
  32.8 21.1 %all-to-all-done.rows_ref = bf16[64,1,4,2048]{3,2,1,0:T(4,128)(2,1)S(1)} async-done(((bf16[64,1,4,2048]{3,2,1,0:T(4,128)(2,1)}), bf16[64,1,4,2048]{3,2,1,0:T(4,128)(2,1)S(1)}, u32[]{:S(2)}, u32[]{:S(2)}) %all-to-all-start) | async-done | bytes 1048608 | tf_op jit(solution)/shard_map/all_to_all | solution.py:249
  69.0 31.6 %collective-permute-done.6.refs_2_ = bf16[2048,768]{1,0:T(8,128)(2,1)} collective-permute-done((bf16[2048,768]{1,0:T(8,128)(2,1)}, bf16[2048,768]{1,0:T(8,128)(2,1)}, u32[]{:S(2)}, u32[]{:S(2)}) %collective-permute-start.6) | collective-permute-done | bytes 3145760 | tf_op jit(solution)/shard_map/ppermute | solution.py:246
  109.4 12.1 %all-to-all-start.2 = ((bf16[64,2,4,2048]{3,2,1,0:T(4,128)(2,1)}), bf16[64,2,4,2048]{3,2,1,0:T(4,128)(2,1)S(1)}, u32[]{:S(2)}, u32[]{:S(2)}) async-start(bf16[64,2,4,2048]{3,2,1,0:T(4,128)(2,1)} %copy-done.1), calls=%async_computation.2 | async-start | bytes 4194304 | tf_op jit(solution)/shard_map/all_to_all | solution.py:249
  131.5 17.4 %collective-permute-done.9.rows_ref = bf16[64,1,4,2048]{3,2,1,0:T(4,128)(2,1)S(1)} collective-permute-done((bf16[64,1,4,2048]{3,2,1,0:T(4,128)(2,1)S(1)}, bf16[64,1,4,2048]{3,2,1,0:T(4,128)(2,1)S(1)}, u32[]{:S(2)}, u32[]{:S(2)}) %collective-permute-start.9) | collective-permute-done | bytes 1048608 | tf_op jit(solution)/shard_map/ppermute | solution.py:246
  153.1 30.9 %collective-permute-done.3.refs_8_.refs_5_.refs_2_ = s32[8,16,8]{2,1,0:T(8,128)S(1)} collective-permute-done((s32[8,16,8]{2,1,0:T(8,128)S(1)}, s32[8,16,8]{2,1,0:T(8,128)S(1)}, u32[]{:S(2)}, u32[]{:S(2)}) %collective-permute-start.3) | collective-permute-done | bytes 4128 | tf_op jit(solution)/shard_map/ppermute | solution.py:246
  199.4 8.9 %shard_map.79 = bf16[64,2,4,2048]{3,2,1,0:T(4,128)(2,1)S(1)} custom-call(s32[1]{0:T(128)} %bitcast.section_ref, bf16[64,2,4,2048]{3,2,1,0:T(4,128)(2,1)S(1)} %all-to-all-done.2.rows_ref, bf16[2048,768]{1,0:T(8,128)(2,1)} %bitcast.45, bf16[2048,768]{1,0:T(8,128)(2,1)} %bitcast.51, bf16[768,2048]{1,0:T(8,128)(2,1)} %bitcast.57, ...), custom_call_target="tpu_custom_call" | custom-call | flops 4831838208 | bytes 13631488 | tf_op jit(solution)/shard_map/pallas_call | solution.py:207
  209.6 14.7 %all-to-all-start.3 = ((bf16[64,2,4,2048]{3,2,1,0:T(4,128)(2,1)}), bf16[64,2,4,2048]{3,2,1,0:T(4,128)(2,1)S(1)}, u32[]{:S(2)}, u32[]{:S(2)}) async-start(bf16[64,2,4,2048]{3,2,1,0:T(4,128)(2,1)} %copy-done), calls=%async_computation.3 | async-start | bytes 4194304 | tf_op jit(solution)/shard_map/all_to_all | solution.py:249
  233.5 28.7 %collective-permute-done.16.refs_4_ = bf16[1024,768]{1,0:T(8,128)(2,1)S(1)} collective-permute-done((bf16[1024,768]{1,0:T(8,128)(2,1)}, bf16[1024,768]{1,0:T(8,128)(2,1)S(1)}, u32[]{:S(2)}, u32[]{:S(2)}) %collective-permute-start.16) | collective-permute-done | bytes 1572896 | tf_op jit(solution)/shard_map/ppermute | solution.py:246
  263.9 32.1 %collective-permute-done.17.refs_5_ = bf16[384,2048]{1,0:T(8,128)(2,1)S(1)} collective-permute-done((bf16[384,2048]{1,0:T(8,128)(2,1)S(1)}, bf16[384,2048]{1,0:T(8,128)(2,1)S(1)}, u32[]{:S(2)}, u32[]{:S(2)}) %collective-permute-start.17) | collective-permute-done | bytes 1572896 | tf_op jit(solution)/shard_map/ppermute | solution.py:246
  310.8 12.2 %all-to-all-start.4 = ((bf16[64,1,4,2048]{3,2,1,0:T(4,128)(2,1)}), bf16[64,1,4,2048]{3,2,1,0:T(4,128)(2,1)S(1)}, u32[]{:S(2)}, u32[]{:S(2)}) async-start(bf16[64,1,4,2048]{3,2,1,0:T(4,128)(2,1)} %get-tuple-element.265), calls=%async_computation.4 | async-start | bytes 2097152 | tf_op jit(solution)/shard_map/all_to_all | solution.py:249
  327.3 35.1 %collective-permute-done.23 = bf16[1024,768]{1,0:T(8,128)(2,1)S(1)} collective-permute-done((bf16[1024,768]{1,0:T(8,128)(2,1)}, bf16[1024,768]{1,0:T(8,128)(2,1)S(1)}, u32[]{:S(2)}, u32[]{:S(2)}) %collective-permute-start.23) | collective-permute-done | bytes 1572896 | tf_op jit(solution)/shard_map/ppermute | solution.py:246
  364.8 7.8 %conditional.3 = (bf16[64,1,4,2048]{3,2,1,0:T(4,128)(2,1)}) conditional(s32[]{:T(128)} %clamp.11, (s32[1]{0:T(128)}, bf16[64,1,4,2048]{3,2,1,0:T(4,128)(2,1)S(1)}, bf16[2048,768]{1,0:T(8,128)(2,1)}, bf16[2048,768]{1,0:T(8,128)(2,1)}, bf16[768,2048]{1,0:T(8,128)(2,1)}, /*index=5*/bf16[1024,768]{1,0:T(8,128)(2,1)S(1)}) %tuple.69, ...), branch_computations={%region_0.1_spmd, %region_1.2_spmd, %region_2.3_spmd} | conditional | flops 2415919104 | bytes 11534344 | solution.py:265
  364.8 7.8 %branch_1_fun.3 = bf16[64,1,4,2048]{3,2,1,0:T(4,128)(2,1)} custom-call(s32[1]{0:T(128)} %get-tuple-element.176.section_ref, bf16[64,1,4,2048]{3,2,1,0:T(4,128)(2,1)S(1)} %get-tuple-element.178.rows_ref, bf16[2048,768]{1,0:T(8,128)(2,1)} %get-tuple-element.179.refs_0_, bf16[1024,768]{1,0:T(8,128)(2,1)} %get-tuple-element.180.refs_1_, ...), custom_call_target="tpu_custom_call" | custom-call | flops 2415919104 | bytes 11534336 | tf_op jit(solution)/shard_map/cond/branch_1_fun/pallas_call | solution.py:207
  372.6 11.0 %all-to-all-start.5 = ((bf16[64,1,4,2048]{3,2,1,0:T(4,128)(2,1)}), bf16[64,1,4,2048]{3,2,1,0:T(4,128)(2,1)S(1)}, u32[]{:S(2)}, u32[]{:S(2)}) async-start(bf16[64,1,4,2048]{3,2,1,0:T(4,128)(2,1)} %get-tuple-element.277), calls=%async_computation.5 | async-start | bytes 2097152 | tf_op jit(solution)/shard_map/all_to_all | solution.py:249
  384.9 37.6 %collective-permute-done.26.refs_6_ = bf16[384,2048]{1,0:T(8,128)(2,1)} collective-permute-done((bf16[384,2048]{1,0:T(8,128)(2,1)}, bf16[384,2048]{1,0:T(8,128)(2,1)}, u32[]{:S(2)}, u32[]{:S(2)}) %collective-permute-start.26) | collective-permute-done | bytes 1572896 | tf_op jit(solution)/shard_map/ppermute | solution.py:246
  431.9 12.4 %all-to-all-start.6 = ((bf16[64,1,4,2048]{3,2,1,0:T(4,128)(2,1)}), bf16[64,1,4,2048]{3,2,1,0:T(4,128)(2,1)S(1)}, u32[]{:S(2)}, u32[]{:S(2)}) async-start(bf16[64,1,4,2048]{3,2,1,0:T(4,128)(2,1)} %get-tuple-element.267), calls=%async_computation.6 | async-start | bytes 2097152 | tf_op jit(solution)/shard_map/all_to_all | solution.py:249
  445.6 27.2 %all-to-all-done.6 = bf16[64,1,4,2048]{3,2,1,0:T(4,128)(2,1)S(1)} async-done(((bf16[64,1,4,2048]{3,2,1,0:T(4,128)(2,1)}), bf16[64,1,4,2048]{3,2,1,0:T(4,128)(2,1)S(1)}, u32[]{:S(2)}, u32[]{:S(2)}) %all-to-all-start.6) | async-done | bytes 1048608 | tf_op jit(solution)/shard_map/all_to_all | solution.py:249
  472.9 10.4 %collective-permute-done.28 = bf16[384,2048]{1,0:T(8,128)(2,1)} collective-permute-done((bf16[384,2048]{1,0:T(8,128)(2,1)}, bf16[384,2048]{1,0:T(8,128)(2,1)}, u32[]{:S(2)}, u32[]{:S(2)}) %collective-permute-start.28) | collective-permute-done | bytes 1572896 | tf_op jit(solution)/shard_map/ppermute | solution.py:246
  490.6 39.8 %all_to_all.50.back_ref = bf16[64,1,4,2048]{3,2,1,0:T(4,128)(2,1)S(1)} all-to-all(bf16[64,1,4,2048]{3,2,1,0:T(4,128)(2,1)} %get-tuple-element.278), channel_id=1, replica_groups=mesh['section'=4,'expert'=64] {'expert'}, dimensions={0} | all-to-all | bytes 2097152 | tf_op jit(solution)/shard_map/all_to_all | solution.py:249
  546.5 28.4 %all-to-all-done.8 = bf16[64,1,4,2048]{3,2,1,0:T(4,128)(2,1)} async-done(((bf16[64,1,4,2048]{3,2,1,0:T(4,128)(2,1)}), bf16[64,1,4,2048]{3,2,1,0:T(4,128)(2,1)}, u32[]{:S(2)}, u32[]{:S(2)}) %all-to-all-start.8) | async-done | bytes 1048608 | tf_op jit(solution)/shard_map/all_to_all | solution.py:249
  574.9 7.8 %conditional.5 = (bf16[64,1,4,2048]{3,2,1,0:T(4,128)(2,1)}) conditional(s32[]{:T(128)} %clamp.9, (s32[1]{0:T(128)}, bf16[64,1,4,2048]{3,2,1,0:T(4,128)(2,1)}, bf16[2048,768]{1,0:T(8,128)(2,1)}, bf16[2048,768]{1,0:T(8,128)(2,1)}, bf16[768,2048]{1,0:T(8,128)(2,1)}) %tuple.71, (s32[1]{0:T(128)}, ...), branch_computations={%region_7.8_spmd, %region_8.9_spmd, %region_9.10_spmd, %region_10.... | conditional | flops 2415919104 | bytes 11534344 | solution.py:265
  575.1 7.6 %branch_3_fun.3 = bf16[64,1,4,2048]{3,2,1,0:T(4,128)(2,1)} custom-call(s32[1]{0:T(128)} %get-tuple-element.239.section_ref, bf16[64,1,4,2048]{3,2,1,0:T(4,128)(2,1)} %get-tuple-element.240.rows_ref, bf16[1024,768]{1,0:T(8,128)(2,1)} %get-tuple-element.241.refs_0_, bf16[1024,768]{1,0:T(8,128)(2,1)} %get-tuple-element.242.refs_1_, ...), custom_call_target="tpu_custom_call" | custom-call | flops 2415919104 | bytes 11534336 | tf_op jit(solution)/shard_map/cond/branch_3_fun/pallas_call | solution.py:207
  582.8 34.7 %all_to_all.51.back_ref = bf16[64,1,4,2048]{3,2,1,0:T(4,128)(2,1)S(1)} all-to-all(bf16[64,1,4,2048]{3,2,1,0:T(4,128)(2,1)} %get-tuple-element.279), channel_id=1, replica_groups=mesh['section'=4,'expert'=64] {'expert'}, dimensions={0} | all-to-all | bytes 2097152 | tf_op jit(solution)/shard_map/all_to_all | solution.py:249
  (133 shorter events, 149.7 us)
Async XLA Ops:
  11.5 42.4 %all-to-all-start = ((bf16[64,1,4,2048]{3,2,1,0:T(4,128)(2,1)}), bf16[64,1,4,2048]{3,2,1,0:T(4,128)(2,1)S(1)}, u32[]{:S(2)}, u32[]{:S(2)}) async-start(bf16[64,1,4,2048]{3,2,1,0:T(4,128)(2,1)} %get-tuple-element.259), calls=%async_computation | async-start | bytes 2097152 | tf_op jit(solution)/shard_map/all_to_all | solution.py:249
  29.2 71.4 %collective-permute-start.6 = (bf16[2048,768]{1,0:T(8,128)(2,1)}, bf16[2048,768]{1,0:T(8,128)(2,1)}, u32[]{:S(2)}, u32[]{:S(2)}) collective-permute-start(bf16[2048,768]{1,0:T(8,128)(2,1)} %shard_map.75), channel_id=1, source_target_pairs={{64,0},{128,64},{192,128},{65,1},{129,65},{193,129},{66,2},{130,66... | collective-permute-start | bytes 9437192 | tf_op jit(solution)/shard_map/ppermute | solution.py:246
  30.5 70.1 %collective-permute-start.7 = (bf16[2048,768]{1,0:T(8,128)(2,1)}, bf16[2048,768]{1,0:T(8,128)(2,1)}, u32[]{:S(2)}, u32[]{:S(2)}) collective-permute-start(bf16[2048,768]{1,0:T(8,128)(2,1)} %shard_map.75), channel_id=1, source_target_pairs={{64,128},{128,192},{65,129},{129,193},{66,130},{130,194},{67,131},... | collective-permute-start | bytes 9437192 | tf_op jit(solution)/shard_map/ppermute | solution.py:246
  61.3 39.3 %all-to-all-start.1 = ((bf16[64,1,4,2048]{3,2,1,0:T(4,128)(2,1)}), bf16[64,1,4,2048]{3,2,1,0:T(4,128)(2,1)S(1)}, u32[]{:S(2)}, u32[]{:S(2)}) async-start(bf16[64,1,4,2048]{3,2,1,0:T(4,128)(2,1)} %shard_map.74), calls=%async_computation.1 | async-start | bytes 2097152 | tf_op jit(solution)/shard_map/all_to_all | solution.py:249
  109.4 89.3 %all-to-all-start.2 = ((bf16[64,2,4,2048]{3,2,1,0:T(4,128)(2,1)}), bf16[64,2,4,2048]{3,2,1,0:T(4,128)(2,1)S(1)}, u32[]{:S(2)}, u32[]{:S(2)}) async-start(bf16[64,2,4,2048]{3,2,1,0:T(4,128)(2,1)} %copy-done.1), calls=%async_computation.2 | async-start | bytes 4194304 | tf_op jit(solution)/shard_map/all_to_all | solution.py:249
  126.3 69.5 %collective-permute-start.11 = (bf16[1024,768]{1,0:T(8,128)(2,1)S(1)}, bf16[1024,768]{1,0:T(8,128)(2,1)S(1)}, u32[]{:S(2)}, u32[]{:S(2)}) collective-permute-start(bf16[1024,768]{1,0:T(8,128)(2,1)S(1)} %get-tuple-element.276), channel_id=1, source_target_pairs={{64,0},{128,64},{192,128},{65,1},{129,65},{193,129},{66,2},{130,66... | collective-permute-start | bytes 4718600 | tf_op jit(solution)/shard_map/ppermute | solution.py:246
  127.6 68.2 %collective-permute-start.12 = (bf16[1024,768]{1,0:T(8,128)(2,1)S(1)}, bf16[1024,768]{1,0:T(8,128)(2,1)S(1)}, u32[]{:S(2)}, u32[]{:S(2)}) collective-permute-start(bf16[1024,768]{1,0:T(8,128)(2,1)S(1)} %get-tuple-element.276), channel_id=1, source_target_pairs={{64,128},{128,192},{65,129},{129,193},{66,130},{130,194},{67,131},... | collective-permute-start | bytes 4718600 | tf_op jit(solution)/shard_map/ppermute | solution.py:246
  129.7 66.0 %collective-permute-start.13 = (bf16[1024,768]{1,0:T(8,128)(2,1)S(1)}, bf16[1024,768]{1,0:T(8,128)(2,1)S(1)}, u32[]{:S(2)}, u32[]{:S(2)}) collective-permute-start(bf16[1024,768]{1,0:T(8,128)(2,1)S(1)} %get-tuple-element.274), channel_id=1, source_target_pairs={{192,0},{193,1},{194,2},{195,3},{196,4},{197,5},{198,6},{199,7},{2... | collective-permute-start | bytes 4718600 | tf_op jit(solution)/shard_map/ppermute | solution.py:246
  151.6 47.0 %collective-permute-start.10 = (bf16[64,1,4,2048]{3,2,1,0:T(4,128)(2,1)S(1)}, bf16[64,1,4,2048]{3,2,1,0:T(4,128)(2,1)S(1)}, u32[]{:S(2)}, u32[]{:S(2)}) collective-permute-start(bf16[64,1,4,2048]{3,2,1,0:T(4,128)(2,1)S(1)} %shard_map.78), channel_id=1, source_target_pairs={{0,192},{1,193},{2,194},{3,195},{4,196},{5,197},{6,198},{7,199},{8... | collective-permute-start | bytes 3145736 | tf_op jit(solution)/shard_map/ppermute | solution.py:246
  209.6 95.1 %all-to-all-start.3 = ((bf16[64,2,4,2048]{3,2,1,0:T(4,128)(2,1)}), bf16[64,2,4,2048]{3,2,1,0:T(4,128)(2,1)S(1)}, u32[]{:S(2)}, u32[]{:S(2)}) async-start(bf16[64,2,4,2048]{3,2,1,0:T(4,128)(2,1)} %copy-done), calls=%async_computation.3 | async-start | bytes 4194304 | tf_op jit(solution)/shard_map/all_to_all | solution.py:249
  224.3 37.9 %collective-permute-start.16 = (bf16[1024,768]{1,0:T(8,128)(2,1)}, bf16[1024,768]{1,0:T(8,128)(2,1)S(1)}, u32[]{:S(2)}, u32[]{:S(2)}) collective-permute-start(bf16[1024,768]{1,0:T(8,128)(2,1)} %get-tuple-element.275), channel_id=1, source_target_pairs={{64,0},{128,64},{192,128},{65,1},{129,65},{193,129},{66,2},{130,66... | collective-permute-start | bytes 4718600 | tf_op jit(solution)/shard_map/ppermute | solution.py:246
  225.9 70.1 %collective-permute-start.18 = (bf16[1024,768]{1,0:T(8,128)(2,1)}, bf16[1024,768]{1,0:T(8,128)(2,1)S(1)}, u32[]{:S(2)}, u32[]{:S(2)}) collective-permute-start(bf16[1024,768]{1,0:T(8,128)(2,1)} %get-tuple-element.275), channel_id=1, source_target_pairs={{64,128},{128,192},{65,129},{129,193},{66,130},{130,194},{67,131},... | collective-permute-start | bytes 4718600 | tf_op jit(solution)/shard_map/ppermute | solution.py:246
  230.1 65.9 %collective-permute-start.17 = (bf16[384,2048]{1,0:T(8,128)(2,1)S(1)}, bf16[384,2048]{1,0:T(8,128)(2,1)S(1)}, u32[]{:S(2)}, u32[]{:S(2)}) collective-permute-start(bf16[384,2048]{1,0:T(8,128)(2,1)S(1)} %get-tuple-element.272), channel_id=1, source_target_pairs={{64,0},{128,64},{192,128},{65,1},{129,65},{193,129},{66,2},{130,66... | collective-permute-start | bytes 4718600 | tf_op jit(solution)/shard_map/ppermute | solution.py:246
  231.4 64.6 %collective-permute-start.19 = (bf16[384,2048]{1,0:T(8,128)(2,1)S(1)}, bf16[384,2048]{1,0:T(8,128)(2,1)S(1)}, u32[]{:S(2)}, u32[]{:S(2)}) collective-permute-start(bf16[384,2048]{1,0:T(8,128)(2,1)S(1)} %get-tuple-element.272), channel_id=1, source_target_pairs={{64,128},{128,192},{65,129},{129,193},{66,130},{130,194},{67,131},... | collective-permute-start | bytes 4718600 | tf_op jit(solution)/shard_map/ppermute | solution.py:246
  232.2 63.8 %collective-permute-start.21 = (bf16[1024,768]{1,0:T(8,128)(2,1)S(1)}, bf16[1024,768]{1,0:T(8,128)(2,1)S(1)}, u32[]{:S(2)}, u32[]{:S(2)}) collective-permute-start(bf16[1024,768]{1,0:T(8,128)(2,1)S(1)} %copy-done.24), channel_id=1, source_target_pairs={{192,0},{193,1},{194,2},{195,3},{196,4},{197,5},{198,6},{199,7},{2... | collective-permute-start | bytes 4718600 | tf_op jit(solution)/shard_map/ppermute | solution.py:246
  262.2 42.4 %collective-permute-start.20 = (bf16[1024,768]{1,0:T(8,128)(2,1)S(1)}, bf16[1024,768]{1,0:T(8,128)(2,1)}, u32[]{:S(2)}, u32[]{:S(2)}) collective-permute-start(bf16[1024,768]{1,0:T(8,128)(2,1)S(1)} %copy-done.25), channel_id=1, source_target_pairs={{192,0},{193,1},{194,2},{195,3},{196,4},{197,5},{198,6},{199,7},{2... | collective-permute-start | bytes 4718600 | tf_op jit(solution)/shard_map/ppermute | solution.py:246
  310.8 51.7 %all-to-all-start.4 = ((bf16[64,1,4,2048]{3,2,1,0:T(4,128)(2,1)}), bf16[64,1,4,2048]{3,2,1,0:T(4,128)(2,1)S(1)}, u32[]{:S(2)}, u32[]{:S(2)}) async-start(bf16[64,1,4,2048]{3,2,1,0:T(4,128)(2,1)} %get-tuple-element.265), calls=%async_computation.4 | async-start | bytes 2097152 | tf_op jit(solution)/shard_map/all_to_all | solution.py:249
  322.9 39.6 %collective-permute-start.23 = (bf16[1024,768]{1,0:T(8,128)(2,1)}, bf16[1024,768]{1,0:T(8,128)(2,1)S(1)}, u32[]{:S(2)}, u32[]{:S(2)}) collective-permute-start(bf16[1024,768]{1,0:T(8,128)(2,1)} %get-tuple-element.275), channel_id=1, source_target_pairs={{192,0},{193,1},{194,2},{195,3},{196,4},{197,5},{198,6},{199,7},{2... | collective-permute-start | bytes 4718600 | tf_op jit(solution)/shard_map/ppermute | solution.py:246
  324.2 38.3 %collective-permute-start.25 = (bf16[384,2048]{1,0:T(8,128)(2,1)}, bf16[384,2048]{1,0:T(8,128)(2,1)}, u32[]{:S(2)}, u32[]{:S(2)}) collective-permute-start(bf16[384,2048]{1,0:T(8,128)(2,1)} %get-tuple-element.271), channel_id=1, source_target_pairs={{64,128},{128,192},{65,129},{129,193},{66,130},{130,194},{67,131},... | collective-permute-start | bytes 4718600 | tf_op jit(solution)/shard_map/ppermute | solution.py:246
  326.0 38.8 %collective-permute-start.24 = (bf16[384,2048]{1,0:T(8,128)(2,1)}, bf16[384,2048]{1,0:T(8,128)(2,1)}, u32[]{:S(2)}, u32[]{:S(2)}) collective-permute-start(bf16[384,2048]{1,0:T(8,128)(2,1)} %get-tuple-element.271), channel_id=1, source_target_pairs={{64,0},{128,64},{192,128},{65,1},{129,65},{193,129},{66,2},{130,66... | collective-permute-start | bytes 4718600 | tf_op jit(solution)/shard_map/ppermute | solution.py:246
  372.6 50.0 %all-to-all-start.5 = ((bf16[64,1,4,2048]{3,2,1,0:T(4,128)(2,1)}), bf16[64,1,4,2048]{3,2,1,0:T(4,128)(2,1)S(1)}, u32[]{:S(2)}, u32[]{:S(2)}) async-start(bf16[64,1,4,2048]{3,2,1,0:T(4,128)(2,1)} %get-tuple-element.277), calls=%async_computation.5 | async-start | bytes 2097152 | tf_op jit(solution)/shard_map/all_to_all | solution.py:249
  383.6 38.9 %collective-permute-start.26 = (bf16[384,2048]{1,0:T(8,128)(2,1)}, bf16[384,2048]{1,0:T(8,128)(2,1)}, u32[]{:S(2)}, u32[]{:S(2)}) collective-permute-start(bf16[384,2048]{1,0:T(8,128)(2,1)} %copy-done.22), channel_id=1, source_target_pairs={{192,0},{193,1},{194,2},{195,3},{196,4},{197,5},{198,6},{199,7},{2... | collective-permute-start | bytes 4718600 | tf_op jit(solution)/shard_map/ppermute | solution.py:246
  431.9 41.0 %all-to-all-start.6 = ((bf16[64,1,4,2048]{3,2,1,0:T(4,128)(2,1)}), bf16[64,1,4,2048]{3,2,1,0:T(4,128)(2,1)S(1)}, u32[]{:S(2)}, u32[]{:S(2)}) async-start(bf16[64,1,4,2048]{3,2,1,0:T(4,128)(2,1)} %get-tuple-element.267), calls=%async_computation.6 | async-start | bytes 2097152 | tf_op jit(solution)/shard_map/all_to_all | solution.py:249
  444.3 38.9 %collective-permute-start.28 = (bf16[384,2048]{1,0:T(8,128)(2,1)}, bf16[384,2048]{1,0:T(8,128)(2,1)}, u32[]{:S(2)}, u32[]{:S(2)}) collective-permute-start(bf16[384,2048]{1,0:T(8,128)(2,1)} %get-tuple-element.271), channel_id=1, source_target_pairs={{192,0},{193,1},{194,2},{195,3},{196,4},{197,5},{198,6},{199,7},{2... | collective-permute-start | bytes 4718600 | tf_op jit(solution)/shard_map/ppermute | solution.py:246
  (41 other events, 554.0 us)

commit v3 on v2

--- a/solution.py
+++ b/solution.py
@@ -97,43 +97,98 @@
         out_ref[:, lane] = sent.astype(jnp.bfloat16).reshape(experts, GROUP, sent.shape[-1])
 
 
-def in_parts(values, parts):
-    total, start = None, 0
-    for depth, part in parts:
-        product = jnp.dot(values[:, start : start + depth], part, preferred_element_type=jnp.float32)
-        total = product if total is None else total + product
-        start += depth
-    return total
-
-
-def copy_kernel(source_ref, tie_ref, out_ref):
-    out_ref[...] = source_ref[...]
-
-
-def ffn_kernel(given, counts, section_ref, rows_ref, *refs):
-    gates, refs = refs[: counts[0]], refs[counts[0] :]
-    ups, refs = refs[: counts[1]], refs[counts[1] :]
-    downs, refs = refs[: counts[2]], refs[counts[2] :]
-    out_ref, activated, flat = refs[-3:]
-    features = rows_ref.shape[-1]
-    lanes = rows_ref.shape[1]
-    units = gates[0].shape[1]
-    cut = 256 if units % 256 == 0 else units
-    wide = 512 if features % 512 == 0 else features
+def pieces(features, units, width):
+    panels = units // width
+    order = [number for panel in range(panels) for number in (panel, panels + panel)]
+    spans = [(number * features, features) for number in order]
+    each = units * (2 if features // width % 2 == 0 else 1)
+    first = 2 * panels * features
+    return spans + [(start, each) for start in range(first, first + units * features // width, each)]
+
+
+def pack_kernel(width, *refs):
+    gate_ref, up_ref, down_ref = refs[:3]
+    out_ref, done = refs[-2:]
+    features, units = gate_ref.shape
+    copies, start = [], 0
+    for ref in (gate_ref, up_ref, down_ref):
+        for column in range(0, ref.shape[1], width):
+            to = out_ref.at[pl.ds(start, ref.shape[0]), :]
+            copies.append(pltpu.make_async_copy(ref.at[:, pl.ds(column, width)], to, done.at[len(copies)]))
+            start += ref.shape[0]
+    for copy in copies:
+        copy.start()
+    for copy in copies:
+        copy.wait()
+
+
+def ffn_kernel(step, given, held, section_ref, rows_ref, *refs):
+    layers, refs = refs[:held], refs[held:]
+    out_ref, weights, activated, flat, arrived = refs[-5:]
+    experts, lanes, _, features = rows_ref.shape
+    units = activated.shape[-1]
+    width = weights.shape[1]
+    panels = units // width
+    section = section_ref[0]
+    spans = pieces(features, units, width)
+
+    def copies(ref):
+        for number, (start, size) in enumerate(spans):
+            rows = pl.ds(start, size)
+            yield pltpu.make_async_copy(ref.at[rows, :], weights.at[rows, :], arrived.at[number])
+
+    if held == 1:
+        for copy in copies(layers[0]):
+            copy.start()
+    else:
+        layer = looked_up(LAYERS[step], section)
+        layer = jnp.where(jnp.logical_and(layer == LOWER, section == 0), LOWER + 1, layer)
+        for number, ref in enumerate(layers):
+
+            @pl.when(layer == number)
+            def _(ref=ref):
+                for copy in copies(ref):
+                    copy.start()
+
+    def arrival(number, start, size):
+        rows = pl.ds(pl.multiple_of(start, width), size)
+        pltpu.make_async_copy(layers[0].at[rows, :], weights.at[rows, :], arrived.at[number]).wait()
+
     for lane in range(lanes):
-        flat[...] = rows_ref[:, lane].reshape(flat.shape)
-        for start in range(0, units, cut):
-            part = slice(start, start + cut)
-            gate = in_parts(flat, [(ref.shape[0], ref[:, part]) for ref in gates])
-            up = in_parts(flat, [(ref.shape[0], ref[:, part]) for ref in ups])
-            activated[:, part] = (gate / (1.0 + jnp.exp(-gate)) * up).astype(jnp.bfloat16)
-        for start in range(0, features, wide):
-            part = slice(start, start + wide)
-            made = in_parts(activated, [(ref.shape[0], ref[:, part]) for ref in downs])
-            made = made.astype(jnp.bfloat16).reshape(out_ref.shape[0], GROUP, wide)
-            if given is not None and lane == lanes - 1:
-                made = jnp.where(section_ref[0] == given, refs[0][:, 0, :, part], made)
-            out_ref[:, lane, :, part] = made
+        flat[lane] = rows_ref[:, lane].reshape(flat.shape[1:])
+
+    def widen(panel, _):
+        start = panel * features
+        arrival(2 * panel, start, features)
+        arrival(2 * panel + 1, start + panels * features, features)
+        gates = weights[pl.ds(pl.multiple_of(start, width), features)]
+        ups = weights[pl.ds(pl.multiple_of(start + panels * features, width), features)]
+        part = pl.ds(pl.multiple_of(panel * width, width), width)
+        for lane in range(lanes):
+            gate = jnp.dot(flat[lane], gates, preferred_element_type=jnp.float32)
+            up = jnp.dot(flat[lane], ups, preferred_element_type=jnp.float32)
+            activated[lane, :, part] = (gate / (1.0 + jnp.exp(-gate)) * up).astype(jnp.bfloat16)
+        return 0
+
+    lax.fori_loop(0, panels, widen, 0)
+    size = spans[-1][1]
+
+    def narrow(number, _):
+        first = 2 * panels * features + number * size
+        arrival(2 * panels + number, first, size)
+        for inner in range(size // units):
+            down = weights[pl.ds(pl.multiple_of(first + inner * units, width), units)]
+            column = (number * (size // units) + inner) * width
+            part = pl.ds(pl.multiple_of(column, width), width)
+            for lane in range(lanes):
+                made = jnp.dot(activated[lane], down, preferred_element_type=jnp.float32)
+                made = made.astype(jnp.bfloat16).reshape(experts, GROUP, width)
+                if given is not None and lane == lanes - 1:
+                    made = jnp.where(section == given, refs[0][:, 0, :, part], made)
+                out_ref[:, lane, :, part] = made
+        return 0
+
+    lax.fori_loop(0, len(spans) - 2 * panels, narrow, 0)
 
 
 def combine_kernel(step, kinds, experts, last, section_ref, back_ref, hidden_ref, *refs):
@@ -172,7 +227,7 @@
     return pltpu.CompilerParams(vmem_limit_bytes=mebibytes * 1024 * 1024)
 
 
-def dispatch(step, experts, section, gains, ids, lanes):
+def dispatch(step, experts, section, gains, ids, lanes, ties=()):
     rows, features = lanes[0][0].shape
     counts = tuple(len(lane) for lane in lanes)
     operands = (*gains, *ids, *(value for lane in lanes for value in lane))
@@ -182,44 +237,48 @@
             jax.ShapeDtypeStruct((len(lanes), rows, features), jnp.bfloat16),
             jax.ShapeDtypeStruct((experts, len(lanes), GROUP, features), jnp.bfloat16),
         ),
-        in_specs=[SMEM] + [VMEM] * len(operands),
+        in_specs=[SMEM] + [VMEM] * len(operands) + [WHEREVER] * len(ties),
         out_specs=(VMEM, VMEM),
         compiler_params=limit(12),
-    )(section, *operands)
-
-
-def copied_after(value, tie):
+    )(section, *operands, *ties)
+
+
+def packed(gate, up, down, ties):
+    features, units = gate.shape
+    width = 256 if units % 256 == 0 and features % 256 == 0 else units
     return pl.pallas_call(
-        copy_kernel,
-        out_shape=jax.ShapeDtypeStruct(value.shape, value.dtype),
-        in_specs=[VMEM, WHEREVER],
-        out_specs=VMEM,
-        compiler_params=limit(12),
-    )(value, tie)
-
-
-def ffn(section, rows, weights, given=None, made=(), ties=()):
-    sources, lanes, group, features = rows.shape
-    units = weights[0][0].shape[1]
-    height = sources * group
-    counts = tuple(len(parts) for parts in weights)
-    weights = [part for parts in weights for part in parts]
+        functools.partial(pack_kernel, width),
+        out_shape=jax.ShapeDtypeStruct((3 * features * units // width, width), gate.dtype),
+        in_specs=[WHEREVER] * (3 + len(ties)),
+        out_specs=WHEREVER,
+        scratch_shapes=[pltpu.SemaphoreType.DMA((2 * units // width + features // width,))],
+        compiler_params=limit(4),
+    )(gate, up, down, *ties)
+
+
+def ffn(step, section, rows, layers, given=None, made=(), ties=()):
+    experts, lanes, group, features = rows.shape
+    length, width = layers[0].shape
+    units = length * width // (3 * features)
+    height = experts * group
     return pl.pallas_call(
-        functools.partial(ffn_kernel, given, counts),
+        functools.partial(ffn_kernel, step, given, len(layers)),
         out_shape=jax.ShapeDtypeStruct(rows.shape, jnp.bfloat16),
-        in_specs=[SMEM] + [VMEM] * (1 + len(weights) + len(made)) + [WHEREVER] * len(ties),
+        in_specs=[SMEM, VMEM] + [WHEREVER] * len(layers) + [VMEM] * len(made) + [WHEREVER] * len(ties),
         out_specs=VMEM,
         scratch_shapes=[
-            pltpu.VMEM((height, units), jnp.bfloat16),
-            pltpu.VMEM((height, features), jnp.bfloat16),
+            pltpu.VMEM((length, width), jnp.bfloat16),
+            pltpu.VMEM((lanes, height, units), jnp.bfloat16),
+            pltpu.VMEM((lanes, height, features), jnp.bfloat16),
+            pltpu.SemaphoreType.DMA((len(pieces(features, units, width)),)),
         ],
         cost_estimate=pl.CostEstimate(
             flops=6 * lanes * height * features * units,
             bytes_accessed=6 * features * units + 4 * lanes * height * features,
             transcendentals=lanes * height * units,
         ),
-        compiler_params=limit(20),
-    )(section, rows, *weights, *made, *ties)
+        compiler_params=limit(28),
+    )(section, rows, *layers, *made, *ties)
 
 
 def combine(step, experts, section, back, hidden, ids, raw, ties=(), last=None, finished=()):
@@ -255,54 +314,41 @@
     small_lower = tuple(move(value, *upward) for value in small)
     gains, ids, raw = zip(small, small_upper, small_lower)
 
-    weights = ((gate_proj[0, 0],), (up_proj[0, 0],), (down_proj[0, 0],))
-    gate, up, down = (jnp.split(parts[0], 2) for parts in weights)
-
-    def layer_of(step, rows, held, ties=()):
-        layer = looked_up(LAYERS[step], section)
-        late = jnp.logical_and(layer == LOWER, section == 0)
-        branches = [functools.partial(ffn, at, weights=value, ties=ties) for value in held]
-        return lax.switch(jnp.where(late, LOWER + 1, layer), branches, rows)
+    weights = (gate_proj[0, 0], up_proj[0, 0], down_proj[0, 0])
 
     first_in = move(own, (2, 0))
     second_in = move(own, (1, 0))
     hidden, sent = dispatch(0, experts, at, gains[:2], ids[:2], [(own, first_in)])
-    first = copied_after(weights[0][0], hidden)
-    upper = [move(value, *downward[:3]) for value in (first, *up, *down)]
-    lower_early = [move(value, *upward[:2]) for value in (first, *up, *down)]
-    lower_late = [move(value, upward[2]) for value in (*gate, *up, *down)]
+    layer = packed(*weights, (hidden, second_in, *small_upper, *small_lower))
+    upper = move(layer, *downward[:3])
+    lower_early = move(layer, *upward[:2])
     rows = exchange(sent)
     away = move(rows, (3, 0))
-    made = exchange(ffn(at, rows, weights))
-    away = move(ffn(at, away, weights), (0, 3))
-    ties = (upper[0], lower_early[0])
-    (state,) = combine(0, experts, at, made, hidden, ids[:1], raw[:1], ties)
+    made = exchange(ffn(0, at, rows, [layer]))
+    (state,) = combine(0, experts, at, made, hidden, ids[:1], raw[:1], (away,))
     state = move(state, (0, 1))
 
+    lower_late = move(packed(*weights, (away,)), upward[2])
+    away = move(ffn(0, at, away, [layer]), (0, 3))
     hidden, sent = dispatch(1, experts, at, gains[:1], ids[:1], [(own,), (own, second_in, state)])
-    rows = exchange(sent)
-    ties = (upper[1], lower_early[1], lower_late[0], *small_lower, *small_upper)
-    made = ffn(at, rows, weights, 3, (away,), ties)
-    ties = (*upper[2:4], *lower_early[2:4], *lower_late[1:3])
-    kept, state = combine(1, experts, at, exchange(made), hidden, ids[:2], raw[:2], ties)
+    made = ffn(1, at, exchange(sent), [layer], 3, (away,))
+    kept, state = combine(1, experts, at, exchange(made), hidden, ids[:2], raw[:2])
     state = move(state, (0, 1), (1, 3), (3, 2))
 
-    held = [weights]
-    held += [(parts[:1], parts[1:3], parts[3:]) for parts in (upper, lower_early)]
-    hidden, sent = dispatch(2, experts, at, gains, ids, [(state, kept)])
-    rows = exchange(sent)
-    made = exchange(layer_of(2, rows, held, (lower_late[3],)))
-    (kept,) = combine(2, experts, at, made, hidden, ids, raw, (lower_late[4],))
+    layers = [layer, upper, lower_early]
+    hidden, sent = dispatch(2, experts, at, gains, ids, [(state, kept)], layers[1:])
+    made = exchange(ffn(2, at, exchange(sent), layers))
+    (kept,) = combine(2, experts, at, made, hidden, ids, raw)
     state = move(kept, (0, 3), (3, 0))
 
-    held.append((lower_late[:2], lower_late[2:4], lower_late[4:]))
-    hidden, sent = dispatch(3, experts, at, gains, ids, [(state, kept)])
-    made = exchange(layer_of(3, exchange(sent), held))
+    layers.append(lower_late)
+    hidden, sent = dispatch(3, experts, at, gains, ids, [(state, kept)], layers[3:])
+    made = exchange(ffn(3, at, exchange(sent), layers))
     (kept,) = combine(3, experts, at, made, hidden, ids, raw)
     state = move(kept, (1, 0), (0, 1))
 
     hidden, sent = dispatch(4, experts, at, gains, ids, [(state, kept)])
-    made = exchange(layer_of(4, exchange(sent), held))
+    made = exchange(ffn(4, at, exchange(sent), layers))
     (finished,) = combine(4, experts, at, made, hidden, ids, raw, (), 1, (state,))
     return finished
 

time: 628 us -> 535 us (0.85); the launches traced: 619 us -> 534 us
  waiting for transfers between devices: 335 us -> 119 us
  blocking collectives: 74.6 us -> 271 us
  starting transfers between devices: 128 us -> 64.4 us
  Pallas kernels: 58.3 us -> 48.4 us
  local copies, waits for them, and re-layouts: 21.7 us -> 30.6 us
    all_to_all x2 -> x7, blocking collectives: 74.6 us -> 271 us  [exchange(): lax.all_to_all(value, 'expert', split_axis=0, concat_axis=0, tiled=True)]
    ppermute x30 -> x17, waiting for transfers between devices: 259 us -> 93.5 us  [move(): return lax.ppermute(value, 'section', route)]
    all_to_all x8 -> x3, starting transfers between devices: 89.3 us -> 29.7 us  [exchange(): lax.all_to_all(value, 'expert', split_axis=0, concat_axis=0, tiled=True)]
    all_to_all x8 -> x3, waiting for transfers between devices: 76.8 us -> 25.9 us  [exchange(): lax.all_to_all(value, 'expert', split_axis=0, concat_axis=0, tiled=True)]
    unnamed x56 -> x58, local copies, waits for them, and re-layouts: 13.4 us -> 30.6 us
    split x3 -> x0, local copies, waits for them, and re-layouts: 8.3 us -> none  [on_device(): gate, up, down = (jnp.split(parts[0], 2) for parts in weights)]
    pallas_call x7 -> x8, Pallas kernels: 45.6 us -> 38.7 us  [the longest x6 34 us: ffn(): pl.pallas_call(functools.partial(ffn_kernel, step, given, len(layers)), o...]
    ppermute x30 -> x17, starting transfers between devices: 39 us -> 34.7 us  [move(): return lax.ppermute(value, 'section', route)]
  transfers between devices with their start and end apart: 38 -> 20, of which waited for: 21 -> 12; matrix products, arithmetic and copies ran while one was open for 1% -> 0% of each run, Pallas kernels for 2% -> 5%
where the time goes in v3:
time: 535 us; the launch traced here: 534 us
  blocking collectives  271 us (51%)
  waiting for transfers between devices  119 us (22%)
  starting transfers between devices  64.4 us (12%)
  Pallas kernels  48.4 us (9%)
  local copies, waits for them, and re-layouts  30.6 us (6%)
    all_to_all x7, blocking collectives, exchange(): lax.all_to_all(value, 'expert', split_axis=0, concat_axis=0, tiled=True)  271 us
    ppermute x17, waiting for transfers between devices, move(): return lax.ppermute(value, 'section', route)  93.5 us
    ppermute x17, starting transfers between devices, move(): return lax.ppermute(value, 'section', route)  34.7 us
    pallas_call x6, Pallas kernels, ffn(): pl.pallas_call(functools.partial(ffn_kernel, step, given, len(layers)), o...  34 us
    unnamed x58, local copies, waits for them, and re-layouts  30.6 us
    all_to_all x3, starting transfers between devices, exchange(): lax.all_to_all(value, 'expert', split_axis=0, concat_axis=0, tiled=True)  29.7 us
    all_to_all x3, waiting for transfers between devices, exchange(): lax.all_to_all(value, 'expert', split_axis=0, concat_axis=0, tiled=True)  25.9 us
  transfers between devices with their start and end apart: 20, of which 12 were waited for; matrix products, arithmetic and copies ran while one was open for 0% of the time, Pallas kernels for 5%

profile of v3, /device:TPU:1, one launch (start us, length us, event | category | flops | bytes accessed | tf_op | source)
XLA Modules:
  0.0 534.1 jit_solution(6348462476291306441)
XLA Ops:
  11.5 13.9 %all-to-all-start = ((bf16[64,1,4,2048]{3,2,1,0:T(4,128)(2,1)}), bf16[64,1,4,2048]{3,2,1,0:T(4,128)(2,1)S(1)}, u32[]{:S(2)}, u32[]{:S(2)}) async-start(bf16[64,1,4,2048]{3,2,1,0:T(4,128)(2,1)} %get-tuple-element.17), calls=%async_computation | async-start | bytes 2097152 | tf_op jit(solution)/shard_map/all_to_all | solution.py:308
  47.4 6.5 %all-to-all-done.rows_ref = bf16[64,1,4,2048]{3,2,1,0:T(4,128)(2,1)S(1)} async-done(((bf16[64,1,4,2048]{3,2,1,0:T(4,128)(2,1)}), bf16[64,1,4,2048]{3,2,1,0:T(4,128)(2,1)S(1)}, u32[]{:S(2)}, u32[]{:S(2)}) %all-to-all-start) | async-done | bytes 1048608 | tf_op jit(solution)/shard_map/all_to_all | solution.py:308
  57.6 5.7 %shard_map.75 = bf16[64,1,4,2048]{3,2,1,0:T(4,128)(2,1)} custom-call(s32[1]{0:T(128)} %bitcast.section_ref, bf16[64,1,4,2048]{3,2,1,0:T(4,128)(2,1)S(1)} %all-to-all-done.rows_ref, bf16[18432,256]{1,0:T(8,128)(2,1)S(1)} %copy-done.1), custom_call_target="tpu_custom_call" | custom-call | flops 2415919104 | bytes 11534336 | tf_op jit(solution)/shard_map/pallas_call | solution.py:264
  63.3 6.2 %all-to-all-start.1 = ((bf16[64,1,4,2048]{3,2,1,0:T(4,128)(2,1)}), bf16[64,1,4,2048]{3,2,1,0:T(4,128)(2,1)S(1)}, u32[]{:S(2)}, u32[]{:S(2)}) async-start(bf16[64,1,4,2048]{3,2,1,0:T(4,128)(2,1)} %shard_map.75), calls=%async_computation.1 | async-start | bytes 2097152 | tf_op jit(solution)/shard_map/all_to_all | solution.py:308
  70.8 4.3 collective-permute-start.13
  76.4 20.5 %collective-permute-done.8.refs_2_.rows_ref.refs_3_ = bf16[64,1,4,2048]{3,2,1,0:T(4,128)(2,1)S(1)} collective-permute-done((bf16[64,1,4,2048]{3,2,1,0:T(4,128)(2,1)S(1)}, bf16[64,1,4,2048]{3,2,1,0:T(4,128)(2,1)S(1)}, u32[]{:S(2)}, u32[]{:S(2)}) %collective-permute-start.8) | collective-permute-done | bytes 1048608 | tf_op jit(solution)/shard_map/ppermute | solution.py:305
  108.9 9.7 %all-to-all-start.2 = ((bf16[64,2,4,2048]{3,2,1,0:T(4,128)(2,1)}), bf16[64,2,4,2048]{3,2,1,0:T(4,128)(2,1)S(1)}, u32[]{:S(2)}, u32[]{:S(2)}) async-start(bf16[64,2,4,2048]{3,2,1,0:T(4,128)(2,1)} %copy-done.10), calls=%async_computation.2 | async-start | bytes 4194304 | tf_op jit(solution)/shard_map/all_to_all | solution.py:308
  122.3 4.6 shard_map.78
  133.4 17.2 %collective-permute-done.10.refs_1_ = bf16[64,1,4,2048]{3,2,1,0:T(4,128)(2,1)S(1)} collective-permute-done((bf16[64,1,4,2048]{3,2,1,0:T(4,128)(2,1)S(1)}, bf16[64,1,4,2048]{3,2,1,0:T(4,128)(2,1)S(1)}, u32[]{:S(2)}, u32[]{:S(2)}) %collective-permute-start.10) | collective-permute-done | bytes 1048608 | tf_op jit(solution)/shard_map/ppermute | solution.py:305
  151.6 18.3 %all-to-all-done.2.rows_ref = bf16[64,2,4,2048]{3,2,1,0:T(4,128)(2,1)S(1)} async-done(((bf16[64,2,4,2048]{3,2,1,0:T(4,128)(2,1)}), bf16[64,2,4,2048]{3,2,1,0:T(4,128)(2,1)S(1)}, u32[]{:S(2)}, u32[]{:S(2)}) %all-to-all-start.2) | async-done | bytes 2097184 | tf_op jit(solution)/shard_map/all_to_all | solution.py:308
  174.7 7.2 %shard_map.79 = bf16[64,2,4,2048]{3,2,1,0:T(4,128)(2,1)S(1)} custom-call(s32[1]{0:T(128)} %bitcast.section_ref, bf16[64,2,4,2048]{3,2,1,0:T(4,128)(2,1)S(1)} %all-to-all-done.2.rows_ref, bf16[18432,256]{1,0:T(8,128)(2,1)S(1)} %copy-done.3, bf16[64,1,4,2048]{3,2,1,0:T(4,128)(2,1)S(1)} %copy-done.24), custom_call_target="tpu_custom_call" | custom-call | flops 4831838208 | bytes 13631488 | tf_op jit(solution)/shard_map/pallas_call | solution.py:264
  181.9 57.0 %all_to_all.50.back_ref = bf16[64,2,4,2048]{3,2,1,0:T(4,128)(2,1)S(1)} all-to-all(bf16[64,2,4,2048]{3,2,1,0:T(4,128)(2,1)S(1)} %shard_map.79), channel_id=1, replica_groups=mesh['section'=4,'expert'=64] {'expert'}, dimensions={0} | all-to-all | bytes 4194304 | tf_op jit(solution)/shard_map/all_to_all | solution.py:308
  244.2 37.5 %collective-permute-done.12.refs_8_.refs_1_ = bf16[18432,256]{1,0:T(8,128)(2,1)} collective-permute-done((bf16[18432,256]{1,0:T(8,128)(2,1)}, bf16[18432,256]{1,0:T(8,128)(2,1)}, u32[]{:S(2)}, u32[]{:S(2)}) %collective-permute-start.12) | collective-permute-done | bytes 9437216 | tf_op jit(solution)/shard_map/ppermute | solution.py:305
  282.5 40.7 %all_to_all.51.rows_ref = bf16[64,1,4,2048]{3,2,1,0:T(4,128)(2,1)S(1)} all-to-all(bf16[64,1,4,2048]{3,2,1,0:T(4,128)(2,1)S(1)} %get-tuple-element.23), channel_id=1, replica_groups=mesh['section'=4,'expert'=64] {'expert'}, dimensions={0} | all-to-all | bytes 2097152 | tf_op jit(solution)/shard_map/all_to_all | solution.py:308
  323.2 5.5 %shard_map.82 = bf16[64,1,4,2048]{3,2,1,0:T(4,128)(2,1)S(1)} custom-call(s32[1]{0:T(128)} %bitcast.section_ref, bf16[64,1,4,2048]{3,2,1,0:T(4,128)(2,1)S(1)} %all_to_all.51.rows_ref, bf16[18432,256]{1,0:T(8,128)(2,1)S(1)} %bitcast.8, bf16[18432,256]{1,0:T(8,128)(2,1)} %collective-permute-done.12.refs_8_.refs_1_, ...), custom_call_target="tpu_custom_call" | custom-call | flops 2415919104 | bytes 11534336 | tf_op jit(solution)/shard_map/pallas_call | solution.py:264
  328.7 34.6 %all_to_all.52.back_ref = bf16[64,1,4,2048]{3,2,1,0:T(4,128)(2,1)S(1)} all-to-all(bf16[64,1,4,2048]{3,2,1,0:T(4,128)(2,1)S(1)} %shard_map.82), channel_id=1, replica_groups=mesh['section'=4,'expert'=64] {'expert'}, dimensions={0} | all-to-all | bytes 2097152 | tf_op jit(solution)/shard_map/all_to_all | solution.py:308
  363.9 6.2 %collective-permute-start.14 = (bf16[32,2048]{1,0:T(8,128)(2,1)S(1)}, bf16[32,2048]{1,0:T(8,128)(2,1)S(1)}, u32[]{:S(2)}, u32[]{:S(2)}) collective-permute-start(bf16[32,2048]{1,0:T(8,128)(2,1)S(1)} %shard_map.83.refs_7_), channel_id=1, source_target_pairs={{0,192},{192,0},{1,193},{193,1},{2,194},{194,2},{3,195},{195,3},{4... | collective-permute-start | bytes 393224 | tf_op jit(solution)/shard_map/ppermute | solution.py:305
  374.7 34.5 %all_to_all.53.rows_ref = bf16[64,1,4,2048]{3,2,1,0:T(4,128)(2,1)S(1)} all-to-all(bf16[64,1,4,2048]{3,2,1,0:T(4,128)(2,1)S(1)} %get-tuple-element.25), channel_id=1, replica_groups=mesh['section'=4,'expert'=64] {'expert'}, dimensions={0} | all-to-all | bytes 2097152 | tf_op jit(solution)/shard_map/all_to_all | solution.py:308
  409.2 5.5 %shard_map.86 = bf16[64,1,4,2048]{3,2,1,0:T(4,128)(2,1)S(1)} custom-call(s32[1]{0:T(128)} %bitcast.section_ref, bf16[64,1,4,2048]{3,2,1,0:T(4,128)(2,1)S(1)} %all_to_all.53.rows_ref, bf16[18432,256]{1,0:T(8,128)(2,1)S(1)} %bitcast.8, bf16[18432,256]{1,0:T(8,128)(2,1)} %collective-permute-done.12.refs_8_.refs_1_, ...), custom_call_target="tpu_custom_call" | custom-call | flops 2415919104 | bytes 11534336 | tf_op jit(solution)/shard_map/pallas_call | solution.py:264
  414.7 34.8 %all_to_all.54.back_ref = bf16[64,1,4,2048]{3,2,1,0:T(4,128)(2,1)S(1)} all-to-all(bf16[64,1,4,2048]{3,2,1,0:T(4,128)(2,1)S(1)} %shard_map.86), channel_id=1, replica_groups=mesh['section'=4,'expert'=64] {'expert'}, dimensions={0} | all-to-all | bytes 2097152 | tf_op jit(solution)/shard_map/all_to_all | solution.py:308
  452.1 5.0 collective-permute-done.16.refs_6_
  457.8 34.8 %all_to_all.55.rows_ref = bf16[64,1,4,2048]{3,2,1,0:T(4,128)(2,1)S(1)} all-to-all(bf16[64,1,4,2048]{3,2,1,0:T(4,128)(2,1)S(1)} %get-tuple-element.27), channel_id=1, replica_groups=mesh['section'=4,'expert'=64] {'expert'}, dimensions={0} | all-to-all | bytes 2097152 | tf_op jit(solution)/shard_map/all_to_all | solution.py:308
  492.7 5.5 %shard_map.89 = bf16[64,1,4,2048]{3,2,1,0:T(4,128)(2,1)S(1)} custom-call(s32[1]{0:T(128)} %bitcast.section_ref, bf16[64,1,4,2048]{3,2,1,0:T(4,128)(2,1)S(1)} %all_to_all.55.rows_ref, bf16[18432,256]{1,0:T(8,128)(2,1)S(1)} %bitcast.8, bf16[18432,256]{1,0:T(8,128)(2,1)} %collective-permute-done.12.refs_8_.refs_1_, ...), custom_call_target="tpu_custom_call" | custom-call | flops 2415919104 | bytes 11534336 | tf_op jit(solution)/shard_map/pallas_call | solution.py:264
  498.2 34.6 %all_to_all.56.back_ref = bf16[64,1,4,2048]{3,2,1,0:T(4,128)(2,1)S(1)} all-to-all(bf16[64,1,4,2048]{3,2,1,0:T(4,128)(2,1)S(1)} %shard_map.89), channel_id=1, replica_groups=mesh['section'=4,'expert'=64] {'expert'}, dimensions={0} | all-to-all | bytes 2097152 | tf_op jit(solution)/shard_map/all_to_all | solution.py:308
  (100 shorter events, 83.6 us)
Async XLA Ops:
  0.0 8.2 %collective-permute-start.5 = (bf16[32,2048]{1,0:T(8,128)(2,1)}, bf16[32,2048]{1,0:T(8,128)(2,1)S(1)}, u32[]{:S(2)}, u32[]{:S(2)}) collective-permute-start(bf16[32,2048]{1,0:T(8,128)(2,1)} %bitcast.34), channel_id=1, source_target_pairs={{128,0},{129,1},{130,2},{131,3},{132,4},{133,5},{134,6},{135,7},{1... | collective-permute-start | bytes 393224 | tf_op jit(solution)/shard_map/ppermute | solution.py:305
  1.3 6.9 %collective-permute-start = (f32[1,2048]{1,0:T(1,128)}, f32[1,2048]{1,0:T(1,128)S(1)}, u32[]{:S(2)}, u32[]{:S(2)}) collective-permute-start(f32[1,2048]{1,0:T(1,128)} %refs_0_.9), channel_id=1, source_target_pairs={{64,0},{128,64},{192,128},{0,192},{65,1},{129,65},{193,129},{1,193... | collective-permute-start | bytes 24584 | tf_op jit(solution)/shard_map/ppermute | solution.py:305
  4.9 3.3 collective-permute-start.2
  11.5 42.4 %all-to-all-start = ((bf16[64,1,4,2048]{3,2,1,0:T(4,128)(2,1)}), bf16[64,1,4,2048]{3,2,1,0:T(4,128)(2,1)S(1)}, u32[]{:S(2)}, u32[]{:S(2)}) async-start(bf16[64,1,4,2048]{3,2,1,0:T(4,128)(2,1)} %get-tuple-element.17), calls=%async_computation | async-start | bytes 2097152 | tf_op jit(solution)/shard_map/all_to_all | solution.py:308
  25.3 11.7 %collective-permute-start.4 = (bf16[32,2048]{1,0:T(8,128)(2,1)}, bf16[32,2048]{1,0:T(8,128)(2,1)S(1)}, u32[]{:S(2)}, u32[]{:S(2)}) collective-permute-start(bf16[32,2048]{1,0:T(8,128)(2,1)} %bitcast.35), channel_id=1, source_target_pairs={{64,0},{65,1},{66,2},{67,3},{68,4},{69,5},{70,6},{71,7},{72,8},{73... | collective-permute-start | bytes 393224 | tf_op jit(solution)/shard_map/ppermute | solution.py:305
  26.6 10.4 %collective-permute-start.1 = (f32[1,2048]{1,0:T(1,128)}, f32[1,2048]{1,0:T(1,128)S(1)}, u32[]{:S(2)}, u32[]{:S(2)}) collective-permute-start(f32[1,2048]{1,0:T(1,128)} %refs_0_.9), channel_id=1, source_target_pairs={{64,128},{128,192},{192,0},{0,64},{65,129},{129,193},{193,1},{1,65... | collective-permute-start | bytes 24584 | tf_op jit(solution)/shard_map/ppermute | solution.py:305
  29.6 4.7 collective-permute-start.7
  29.7 4.6 collective-permute-start.6
  32.4 4.6 collective-permute-start.3
  63.3 34.8 %all-to-all-start.1 = ((bf16[64,1,4,2048]{3,2,1,0:T(4,128)(2,1)}), bf16[64,1,4,2048]{3,2,1,0:T(4,128)(2,1)S(1)}, u32[]{:S(2)}, u32[]{:S(2)}) async-start(bf16[64,1,4,2048]{3,2,1,0:T(4,128)(2,1)} %shard_map.75), calls=%async_computation.1 | async-start | bytes 2097152 | tf_op jit(solution)/shard_map/all_to_all | solution.py:308
  69.5 27.4 %collective-permute-start.8 = (bf16[64,1,4,2048]{3,2,1,0:T(4,128)(2,1)S(1)}, bf16[64,1,4,2048]{3,2,1,0:T(4,128)(2,1)S(1)}, u32[]{:S(2)}, u32[]{:S(2)}) collective-permute-start(bf16[64,1,4,2048]{3,2,1,0:T(4,128)(2,1)S(1)} %all-to-all-done.rows_ref), channel_id=1, source_target_pairs={{192,0},{193,1},{194,2},{195,3},{196,4},{197,5},{198,6},{199,7},{2... | collective-permute-start | bytes 3145736 | tf_op jit(solution)/shard_map/ppermute | solution.py:305
  70.8 173.4 %collective-permute-start.13 = (bf16[18432,256]{1,0:T(8,128)(2,1)}, bf16[18432,256]{1,0:T(8,128)(2,1)}, u32[]{:S(2)}, u32[]{:S(2)}) collective-permute-start(bf16[18432,256]{1,0:T(8,128)(2,1)} %copy-done), channel_id=1, source_target_pairs={{64,128},{128,192},{65,129},{129,193},{66,130},{130,194},{67,131},... | collective-permute-start | bytes 28311560 | tf_op jit(solution)/shard_map/ppermute | solution.py:305
  75.1 206.7 %collective-permute-start.12 = (bf16[18432,256]{1,0:T(8,128)(2,1)}, bf16[18432,256]{1,0:T(8,128)(2,1)}, u32[]{:S(2)}, u32[]{:S(2)}) collective-permute-start(bf16[18432,256]{1,0:T(8,128)(2,1)} %copy-done), channel_id=1, source_target_pairs={{64,0},{128,64},{192,128},{65,1},{129,65},{193,129},{66,2},{130,66... | collective-permute-start | bytes 28311560 | tf_op jit(solution)/shard_map/ppermute | solution.py:305
  99.6 4.2 collective-permute-start.9
  108.9 60.9 %all-to-all-start.2 = ((bf16[64,2,4,2048]{3,2,1,0:T(4,128)(2,1)}), bf16[64,2,4,2048]{3,2,1,0:T(4,128)(2,1)S(1)}, u32[]{:S(2)}, u32[]{:S(2)}) async-start(bf16[64,2,4,2048]{3,2,1,0:T(4,128)(2,1)} %copy-done.10), calls=%async_computation.2 | async-start | bytes 4194304 | tf_op jit(solution)/shard_map/all_to_all | solution.py:308
  126.9 23.7 %collective-permute-start.10 = (bf16[64,1,4,2048]{3,2,1,0:T(4,128)(2,1)S(1)}, bf16[64,1,4,2048]{3,2,1,0:T(4,128)(2,1)S(1)}, u32[]{:S(2)}, u32[]{:S(2)}) collective-permute-start(bf16[64,1,4,2048]{3,2,1,0:T(4,128)(2,1)S(1)} %shard_map.78), channel_id=1, source_target_pairs={{0,192},{1,193},{2,194},{3,195},{4,196},{5,197},{6,198},{7,199},{8... | collective-permute-start | bytes 3145736 | tf_op jit(solution)/shard_map/ppermute | solution.py:305
  132.1 238.1 %collective-permute-start.15 = (bf16[18432,256]{1,0:T(8,128)(2,1)}, bf16[18432,256]{1,0:T(8,128)(2,1)}, u32[]{:S(2)}, u32[]{:S(2)}) collective-permute-start(bf16[18432,256]{1,0:T(8,128)(2,1)} %shard_map.84), channel_id=1, source_target_pairs={{192,0},{193,1},{194,2},{195,3},{196,4},{197,5},{198,6},{199,7},{2... | collective-permute-start | bytes 28311560 | tf_op jit(solution)/shard_map/ppermute | solution.py:305
  181.9 57.0 %copy-start.18 = (bf16[2,32,2048]{2,1,0:T(8,128)(2,1)S(1)}, bf16[2,32,2048]{2,1,0:T(8,128)(2,1)}, u32[]{:S(2)}) copy-start(bf16[2,32,2048]{2,1,0:T(8,128)(2,1)} %copy-done.17) | copy-start | bytes 786436
  181.9 99.9 %copy-start.22 = (f32[1,2048]{1,0:T(1,128)S(1)}, f32[1,2048]{1,0:T(1,128)}, u32[]{:S(2)}) copy-start(f32[1,2048]{1,0:T(1,128)} %copy-done.21) | copy-start | bytes 24580
  240.1 41.7 %collective-permute-start.11 = (bf16[32,2048]{1,0:T(8,128)(2,1)S(1)}, bf16[32,2048]{1,0:T(8,128)(2,1)S(1)}, u32[]{:S(2)}, u32[]{:S(2)}) collective-permute-start(bf16[32,2048]{1,0:T(8,128)(2,1)S(1)} %get-tuple-element.21), channel_id=1, source_target_pairs={{0,64},{64,192},{192,128},{1,65},{65,193},{193,129},{2,66},{66,194... | collective-permute-start | bytes 393224 | tf_op jit(solution)/shard_map/ppermute | solution.py:305
  281.8 41.4 %slice-start = ((s8[9437184]{0:T(1024)(128)(4,1)}), s8[4194304]{0:T(1024)(128)(4,1)S(1)}, s32[]{:S(2)}) async-start(s8[9437184]{0:T(1024)(128)(4,1)} %bitcast.7), calls=%async_computation.10 | async-start | bytes 8388608
  281.8 41.4 %slice-start.1 = ((s8[9437184]{0:T(1024)(128)(4,1)}), s8[4194304]{0:T(1024)(128)(4,1)S(1)}, s32[]{:S(2)}) async-start(s8[9437184]{0:T(1024)(128)(4,1)} %bitcast.7), calls=%async_computation.11 | async-start | bytes 8388608
  363.9 10.0 %collective-permute-start.14 = (bf16[32,2048]{1,0:T(8,128)(2,1)S(1)}, bf16[32,2048]{1,0:T(8,128)(2,1)S(1)}, u32[]{:S(2)}, u32[]{:S(2)}) collective-permute-start(bf16[32,2048]{1,0:T(8,128)(2,1)S(1)} %shard_map.83.refs_7_), channel_id=1, source_target_pairs={{0,192},{192,0},{1,193},{193,1},{2,194},{194,2},{3,195},{195,3},{4... | collective-permute-start | bytes 393224 | tf_op jit(solution)/shard_map/ppermute | solution.py:305
  450.2 7.0 %collective-permute-start.16 = (bf16[32,2048]{1,0:T(8,128)(2,1)S(1)}, bf16[32,2048]{1,0:T(8,128)(2,1)S(1)}, u32[]{:S(2)}, u32[]{:S(2)}) collective-permute-start(bf16[32,2048]{1,0:T(8,128)(2,1)S(1)} %shard_map.87.refs_7_), channel_id=1, source_target_pairs={{64,0},{0,64},{65,1},{1,65},{66,2},{2,66},{67,3},{3,67},{68,4},{4,... | collective-permute-start | bytes 393224 | tf_op jit(solution)/shard_map/ppermute | solution.py:305
  (24 other events, 174.9 us)

commit v4 on v3

--- a/solution.py
+++ b/solution.py
@@ -8,6 +8,7 @@
 from jax.sharding import PartitionSpec as P
 
 EPSILON = 1e-06
+LONG, LONGER = 20_000_000_000, 60_000_000_000
 SLOTS = 2
 GROUP = 2 * SLOTS
 
@@ -101,19 +102,23 @@
     panels = units // width
     order = [number for panel in range(panels) for number in (panel, panels + panel)]
     spans = [(number * features, features) for number in order]
-    each = units * (2 if features // width % 2 == 0 else 1)
     first = 2 * panels * features
-    return spans + [(start, each) for start in range(first, first + units * features // width, each)]
-
-
-def pack_kernel(width, *refs):
-    gate_ref, up_ref, down_ref = refs[:3]
-    out_ref, done = refs[-2:]
-    features, units = gate_ref.shape
+    return spans + [(first + panel * units, units) for panel in range(features // width)]
+
+
+def spread(refs, start, size):
+    for ref in refs:
+        if start < ref.shape[0]:
+            return ref.at[pl.ds(start, size), :]
+        start -= ref.shape[0]
+
+
+def pack_kernel(width, outputs, *refs):
+    out_refs, done = refs[-1 - outputs : -1], refs[-1]
     copies, start = [], 0
-    for ref in (gate_ref, up_ref, down_ref):
+    for ref in refs[:3]:
         for column in range(0, ref.shape[1], width):
-            to = out_ref.at[pl.ds(start, ref.shape[0]), :]
+            to = spread(out_refs, start, ref.shape[0])
             copies.append(pltpu.make_async_copy(ref.at[:, pl.ds(column, width)], to, done.at[len(copies)]))
             start += ref.shape[0]
     for copy in copies:
@@ -123,7 +128,7 @@
 
 
 def ffn_kernel(step, given, held, section_ref, rows_ref, *refs):
-    layers, refs = refs[:held], refs[held:]
+    layers, refs = [refs[2 * number : 2 * number + 2] for number in range(held)], refs[2 * held :]
     out_ref, weights, activated, flat, arrived = refs[-5:]
     experts, lanes, _, features = rows_ref.shape
     units = activated.shape[-1]
@@ -132,10 +137,10 @@
     section = section_ref[0]
     spans = pieces(features, units, width)
 
-    def copies(ref):
+    def copies(parts):
         for number, (start, size) in enumerate(spans):
-            rows = pl.ds(start, size)
-            yield pltpu.make_async_copy(ref.at[rows, :], weights.at[rows, :], arrived.at[number])
+            to = weights.at[pl.ds(start, size), :]
+            yield pltpu.make_async_copy(spread(parts, start, size), to, arrived.at[number])
 
     if held == 1:
         for copy in copies(layers[0]):
@@ -143,16 +148,16 @@
     else:
         layer = looked_up(LAYERS[step], section)
         layer = jnp.where(jnp.logical_and(layer == LOWER, section == 0), LOWER + 1, layer)
-        for number, ref in enumerate(layers):
+        for number, held_parts in enumerate(layers):
 
             @pl.when(layer == number)
-            def _(ref=ref):
-                for copy in copies(ref):
+            def _(held_parts=held_parts):
+                for copy in copies(held_parts):
                     copy.start()
 
     def arrival(number, start, size):
-        rows = pl.ds(pl.multiple_of(start, width), size)
-        pltpu.make_async_copy(layers[0].at[rows, :], weights.at[rows, :], arrived.at[number]).wait()
+        to = weights.at[pl.ds(pl.multiple_of(start, width), size), :]
+        pltpu.make_async_copy(to, to, arrived.at[number]).wait()
 
     for lane in range(lanes):
         flat[lane] = rows_ref[:, lane].reshape(flat.shape[1:])
@@ -171,24 +176,20 @@
         return 0
 
     lax.fori_loop(0, panels, widen, 0)
-    size = spans[-1][1]
-
-    def narrow(number, _):
-        first = 2 * panels * features + number * size
-        arrival(2 * panels + number, first, size)
-        for inner in range(size // units):
-            down = weights[pl.ds(pl.multiple_of(first + inner * units, width), units)]
-            column = (number * (size // units) + inner) * width
-            part = pl.ds(pl.multiple_of(column, width), width)
-            for lane in range(lanes):
-                made = jnp.dot(activated[lane], down, preferred_element_type=jnp.float32)
-                made = made.astype(jnp.bfloat16).reshape(experts, GROUP, width)
-                if given is not None and lane == lanes - 1:
-                    made = jnp.where(section == given, refs[0][:, 0, :, part], made)
-                out_ref[:, lane, :, part] = made
+    def narrow(panel, _):
+        first = 2 * panels * features + panel * units
+        arrival(2 * panels + panel, first, units)
+        down = weights[pl.ds(pl.multiple_of(first, width), units)]
+        part = pl.ds(pl.multiple_of(panel * width, width), width)
+        for lane in range(lanes):
+            made = jnp.dot(activated[lane], down, preferred_element_type=jnp.float32)
+            made = made.astype(jnp.bfloat16).reshape(experts, GROUP, width)
+            if given is not None and lane == lanes - 1:
+                made = jnp.where(section == given, refs[0][:, 0, :, part], made)
+            out_ref[:, lane, :, part] = made
         return 0
 
-    lax.fori_loop(0, len(spans) - 2 * panels, narrow, 0)
+    lax.fori_loop(0, features // width, narrow, 0)
 
 
 def combine_kernel(step, kinds, experts, last, section_ref, back_ref, hidden_ref, *refs):
@@ -243,26 +244,47 @@
     )(section, *operands, *ties)
 
 
+def token_kernel(*refs):
+    refs[-1][...] = jnp.zeros_like(refs[-1])
+
+
+def arrived_token(flops, *values):
+    return pl.pallas_call(
+        token_kernel,
+        out_shape=jax.ShapeDtypeStruct((8, 128), jnp.float32),
+        in_specs=[WHEREVER] * len(values),
+        out_specs=VMEM,
+        cost_estimate=pl.CostEstimate(flops=flops, bytes_accessed=4096, transcendentals=0),
+        compiler_params=limit(4),
+    )(*values)
+
+
 def packed(gate, up, down, ties):
     features, units = gate.shape
     width = 256 if units % 256 == 0 and features % 256 == 0 else units
-    return pl.pallas_call(
-        functools.partial(pack_kernel, width),
-        out_shape=jax.ShapeDtypeStruct((3 * features * units // width, width), gate.dtype),
+    panels = features // width
+    ahead = panels - panels * 3 // 8
+    rows = (2 * features * units // width + ahead * units, (panels - ahead) * units)
+    return pl.pallas_call(
+        functools.partial(pack_kernel, width, 2),
+        out_shape=tuple(jax.ShapeDtypeStruct((count, width), gate.dtype) for count in rows),
         in_specs=[WHEREVER] * (3 + len(ties)),
-        out_specs=WHEREVER,
-        scratch_shapes=[pltpu.SemaphoreType.DMA((2 * units // width + features // width,))],
+        out_specs=(WHEREVER, WHEREVER),
+        scratch_shapes=[pltpu.SemaphoreType.DMA((2 * units // width + panels,))],
         compiler_params=limit(4),
     )(gate, up, down, *ties)
 
 
 def ffn(step, section, rows, layers, given=None, made=(), ties=()):
     experts, lanes, group, features = rows.shape
-    length, width = layers[0].shape
+    width = layers[0][0].shape[1]
+    length = sum(part.shape[0] for part in layers[0])
+    held = len(layers)
+    layers = [part for parts in layers for part in parts]
     units = length * width // (3 * features)
     height = experts * group
     return pl.pallas_call(
-        functools.partial(ffn_kernel, step, given, len(layers)),
+        functools.partial(ffn_kernel, step, given, held),
         out_shape=jax.ShapeDtypeStruct(rows.shape, jnp.bfloat16),
         in_specs=[SMEM, VMEM] + [WHEREVER] * len(layers) + [VMEM] * len(made) + [WHEREVER] * len(ties),
         out_specs=VMEM,
@@ -320,29 +342,31 @@
     second_in = move(own, (1, 0))
     hidden, sent = dispatch(0, experts, at, gains[:2], ids[:2], [(own, first_in)])
     layer = packed(*weights, (hidden, second_in, *small_upper, *small_lower))
-    upper = move(layer, *downward[:3])
-    lower_early = move(layer, *upward[:2])
+    upper = [move(part, *downward[:3]) for part in layer]
+    lower_early = [move(part, *upward[:2]) for part in layer]
+    lower_late = [move(part, upward[2]) for part in layer]
     rows = exchange(sent)
     away = move(rows, (3, 0))
     made = exchange(ffn(0, at, rows, [layer]))
     (state,) = combine(0, experts, at, made, hidden, ids[:1], raw[:1], (away,))
     state = move(state, (0, 1))
 
-    lower_late = move(packed(*weights, (away,)), upward[2])
     away = move(ffn(0, at, away, [layer]), (0, 3))
     hidden, sent = dispatch(1, experts, at, gains[:1], ids[:1], [(own,), (own, second_in, state)])
     made = ffn(1, at, exchange(sent), [layer], 3, (away,))
-    kept, state = combine(1, experts, at, exchange(made), hidden, ids[:2], raw[:2])
+    here = arrived_token(LONGER, upper[0], lower_early[0])
+    kept, state = combine(1, experts, at, exchange(made), hidden, ids[:2], raw[:2], (here,))
     state = move(state, (0, 1), (1, 3), (3, 2))
 
     layers = [layer, upper, lower_early]
-    hidden, sent = dispatch(2, experts, at, gains, ids, [(state, kept)], layers[1:])
+    hidden, sent = dispatch(2, experts, at, gains, ids, [(state, kept)])
     made = exchange(ffn(2, at, exchange(sent), layers))
-    (kept,) = combine(2, experts, at, made, hidden, ids, raw)
+    here = arrived_token(LONG, *lower_late)
+    (kept,) = combine(2, experts, at, made, hidden, ids, raw, (here,))
     state = move(kept, (0, 3), (3, 0))
 
     layers.append(lower_late)
-    hidden, sent = dispatch(3, experts, at, gains, ids, [(state, kept)], layers[3:])
+    hidden, sent = dispatch(3, experts, at, gains, ids, [(state, kept)])
     made = exchange(ffn(3, at, exchange(sent), layers))
     (kept,) = combine(3, experts, at, made, hidden, ids, raw)
     state = move(kept, (1, 0), (0, 1))

time: 535 us -> 525 us (0.981)
  blocking collectives: 271 us -> 141 us
  waiting for transfers between devices: 119 us -> 199 us
  starting transfers between devices: 64.4 us -> 94.5 us
  Pallas kernels: 48.4 us -> 59.2 us
    all_to_all x7 -> x4, blocking collectives: 271 us -> 141 us  [exchange(): lax.all_to_all(value, 'expert', split_axis=0, concat_axis=0, tiled=True)]
    ppermute x17 -> x20, waiting for transfers between devices: 93.5 us -> 155 us  [move(): return lax.ppermute(value, 'section', route)]
    all_to_all x3 -> x6, starting transfers between devices: 29.7 us -> 53.5 us  [exchange(): lax.all_to_all(value, 'expert', split_axis=0, concat_axis=0, tiled=True)]
    all_to_all x3 -> x6, waiting for transfers between devices: 25.9 us -> 43.4 us  [exchange(): lax.all_to_all(value, 'expert', split_axis=0, concat_axis=0, tiled=True)]
    pallas_call x8 -> x9, Pallas kernels: 38.7 us -> 46.1 us  [the longest x6 42.7 us: ffn(): pl.pallas_call(functools.partial(ffn_kernel, step, given, held), out_shap...]
    ppermute x17 -> x20, starting transfers between devices: 34.7 us -> 41 us  [move(): return lax.ppermute(value, 'section', route)]
    unnamed x58 -> x102, local copies, waits for them, and re-layouts: 30.6 us -> 29.6 us
  transfers between devices with their start and end apart: 20 -> 26, of which waited for: 12 -> 17; matrix products, arithmetic and copies ran while one was open for 0% -> 0% of each run, Pallas kernels for 5% -> 8%
where the time goes in v4:
time: 525 us; the launch traced here: 523 us
  waiting for transfers between devices  199 us (38%)
  blocking collectives  141 us (27%)
  starting transfers between devices  94.5 us (18%)
  Pallas kernels  59.2 us (11%)
  local copies, waits for them, and re-layouts  29.6 us (6%)
    ppermute x20, waiting for transfers between devices, move(): return lax.ppermute(value, 'section', route)  155 us
    all_to_all x4, blocking collectives, exchange(): lax.all_to_all(value, 'expert', split_axis=0, concat_axis=0, tiled=True)  141 us
    all_to_all x6, starting transfers between devices, exchange(): lax.all_to_all(value, 'expert', split_axis=0, concat_axis=0, tiled=True)  53.5 us
    all_to_all x6, waiting for transfers between devices, exchange(): lax.all_to_all(value, 'expert', split_axis=0, concat_axis=0, tiled=True)  43.4 us
    pallas_call x6, Pallas kernels, ffn(): pl.pallas_call(functools.partial(ffn_kernel, step, given, held), out_shap...  42.7 us
    ppermute x20, starting transfers between devices, move(): return lax.ppermute(value, 'section', route)  41 us
    unnamed x102, local copies, waits for them, and re-layouts  29.6 us
  transfers between devices with their start and end apart: 26, of which 17 were waited for; matrix products, arithmetic and copies ran while one was open for 0% of the time, Pallas kernels for 8%

profile of v4, /device:TPU:1, one launch (start us, length us, event | category | flops | bytes accessed | tf_op | source)
XLA Modules:
  0.0 523.2 jit_solution(1001151587695787897)
XLA Ops:
  11.6 13.9 %all-to-all-start = ((bf16[64,1,4,2048]{3,2,1,0:T(4,128)(2,1)}), bf16[64,1,4,2048]{3,2,1,0:T(4,128)(2,1)S(1)}, u32[]{:S(2)}, u32[]{:S(2)}) async-start(bf16[64,1,4,2048]{3,2,1,0:T(4,128)(2,1)} %get-tuple-element.19), calls=%async_computation | async-start | bytes 2097152 | tf_op jit(solution)/shard_map/all_to_all | solution.py:330
  54.1 7.0 %shard_map.75 = bf16[64,1,4,2048]{3,2,1,0:T(4,128)(2,1)} custom-call(s32[1]{0:T(128)} %bitcast.section_ref, bf16[64,1,4,2048]{3,2,1,0:T(4,128)(2,1)S(1)} %all-to-all-done.rows_ref, bf16[16128,256]{1,0:T(8,128)(2,1)} %get-tuple-element.21.refs_0_, bf16[2304,256]{1,0:T(8,128)(2,1)S(1)} %get-tuple-element.22.refs_1_), custom_call_target="tpu_custom_call" | custom-call | flops 2415919104 | bytes 11534336 | tf_op jit(solution)/shard_map/pallas_call | solution.py:286
  61.1 9.4 %all-to-all-start.1 = ((bf16[64,1,4,2048]{3,2,1,0:T(4,128)(2,1)}), bf16[64,1,4,2048]{3,2,1,0:T(4,128)(2,1)}, u32[]{:S(2)}, u32[]{:S(2)}) async-start(bf16[64,1,4,2048]{3,2,1,0:T(4,128)(2,1)} %shard_map.75), calls=%async_computation.1 | async-start | bytes 2097152 | tf_op jit(solution)/shard_map/all_to_all | solution.py:330
  71.8 26.1 %collective-permute-done.8.refs_2_.rows_ref = bf16[64,1,4,2048]{3,2,1,0:T(4,128)(2,1)S(1)} collective-permute-done((bf16[64,1,4,2048]{3,2,1,0:T(4,128)(2,1)S(1)}, bf16[64,1,4,2048]{3,2,1,0:T(4,128)(2,1)S(1)}, u32[]{:S(2)}, u32[]{:S(2)}) %collective-permute-start.8) | collective-permute-done | bytes 1048608 | tf_op jit(solution)/shard_map/ppermute | solution.py:327
  114.6 6.7 %all-to-all-start.2 = ((bf16[64,2,4,2048]{3,2,1,0:T(4,128)(2,1)}), bf16[64,2,4,2048]{3,2,1,0:T(4,128)(2,1)}, u32[]{:S(2)}, u32[]{:S(2)}) async-start(bf16[64,2,4,2048]{3,2,1,0:T(4,128)(2,1)} %copy-done.19), calls=%async_computation.2 | async-start | bytes 4194304 | tf_op jit(solution)/shard_map/all_to_all | solution.py:330
  121.3 6.1 %shard_map.78 = bf16[64,1,4,2048]{3,2,1,0:T(4,128)(2,1)S(1)} custom-call(s32[1]{0:T(128)} %bitcast.section_ref, bf16[64,1,4,2048]{3,2,1,0:T(4,128)(2,1)S(1)} %collective-permute-done.8.refs_2_.rows_ref, bf16[16128,256]{1,0:T(8,128)(2,1)} %get-tuple-element.21.refs_0_, bf16[2304,256]{1,0:T(8,128)(2,1)S(1)} %get-tuple-element.22.refs_1_), custom_call_target="tpu_custom_call" | custom-call | flops 2415919104 | bytes 11534336 | tf_op jit(solution)/shard_map/pallas_call | solution.py:286
  130.0 20.7 %collective-permute-done.10.refs_2_ = bf16[64,1,4,2048]{3,2,1,0:T(4,128)(2,1)S(1)} collective-permute-done((bf16[64,1,4,2048]{3,2,1,0:T(4,128)(2,1)S(1)}, bf16[64,1,4,2048]{3,2,1,0:T(4,128)(2,1)S(1)}, u32[]{:S(2)}, u32[]{:S(2)}) %collective-permute-start.10) | collective-permute-done | bytes 1048608 | tf_op jit(solution)/shard_map/ppermute | solution.py:327
  150.8 21.7 %all-to-all-done.2.rows_ref = bf16[64,2,4,2048]{3,2,1,0:T(4,128)(2,1)} async-done(((bf16[64,2,4,2048]{3,2,1,0:T(4,128)(2,1)}), bf16[64,2,4,2048]{3,2,1,0:T(4,128)(2,1)}, u32[]{:S(2)}, u32[]{:S(2)}) %all-to-all-start.2) | async-done | bytes 2097184 | tf_op jit(solution)/shard_map/all_to_all | solution.py:330
  172.4 10.2 %shard_map.79 = bf16[64,2,4,2048]{3,2,1,0:T(4,128)(2,1)S(1)} custom-call(s32[1]{0:T(128)} %bitcast.section_ref, bf16[64,2,4,2048]{3,2,1,0:T(4,128)(2,1)} %all-to-all-done.2.rows_ref, bf16[16128,256]{1,0:T(8,128)(2,1)} %get-tuple-element.21.refs_0_, bf16[2304,256]{1,0:T(8,128)(2,1)S(1)} %get-tuple-element.22.refs_1_, ...), custom_call_target="tpu_custom_call" | custom-call | flops 4831838208 | bytes 13631488 | tf_op jit(solution)/shard_map/pallas_call | solution.py:286
  184.0 5.8 %all-to-all-start.3 = ((bf16[64,2,4,2048]{3,2,1,0:T(4,128)(2,1)}), bf16[64,2,4,2048]{3,2,1,0:T(4,128)(2,1)S(1)}, u32[]{:S(2)}, u32[]{:S(2)}) async-start(bf16[64,2,4,2048]{3,2,1,0:T(4,128)(2,1)} %copy-done.20), calls=%async_computation.3 | async-start | bytes 4194304 | tf_op jit(solution)/shard_map/all_to_all | solution.py:330
  189.8 34.9 %collective-permute-done.11.refs_0_.refs_2_ = bf16[16128,256]{1,0:T(8,128)(2,1)} collective-permute-done((bf16[16128,256]{1,0:T(8,128)(2,1)}, bf16[16128,256]{1,0:T(8,128)(2,1)}, u32[]{:S(2)}, u32[]{:S(2)}) %collective-permute-start.11) | collective-permute-done | bytes 8257568 | tf_op jit(solution)/shard_map/ppermute | solution.py:327
  225.2 15.8 %all-to-all-done.3.back_ref = bf16[64,2,4,2048]{3,2,1,0:T(4,128)(2,1)S(1)} async-done(((bf16[64,2,4,2048]{3,2,1,0:T(4,128)(2,1)}), bf16[64,2,4,2048]{3,2,1,0:T(4,128)(2,1)S(1)}, u32[]{:S(2)}, u32[]{:S(2)}) %all-to-all-start.3) | async-done | bytes 2097184 | tf_op jit(solution)/shard_map/all_to_all | solution.py:330
  253.6 6.6 %all-to-all-start.4 = ((bf16[64,1,4,2048]{3,2,1,0:T(4,128)(2,1)}), bf16[64,1,4,2048]{3,2,1,0:T(4,128)(2,1)}, u32[]{:S(2)}, u32[]{:S(2)}) async-start(bf16[64,1,4,2048]{3,2,1,0:T(4,128)(2,1)} %get-tuple-element.27), calls=%async_computation.4 | async-start | bytes 2097152 | tf_op jit(solution)/shard_map/all_to_all | solution.py:330
  263.6 26.7 %collective-permute-done.14.refs_3_ = bf16[2304,256]{1,0:T(8,128)(2,1)S(1)} collective-permute-done((bf16[2304,256]{1,0:T(8,128)(2,1)S(1)}, bf16[2304,256]{1,0:T(8,128)(2,1)S(1)}, u32[]{:S(2)}, u32[]{:S(2)}) %collective-permute-start.14) | collective-permute-done | bytes 1179680 | tf_op jit(solution)/shard_map/ppermute | solution.py:327
  290.4 7.3 %shard_map.83 = bf16[64,1,4,2048]{3,2,1,0:T(4,128)(2,1)S(1)} custom-call(s32[1]{0:T(128)} %bitcast.section_ref, bf16[64,1,4,2048]{3,2,1,0:T(4,128)(2,1)} %all-to-all-done.4.rows_ref, bf16[16128,256]{1,0:T(8,128)(2,1)} %get-tuple-element.21.refs_0_, bf16[2304,256]{1,0:T(8,128)(2,1)S(1)} %get-tuple-element.22.refs_1_, ...), custom_call_target="tpu_custom_call" | custom-call | flops 2415919104 | bytes 11534336 | tf_op jit(solution)/shard_map/pallas_call | solution.py:286
  298.7 11.1 %all-to-all-start.5 = ((bf16[64,1,4,2048]{3,2,1,0:T(4,128)(2,1)}), bf16[64,1,4,2048]{3,2,1,0:T(4,128)(2,1)}, u32[]{:S(2)}, u32[]{:S(2)}) async-start(bf16[64,1,4,2048]{3,2,1,0:T(4,128)(2,1)} %copy-done.8), calls=%async_computation.5 | async-start | bytes 2097152 | tf_op jit(solution)/shard_map/all_to_all | solution.py:330
  309.8 26.1 %collective-permute-done.17.refs_1_.refs_7_ = bf16[2304,256]{1,0:T(8,128)(2,1)} collective-permute-done((bf16[2304,256]{1,0:T(8,128)(2,1)S(1)}, bf16[2304,256]{1,0:T(8,128)(2,1)}, u32[]{:S(2)}, u32[]{:S(2)}) %collective-permute-start.17) | collective-permute-done | bytes 1179680 | tf_op jit(solution)/shard_map/ppermute | solution.py:327
  346.8 5.9 %collective-permute-start.18 = (bf16[32,2048]{1,0:T(8,128)(2,1)S(1)}, bf16[32,2048]{1,0:T(8,128)(2,1)S(1)}, u32[]{:S(2)}, u32[]{:S(2)}) collective-permute-start(bf16[32,2048]{1,0:T(8,128)(2,1)S(1)} %shard_map.85.refs_7_), channel_id=1, source_target_pairs={{0,192},{192,0},{1,193},{193,1},{2,194},{194,2},{3,195},{195,3},{4... | collective-permute-start | bytes 393224 | tf_op jit(solution)/shard_map/ppermute | solution.py:327
  360.4 36.5 %all_to_all.50.rows_ref = bf16[64,1,4,2048]{3,2,1,0:T(4,128)(2,1)S(1)} all-to-all(bf16[64,1,4,2048]{3,2,1,0:T(4,128)(2,1)S(1)} %get-tuple-element.29), channel_id=1, replica_groups=mesh['section'=4,'expert'=64] {'expert'}, dimensions={0} | all-to-all | bytes 2097152 | tf_op jit(solution)/shard_map/all_to_all | solution.py:330
  397.0 6.1 %shard_map.87 = bf16[64,1,4,2048]{3,2,1,0:T(4,128)(2,1)S(1)} custom-call(s32[1]{0:T(128)} %bitcast.section_ref, bf16[64,1,4,2048]{3,2,1,0:T(4,128)(2,1)S(1)} %all_to_all.50.rows_ref, bf16[16128,256]{1,0:T(8,128)(2,1)} %get-tuple-element.21.refs_0_, bf16[2304,256]{1,0:T(8,128)(2,1)S(1)} %get-tuple-element.22.refs_1_, ...), custom_call_target="tpu_custom_call" | custom-call | flops 2415919104 | bytes 11534336 | tf_op jit(solution)/shard_map/pallas_call | solution.py:286
  403.1 34.9 %all_to_all.51.back_ref = bf16[64,1,4,2048]{3,2,1,0:T(4,128)(2,1)S(1)} all-to-all(bf16[64,1,4,2048]{3,2,1,0:T(4,128)(2,1)S(1)} %shard_map.87), channel_id=1, replica_groups=mesh['section'=4,'expert'=64] {'expert'}, dimensions={0} | all-to-all | bytes 2097152 | tf_op jit(solution)/shard_map/all_to_all | solution.py:330
  446.4 34.8 %all_to_all.52.rows_ref = bf16[64,1,4,2048]{3,2,1,0:T(4,128)(2,1)S(1)} all-to-all(bf16[64,1,4,2048]{3,2,1,0:T(4,128)(2,1)S(1)} %get-tuple-element.31), channel_id=1, replica_groups=mesh['section'=4,'expert'=64] {'expert'}, dimensions={0} | all-to-all | bytes 2097152 | tf_op jit(solution)/shard_map/all_to_all | solution.py:330
  481.3 6.1 %shard_map.90 = bf16[64,1,4,2048]{3,2,1,0:T(4,128)(2,1)S(1)} custom-call(s32[1]{0:T(128)} %bitcast.section_ref, bf16[64,1,4,2048]{3,2,1,0:T(4,128)(2,1)S(1)} %all_to_all.52.rows_ref, bf16[16128,256]{1,0:T(8,128)(2,1)} %get-tuple-element.21.refs_0_, bf16[2304,256]{1,0:T(8,128)(2,1)S(1)} %get-tuple-element.22.refs_1_, ...), custom_call_target="tpu_custom_call" | custom-call | flops 2415919104 | bytes 11534336 | tf_op jit(solution)/shard_map/pallas_call | solution.py:286
  487.3 34.5 %all_to_all.53.back_ref = bf16[64,1,4,2048]{3,2,1,0:T(4,128)(2,1)S(1)} all-to-all(bf16[64,1,4,2048]{3,2,1,0:T(4,128)(2,1)S(1)} %shard_map.90), channel_id=1, replica_groups=mesh['section'=4,'expert'=64] {'expert'}, dimensions={0} | all-to-all | bytes 2097152 | tf_op jit(solution)/shard_map/all_to_all | solution.py:330
  (153 shorter events, 107.8 us)
Async XLA Ops:
  0.0 8.3 %collective-permute-start.5 = (bf16[32,2048]{1,0:T(8,128)(2,1)}, bf16[32,2048]{1,0:T(8,128)(2,1)S(1)}, u32[]{:S(2)}, u32[]{:S(2)}) collective-permute-start(bf16[32,2048]{1,0:T(8,128)(2,1)} %bitcast.29), channel_id=1, source_target_pairs={{128,0},{129,1},{130,2},{131,3},{132,4},{133,5},{134,6},{135,7},{1... | collective-permute-start | bytes 393224 | tf_op jit(solution)/shard_map/ppermute | solution.py:327
  1.4 6.9 %collective-permute-start = (f32[1,2048]{1,0:T(1,128)}, f32[1,2048]{1,0:T(1,128)S(1)}, u32[]{:S(2)}, u32[]{:S(2)}) collective-permute-start(f32[1,2048]{1,0:T(1,128)} %refs_0_.9), channel_id=1, source_target_pairs={{64,0},{128,64},{192,128},{0,192},{65,1},{129,65},{193,129},{1,193... | collective-permute-start | bytes 24584 | tf_op jit(solution)/shard_map/ppermute | solution.py:327
  11.6 42.4 %all-to-all-start = ((bf16[64,1,4,2048]{3,2,1,0:T(4,128)(2,1)}), bf16[64,1,4,2048]{3,2,1,0:T(4,128)(2,1)S(1)}, u32[]{:S(2)}, u32[]{:S(2)}) async-start(bf16[64,1,4,2048]{3,2,1,0:T(4,128)(2,1)} %get-tuple-element.19), calls=%async_computation | async-start | bytes 2097152 | tf_op jit(solution)/shard_map/all_to_all | solution.py:330
  25.5 10.9 %collective-permute-start.4 = (bf16[32,2048]{1,0:T(8,128)(2,1)S(1)}, bf16[32,2048]{1,0:T(8,128)(2,1)S(1)}, u32[]{:S(2)}, u32[]{:S(2)}) collective-permute-start(bf16[32,2048]{1,0:T(8,128)(2,1)S(1)} %bitcast.31), channel_id=1, source_target_pairs={{64,0},{65,1},{66,2},{67,3},{68,4},{69,5},{70,6},{71,7},{72,8},{73... | collective-permute-start | bytes 393224 | tf_op jit(solution)/shard_map/ppermute | solution.py:327
  26.8 9.6 %collective-permute-start.1 = (f32[1,2048]{1,0:T(1,128)S(1)}, f32[1,2048]{1,0:T(1,128)S(1)}, u32[]{:S(2)}, u32[]{:S(2)}) collective-permute-start(f32[1,2048]{1,0:T(1,128)S(1)} %copy-done.38), channel_id=1, source_target_pairs={{64,128},{128,192},{192,0},{0,64},{65,129},{129,193},{193,1},{1,65... | collective-permute-start | bytes 24584 | tf_op jit(solution)/shard_map/ppermute | solution.py:327
  29.0 4.6 collective-permute-start.3
  31.8 4.6 collective-permute-start.7
  45.7 178.9 %collective-permute-start.11 = (bf16[16128,256]{1,0:T(8,128)(2,1)}, bf16[16128,256]{1,0:T(8,128)(2,1)}, u32[]{:S(2)}, u32[]{:S(2)}) collective-permute-start(bf16[16128,256]{1,0:T(8,128)(2,1)} %get-tuple-element.21.refs_0_), channel_id=1, source_target_pairs={{64,0},{128,64},{192,128},{65,1},{129,65},{193,129},{66,2},{130,66... | collective-permute-start | bytes 24772616 | tf_op jit(solution)/shard_map/ppermute | solution.py:327
  47.0 177.6 %collective-permute-start.12 = (bf16[16128,256]{1,0:T(8,128)(2,1)}, bf16[16128,256]{1,0:T(8,128)(2,1)}, u32[]{:S(2)}, u32[]{:S(2)}) collective-permute-start(bf16[16128,256]{1,0:T(8,128)(2,1)} %get-tuple-element.21.refs_0_), channel_id=1, source_target_pairs={{64,128},{128,192},{65,129},{129,193},{66,130},{130,194},{67,131},... | collective-permute-start | bytes 24772616 | tf_op jit(solution)/shard_map/ppermute | solution.py:327
  61.1 37.9 %all-to-all-start.1 = ((bf16[64,1,4,2048]{3,2,1,0:T(4,128)(2,1)}), bf16[64,1,4,2048]{3,2,1,0:T(4,128)(2,1)}, u32[]{:S(2)}, u32[]{:S(2)}) async-start(bf16[64,1,4,2048]{3,2,1,0:T(4,128)(2,1)} %shard_map.75), calls=%async_computation.1 | async-start | bytes 2097152 | tf_op jit(solution)/shard_map/all_to_all | solution.py:330
  70.5 27.4 %collective-permute-start.8 = (bf16[64,1,4,2048]{3,2,1,0:T(4,128)(2,1)S(1)}, bf16[64,1,4,2048]{3,2,1,0:T(4,128)(2,1)S(1)}, u32[]{:S(2)}, u32[]{:S(2)}) collective-permute-start(bf16[64,1,4,2048]{3,2,1,0:T(4,128)(2,1)S(1)} %all-to-all-done.rows_ref), channel_id=1, source_target_pairs={{192,0},{193,1},{194,2},{195,3},{196,4},{197,5},{198,6},{199,7},{2... | collective-permute-start | bytes 3145736 | tf_op jit(solution)/shard_map/ppermute | solution.py:327
  101.8 7.8 %collective-permute-start.9 = (bf16[32,2048]{1,0:T(8,128)(2,1)S(1)}, bf16[32,2048]{1,0:T(8,128)(2,1)S(1)}, u32[]{:S(2)}, u32[]{:S(2)}) collective-permute-start(bf16[32,2048]{1,0:T(8,128)(2,1)S(1)} %shard_map.76), channel_id=1, source_target_pairs={{0,64},{1,65},{2,66},{3,67},{4,68},{5,69},{6,70},{7,71},{8,72},{9,... | collective-permute-start | bytes 393224 | tf_op jit(solution)/shard_map/ppermute | solution.py:327
  114.6 57.8 %all-to-all-start.2 = ((bf16[64,2,4,2048]{3,2,1,0:T(4,128)(2,1)}), bf16[64,2,4,2048]{3,2,1,0:T(4,128)(2,1)}, u32[]{:S(2)}, u32[]{:S(2)}) async-start(bf16[64,2,4,2048]{3,2,1,0:T(4,128)(2,1)} %copy-done.19), calls=%async_computation.2 | async-start | bytes 4194304 | tf_op jit(solution)/shard_map/all_to_all | solution.py:330
  127.4 23.4 %collective-permute-start.10 = (bf16[64,1,4,2048]{3,2,1,0:T(4,128)(2,1)S(1)}, bf16[64,1,4,2048]{3,2,1,0:T(4,128)(2,1)S(1)}, u32[]{:S(2)}, u32[]{:S(2)}) collective-permute-start(bf16[64,1,4,2048]{3,2,1,0:T(4,128)(2,1)S(1)} %shard_map.78), channel_id=1, source_target_pairs={{0,192},{1,193},{2,194},{3,195},{4,196},{5,197},{6,198},{7,199},{8... | collective-permute-start | bytes 3145736 | tf_op jit(solution)/shard_map/ppermute | solution.py:327
  128.7 207.2 %collective-permute-start.16 = (bf16[16128,256]{1,0:T(8,128)(2,1)}, bf16[16128,256]{1,0:T(8,128)(2,1)}, u32[]{:S(2)}, u32[]{:S(2)}) collective-permute-start(bf16[16128,256]{1,0:T(8,128)(2,1)} %get-tuple-element.21.refs_0_), channel_id=1, source_target_pairs={{192,0},{193,1},{194,2},{195,3},{196,4},{197,5},{198,6},{199,7},{2... | collective-permute-start | bytes 24772616 | tf_op jit(solution)/shard_map/ppermute | solution.py:327
  184.0 57.1 %all-to-all-start.3 = ((bf16[64,2,4,2048]{3,2,1,0:T(4,128)(2,1)}), bf16[64,2,4,2048]{3,2,1,0:T(4,128)(2,1)S(1)}, u32[]{:S(2)}, u32[]{:S(2)}) async-start(bf16[64,2,4,2048]{3,2,1,0:T(4,128)(2,1)} %copy-done.20), calls=%async_computation.3 | async-start | bytes 4194304 | tf_op jit(solution)/shard_map/all_to_all | solution.py:330
  244.7 6.6 %collective-permute-start.13 = (bf16[32,2048]{1,0:T(8,128)(2,1)S(1)}, bf16[32,2048]{1,0:T(8,128)(2,1)S(1)}, u32[]{:S(2)}, u32[]{:S(2)}) collective-permute-start(bf16[32,2048]{1,0:T(8,128)(2,1)S(1)} %get-tuple-element.25), channel_id=1, source_target_pairs={{0,64},{64,192},{192,128},{1,65},{65,193},{193,129},{2,66},{66,194... | collective-permute-start | bytes 393224 | tf_op jit(solution)/shard_map/ppermute | solution.py:327
  253.6 36.7 %all-to-all-start.4 = ((bf16[64,1,4,2048]{3,2,1,0:T(4,128)(2,1)}), bf16[64,1,4,2048]{3,2,1,0:T(4,128)(2,1)}, u32[]{:S(2)}, u32[]{:S(2)}) async-start(bf16[64,1,4,2048]{3,2,1,0:T(4,128)(2,1)} %get-tuple-element.27), calls=%async_computation.4 | async-start | bytes 2097152 | tf_op jit(solution)/shard_map/all_to_all | solution.py:330
  260.3 30.1 %collective-permute-start.14 = (bf16[2304,256]{1,0:T(8,128)(2,1)S(1)}, bf16[2304,256]{1,0:T(8,128)(2,1)S(1)}, u32[]{:S(2)}, u32[]{:S(2)}) collective-permute-start(bf16[2304,256]{1,0:T(8,128)(2,1)S(1)} %get-tuple-element.22.refs_1_), channel_id=1, source_target_pairs={{64,0},{128,64},{192,128},{65,1},{129,65},{193,129},{66,2},{130,66... | collective-permute-start | bytes 3538952 | tf_op jit(solution)/shard_map/ppermute | solution.py:327
  261.6 28.8 %collective-permute-start.15 = (bf16[2304,256]{1,0:T(8,128)(2,1)S(1)}, bf16[2304,256]{1,0:T(8,128)(2,1)S(1)}, u32[]{:S(2)}, u32[]{:S(2)}) collective-permute-start(bf16[2304,256]{1,0:T(8,128)(2,1)S(1)} %get-tuple-element.22.refs_1_), channel_id=1, source_target_pairs={{64,128},{128,192},{65,129},{129,193},{66,130},{130,194},{67,131},... | collective-permute-start | bytes 3538952 | tf_op jit(solution)/shard_map/ppermute | solution.py:327
  262.3 73.6 %collective-permute-start.17 = (bf16[2304,256]{1,0:T(8,128)(2,1)S(1)}, bf16[2304,256]{1,0:T(8,128)(2,1)}, u32[]{:S(2)}, u32[]{:S(2)}) collective-permute-start(bf16[2304,256]{1,0:T(8,128)(2,1)S(1)} %get-tuple-element.22.refs_1_), channel_id=1, source_target_pairs={{192,0},{193,1},{194,2},{195,3},{196,4},{197,5},{198,6},{199,7},{2... | collective-permute-start | bytes 3538952 | tf_op jit(solution)/shard_map/ppermute | solution.py:327
  298.7 39.6 %all-to-all-start.5 = ((bf16[64,1,4,2048]{3,2,1,0:T(4,128)(2,1)}), bf16[64,1,4,2048]{3,2,1,0:T(4,128)(2,1)}, u32[]{:S(2)}, u32[]{:S(2)}) async-start(bf16[64,1,4,2048]{3,2,1,0:T(4,128)(2,1)} %copy-done.8), calls=%async_computation.5 | async-start | bytes 2097152 | tf_op jit(solution)/shard_map/all_to_all | solution.py:330
  346.8 9.7 %collective-permute-start.18 = (bf16[32,2048]{1,0:T(8,128)(2,1)S(1)}, bf16[32,2048]{1,0:T(8,128)(2,1)S(1)}, u32[]{:S(2)}, u32[]{:S(2)}) collective-permute-start(bf16[32,2048]{1,0:T(8,128)(2,1)S(1)} %shard_map.85.refs_7_), channel_id=1, source_target_pairs={{0,192},{192,0},{1,193},{193,1},{2,194},{194,2},{3,195},{195,3},{4... | collective-permute-start | bytes 393224 | tf_op jit(solution)/shard_map/ppermute | solution.py:327
  438.7 7.0 %collective-permute-start.19 = (bf16[32,2048]{1,0:T(8,128)(2,1)S(1)}, bf16[32,2048]{1,0:T(8,128)(2,1)S(1)}, u32[]{:S(2)}, u32[]{:S(2)}) collective-permute-start(bf16[32,2048]{1,0:T(8,128)(2,1)S(1)} %shard_map.88.refs_7_), channel_id=1, source_target_pairs={{64,0},{0,64},{65,1},{1,65},{66,2},{2,66},{67,3},{3,67},{68,4},{4,... | collective-permute-start | bytes 393224 | tf_op jit(solution)/shard_map/ppermute | solution.py:327
  (52 other events, 1360.4 us)

commit v5 on v4

--- a/solution.py
+++ b/solution.py
@@ -125,6 +125,57 @@
         copy.start()
     for copy in copies:
         copy.wait()
+
+
+def tables_kernel(kinds, experts, section_ref, *refs):
+    section = section_ref[0]
+    gains, ids, raw = refs[:kinds], refs[kinds : 2 * kinds], refs[2 * kinds : 3 * kinds]
+    outs = iter(refs[3 * kinds :])
+    for step in range(1, len(PAIRS)):
+        gain_ref, placing_ref, scale_ref = next(outs), next(outs), next(outs)
+        layer = looked_up(LAYERS[step], section)
+        gain_ref[...] = picked([ref[...] for ref in gains], layer)
+        for lane, table in enumerate(PAIRS[step]):
+            pair = looked_up(table, section)
+            named = of_pair(ids, layer, pair)
+            weights = of_pair(raw, layer, pair)
+            weights = weights / jnp.sum(weights, axis=-1, keepdims=True)
+            placing_ref[lane] = chosen_places(named, experts).T.astype(jnp.bfloat16)
+            scale = chosen_places(named, experts, weights)
+            high = scale.astype(jnp.bfloat16)
+            scale_ref[lane, 0] = high
+            scale_ref[lane, 1] = (scale - high.astype(jnp.float32)).astype(jnp.bfloat16)
+
+
+def dispatch_by_table_kernel(step, counts, section_ref, gain_ref, placing_ref, *refs):
+    section = section_ref[0]
+    hidden_ref, out_ref = refs[-2:]
+    for lane, count in enumerate(counts):
+        candidates, refs = refs[:count], refs[count:]
+        hidden = picked([ref[...] for ref in candidates], looked_up(TAKES[step][lane], section))
+        hidden_ref[lane] = hidden
+        values = hidden.astype(jnp.float32)
+        inverse = lax.rsqrt(jnp.mean(values * values, axis=-1, keepdims=True) + EPSILON)
+        normed = (values * inverse * gain_ref[...]).astype(jnp.bfloat16)
+        sent = jnp.dot(placing_ref[lane], normed, preferred_element_type=jnp.float32)
+        out_ref[:, lane] = sent.astype(jnp.bfloat16).reshape(out_ref.shape[0], GROUP, sent.shape[-1])
+
+
+def combine_by_table_kernel(last, section_ref, back_ref, hidden_ref, scale_ref, *refs):
+    experts, lanes, _, features = back_ref.shape
+    outs = refs[-lanes:]
+    for lane in range(lanes):
+        back = back_ref[:, lane].reshape(experts * GROUP, features)
+        mixed = jnp.dot(scale_ref[lane, 0], back, preferred_element_type=jnp.float32)
+        mixed += jnp.dot(scale_ref[lane, 1], back, preferred_element_type=jnp.float32)
+        made = (hidden_ref[lane].astype(jnp.float32) + mixed).astype(jnp.bfloat16)
+        if last is None:
+            outs[lane][...] = made
+        else:
+            made = jnp.where(section_ref[0] == last, refs[0][...], made)
+            block = made.shape[0] // 2
+            outs[lane][0] = made[block:]
+            outs[lane][1] = made[:block]
 
 
 def ffn_kernel(step, given, held, section_ref, rows_ref, *refs):
@@ -244,6 +295,54 @@
     )(section, *operands, *ties)
 
 
+def tables(experts, section, gains, ids, raw):
+    rows = 2 * ids[0].shape[1]
+    width = experts * GROUP
+    shapes = []
+    for lanes in map(len, PAIRS[1:]):
+        shapes.append(jax.ShapeDtypeStruct(gains[0].shape, jnp.float32))
+        shapes.append(jax.ShapeDtypeStruct((lanes, width, rows), jnp.bfloat16))
+        shapes.append(jax.ShapeDtypeStruct((lanes, 2, rows, width), jnp.bfloat16))
+    made = pl.pallas_call(
+        functools.partial(tables_kernel, len(gains), experts),
+        out_shape=tuple(shapes),
+        in_specs=[SMEM] + [VMEM] * (3 * len(gains)),
+        out_specs=tuple(VMEM for _ in shapes),
+        cost_estimate=pl.CostEstimate(flops=LONG // 4, bytes_accessed=4096, transcendentals=0),
+        compiler_params=limit(12),
+    )(section, *gains, *ids, *raw)
+    return [None] + [made[start : start + 3] for start in range(0, len(made), 3)]
+
+
+def dispatch_by_table(step, experts, section, table, lanes, ties=()):
+    rows, features = lanes[0][0].shape
+    counts = tuple(len(lane) for lane in lanes)
+    operands = (*table[:2], *(value for lane in lanes for value in lane))
+    return pl.pallas_call(
+        functools.partial(dispatch_by_table_kernel, step, counts),
+        out_shape=(
+            jax.ShapeDtypeStruct((len(lanes), rows, features), jnp.bfloat16),
+            jax.ShapeDtypeStruct((experts, len(lanes), GROUP, features), jnp.bfloat16),
+        ),
+        in_specs=[SMEM] + [VMEM] * len(operands) + [WHEREVER] * len(ties),
+        out_specs=(VMEM, VMEM),
+        compiler_params=limit(12),
+    )(section, *operands, *ties)
+
+
+def combine_by_table(section, back, hidden, table, ties=(), last=None, finished=()):
+    lanes, rows, features = hidden.shape
+    shape = (rows, features) if last is None else (2, rows // 2, features)
+    operands = (back, hidden, table[2], *finished)
+    return pl.pallas_call(
+        functools.partial(combine_by_table_kernel, last),
+        out_shape=tuple(jax.ShapeDtypeStruct(shape, jnp.bfloat16) for _ in range(lanes)),
+        in_specs=[SMEM] + [VMEM] * len(operands) + [WHEREVER] * len(ties),
+        out_specs=tuple(VMEM for _ in range(lanes)),
+        compiler_params=limit(12),
+    )(section, *operands, *ties)
+
+
 def token_kernel(*refs):
     refs[-1][...] = jnp.zeros_like(refs[-1])
 
@@ -348,32 +447,33 @@
     rows = exchange(sent)
     away = move(rows, (3, 0))
     made = exchange(ffn(0, at, rows, [layer]))
-    (state,) = combine(0, experts, at, made, hidden, ids[:1], raw[:1], (away,))
+    table = tables(experts, at, gains, ids, raw)
+    (state,) = combine(0, experts, at, made, hidden, ids[:1], raw[:1], (away, table[1][0]))
     state = move(state, (0, 1))
 
     away = move(ffn(0, at, away, [layer]), (0, 3))
-    hidden, sent = dispatch(1, experts, at, gains[:1], ids[:1], [(own,), (own, second_in, state)])
+    hidden, sent = dispatch_by_table(1, experts, at, table[1], [(own,), (own, second_in, state)])
     made = ffn(1, at, exchange(sent), [layer], 3, (away,))
     here = arrived_token(LONGER, upper[0], lower_early[0])
-    kept, state = combine(1, experts, at, exchange(made), hidden, ids[:2], raw[:2], (here,))
+    kept, state = combine_by_table(at, exchange(made), hidden, table[1], (here,))
     state = move(state, (0, 1), (1, 3), (3, 2))
 
     layers = [layer, upper, lower_early]
-    hidden, sent = dispatch(2, experts, at, gains, ids, [(state, kept)])
+    hidden, sent = dispatch_by_table(2, experts, at, table[2], [(state, kept)])
     made = exchange(ffn(2, at, exchange(sent), layers))
     here = arrived_token(LONG, *lower_late)
-    (kept,) = combine(2, experts, at, made, hidden, ids, raw, (here,))
+    (kept,) = combine_by_table(at, made, hidden, table[2], (here,))
     state = move(kept, (0, 3), (3, 0))
 
     layers.append(lower_late)
-    hidden, sent = dispatch(3, experts, at, gains, ids, [(state, kept)])
+    hidden, sent = dispatch_by_table(3, experts, at, table[3], [(state, kept)])
     made = exchange(ffn(3, at, exchange(sent), layers))
-    (kept,) = combine(3, experts, at, made, hidden, ids, raw)
+    (kept,) = combine_by_table(at, made, hidden, table[3])
     state = move(kept, (1, 0), (0, 1))
 
-    hidden, sent = dispatch(4, experts, at, gains, ids, [(state, kept)])
+    hidden, sent = dispatch_by_table(4, experts, at, table[4], [(state, kept)])
     made = exchange(ffn(4, at, exchange(sent), layers))
-    (finished,) = combine(4, experts, at, made, hidden, ids, raw, (), 1, (state,))
+    (finished,) = combine_by_table(at, made, hidden, table[4], (), 1, (state,))
     return finished
 
 

time: 525 us -> 515 us (0.981)
  waiting for transfers between devices: 199 us -> 189 us
    pallas_call x0 -> x9, Pallas kernels: none -> 9.64 us  [the longest x4 4.13 us: combine_by_table(): pl.pallas_call(functools.partial(combine_by_table_kernel, last), out_shap...]
    ppermute x20, waiting for transfers between devices: 155 us -> 148 us  [move(): return lax.ppermute(value, 'section', route)]
    unnamed x102 -> x92, local copies, waits for them, and re-layouts: 29.6 us -> 26.9 us
  transfers between devices with their start and end apart: 26 -> 26, of which waited for: 17 -> 16; matrix products, arithmetic and copies ran while one was open for 0% -> 0% of each run, Pallas kernels for 8% -> 8%
where the time goes in v5:
time: 515 us; the launch traced here: 513 us
  waiting for transfers between devices  189 us (37%)
  blocking collectives  142 us (28%)
  starting transfers between devices  94.4 us (18%)
  Pallas kernels  60 us (12%)
  local copies, waits for them, and re-layouts  26.9 us (5%)
    ppermute x20, waiting for transfers between devices, move(): return lax.ppermute(value, 'section', route)  148 us
    all_to_all x4, blocking collectives, exchange(): lax.all_to_all(value, 'expert', split_axis=0, concat_axis=0, tiled=True)  142 us
    all_to_all x6, starting transfers between devices, exchange(): lax.all_to_all(value, 'expert', split_axis=0, concat_axis=0, tiled=True)  53.4 us
    pallas_call x6, Pallas kernels, ffn(): pl.pallas_call(functools.partial(ffn_kernel, step, given, held), out_shap...  42.6 us
    ppermute x20, starting transfers between devices, move(): return lax.ppermute(value, 'section', route)  40.9 us
    all_to_all x6, waiting for transfers between devices, exchange(): lax.all_to_all(value, 'expert', split_axis=0, concat_axis=0, tiled=True)  40.9 us
    unnamed x92, local copies, waits for them, and re-layouts  26.9 us
  transfers between devices with their start and end apart: 26, of which 16 were waited for; matrix products, arithmetic and copies ran while one was open for 0% of the time, Pallas kernels for 8%

profile of v5, /device:TPU:1, one launch (start us, length us, event | category | flops | bytes accessed | tf_op | source)
XLA Modules:
  0.0 512.6 jit_solution(10355917736476847297)
XLA Ops:
  11.6 13.9 %all-to-all-start = ((bf16[64,1,4,2048]{3,2,1,0:T(4,128)(2,1)}), bf16[64,1,4,2048]{3,2,1,0:T(4,128)(2,1)S(1)}, u32[]{:S(2)}, u32[]{:S(2)}) async-start(bf16[64,1,4,2048]{3,2,1,0:T(4,128)(2,1)} %get-tuple-element.39), calls=%async_computation | async-start | bytes 2097152 | tf_op jit(solution)/shard_map/all_to_all | solution.py:429
  54.0 7.0 %shard_map.76 = bf16[64,1,4,2048]{3,2,1,0:T(4,128)(2,1)} custom-call(s32[1]{0:T(128)} %bitcast.section_ref, bf16[64,1,4,2048]{3,2,1,0:T(4,128)(2,1)S(1)} %all-to-all-done.rows_ref, bf16[16128,256]{1,0:T(8,128)(2,1)} %get-tuple-element.41.refs_0_, bf16[2304,256]{1,0:T(8,128)(2,1)S(1)} %get-tuple-element.42.refs_1_), custom_call_target="tpu_custom_call" | custom-call | flops 2415919104 | bytes 11534336 | tf_op jit(solution)/shard_map/pallas_call | solution.py:385
  61.0 9.3 %all-to-all-start.1 = ((bf16[64,1,4,2048]{3,2,1,0:T(4,128)(2,1)}), bf16[64,1,4,2048]{3,2,1,0:T(4,128)(2,1)}, u32[]{:S(2)}, u32[]{:S(2)}) async-start(bf16[64,1,4,2048]{3,2,1,0:T(4,128)(2,1)} %shard_map.76), calls=%async_computation.1 | async-start | bytes 2097152 | tf_op jit(solution)/shard_map/all_to_all | solution.py:429
  82.9 14.9 %collective-permute-done.8.refs_2_.rows_ref = bf16[64,1,4,2048]{3,2,1,0:T(4,128)(2,1)S(1)} collective-permute-done((bf16[64,1,4,2048]{3,2,1,0:T(4,128)(2,1)S(1)}, bf16[64,1,4,2048]{3,2,1,0:T(4,128)(2,1)S(1)}, u32[]{:S(2)}, u32[]{:S(2)}) %collective-permute-start.8) | collective-permute-done | bytes 1048608 | tf_op jit(solution)/shard_map/ppermute | solution.py:426
  113.2 6.7 %all-to-all-start.2 = ((bf16[64,2,4,2048]{3,2,1,0:T(4,128)(2,1)}), bf16[64,2,4,2048]{3,2,1,0:T(4,128)(2,1)}, u32[]{:S(2)}, u32[]{:S(2)}) async-start(bf16[64,2,4,2048]{3,2,1,0:T(4,128)(2,1)} %copy-done.4), calls=%async_computation.2 | async-start | bytes 4194304 | tf_op jit(solution)/shard_map/all_to_all | solution.py:429
  119.9 6.1 %shard_map.79 = bf16[64,1,4,2048]{3,2,1,0:T(4,128)(2,1)S(1)} custom-call(s32[1]{0:T(128)} %bitcast.section_ref, bf16[64,1,4,2048]{3,2,1,0:T(4,128)(2,1)S(1)} %collective-permute-done.8.refs_2_.rows_ref, bf16[16128,256]{1,0:T(8,128)(2,1)} %get-tuple-element.41.refs_0_, bf16[2304,256]{1,0:T(8,128)(2,1)S(1)} %get-tuple-element.42.refs_1_), custom_call_target="tpu_custom_call" | custom-call | flops 2415919104 | bytes 11534336 | tf_op jit(solution)/shard_map/pallas_call | solution.py:385
  128.6 20.9 %collective-permute-done.10.refs_2_ = bf16[64,1,4,2048]{3,2,1,0:T(4,128)(2,1)S(1)} collective-permute-done((bf16[64,1,4,2048]{3,2,1,0:T(4,128)(2,1)S(1)}, bf16[64,1,4,2048]{3,2,1,0:T(4,128)(2,1)S(1)}, u32[]{:S(2)}, u32[]{:S(2)}) %collective-permute-start.10) | collective-permute-done | bytes 1048608 | tf_op jit(solution)/shard_map/ppermute | solution.py:426
  149.6 21.5 %all-to-all-done.2.rows_ref = bf16[64,2,4,2048]{3,2,1,0:T(4,128)(2,1)} async-done(((bf16[64,2,4,2048]{3,2,1,0:T(4,128)(2,1)}), bf16[64,2,4,2048]{3,2,1,0:T(4,128)(2,1)}, u32[]{:S(2)}, u32[]{:S(2)}) %all-to-all-start.2) | async-done | bytes 2097184 | tf_op jit(solution)/shard_map/all_to_all | solution.py:429
  171.1 10.2 %shard_map.80 = bf16[64,2,4,2048]{3,2,1,0:T(4,128)(2,1)S(1)} custom-call(s32[1]{0:T(128)} %bitcast.section_ref, bf16[64,2,4,2048]{3,2,1,0:T(4,128)(2,1)} %all-to-all-done.2.rows_ref, bf16[16128,256]{1,0:T(8,128)(2,1)} %get-tuple-element.41.refs_0_, bf16[2304,256]{1,0:T(8,128)(2,1)S(1)} %get-tuple-element.42.refs_1_, ...), custom_call_target="tpu_custom_call" | custom-call | flops 4831838208 | bytes 13631488 | tf_op jit(solution)/shard_map/pallas_call | solution.py:385
  182.6 5.8 %all-to-all-start.3 = ((bf16[64,2,4,2048]{3,2,1,0:T(4,128)(2,1)}), bf16[64,2,4,2048]{3,2,1,0:T(4,128)(2,1)S(1)}, u32[]{:S(2)}, u32[]{:S(2)}) async-start(bf16[64,2,4,2048]{3,2,1,0:T(4,128)(2,1)} %copy-done.5), calls=%async_computation.3 | async-start | bytes 4194304 | tf_op jit(solution)/shard_map/all_to_all | solution.py:429
  188.4 36.1 %collective-permute-done.11.refs_0_.refs_2_ = bf16[16128,256]{1,0:T(8,128)(2,1)} collective-permute-done((bf16[16128,256]{1,0:T(8,128)(2,1)}, bf16[16128,256]{1,0:T(8,128)(2,1)}, u32[]{:S(2)}, u32[]{:S(2)}) %collective-permute-start.11) | collective-permute-done | bytes 8257568 | tf_op jit(solution)/shard_map/ppermute | solution.py:426
  224.5 15.1 %all-to-all-done.3.back_ref = bf16[64,2,4,2048]{3,2,1,0:T(4,128)(2,1)S(1)} async-done(((bf16[64,2,4,2048]{3,2,1,0:T(4,128)(2,1)}), bf16[64,2,4,2048]{3,2,1,0:T(4,128)(2,1)S(1)}, u32[]{:S(2)}, u32[]{:S(2)}) %all-to-all-start.3) | async-done | bytes 2097184 | tf_op jit(solution)/shard_map/all_to_all | solution.py:429
  250.1 6.6 %all-to-all-start.4 = ((bf16[64,1,4,2048]{3,2,1,0:T(4,128)(2,1)}), bf16[64,1,4,2048]{3,2,1,0:T(4,128)(2,1)}, u32[]{:S(2)}, u32[]{:S(2)}) async-start(bf16[64,1,4,2048]{3,2,1,0:T(4,128)(2,1)} %get-tuple-element.48), calls=%async_computation.4 | async-start | bytes 2097152 | tf_op jit(solution)/shard_map/all_to_all | solution.py:429
  260.1 26.7 %collective-permute-done.14.refs_3_ = bf16[2304,256]{1,0:T(8,128)(2,1)S(1)} collective-permute-done((bf16[2304,256]{1,0:T(8,128)(2,1)S(1)}, bf16[2304,256]{1,0:T(8,128)(2,1)S(1)}, u32[]{:S(2)}, u32[]{:S(2)}) %collective-permute-start.14) | collective-permute-done | bytes 1179680 | tf_op jit(solution)/shard_map/ppermute | solution.py:426
  286.8 7.3 %shard_map.84 = bf16[64,1,4,2048]{3,2,1,0:T(4,128)(2,1)S(1)} custom-call(s32[1]{0:T(128)} %bitcast.section_ref, bf16[64,1,4,2048]{3,2,1,0:T(4,128)(2,1)} %all-to-all-done.4.rows_ref, bf16[16128,256]{1,0:T(8,128)(2,1)} %get-tuple-element.41.refs_0_, bf16[2304,256]{1,0:T(8,128)(2,1)S(1)} %get-tuple-element.42.refs_1_, ...), custom_call_target="tpu_custom_call" | custom-call | flops 2415919104 | bytes 11534336 | tf_op jit(solution)/shard_map/pallas_call | solution.py:385
  295.1 11.1 %all-to-all-start.5 = ((bf16[64,1,4,2048]{3,2,1,0:T(4,128)(2,1)}), bf16[64,1,4,2048]{3,2,1,0:T(4,128)(2,1)}, u32[]{:S(2)}, u32[]{:S(2)}) async-start(bf16[64,1,4,2048]{3,2,1,0:T(4,128)(2,1)} %copy-done), calls=%async_computation.5 | async-start | bytes 2097152 | tf_op jit(solution)/shard_map/all_to_all | solution.py:429
  306.3 28.4 %collective-permute-done.17.refs_1_.refs_7_ = bf16[2304,256]{1,0:T(8,128)(2,1)} collective-permute-done((bf16[2304,256]{1,0:T(8,128)(2,1)S(1)}, bf16[2304,256]{1,0:T(8,128)(2,1)}, u32[]{:S(2)}, u32[]{:S(2)}) %collective-permute-start.17) | collective-permute-done | bytes 1179680 | tf_op jit(solution)/shard_map/ppermute | solution.py:426
  338.1 5.9 %collective-permute-start.18 = (bf16[32,2048]{1,0:T(8,128)(2,1)S(1)}, bf16[32,2048]{1,0:T(8,128)(2,1)S(1)}, u32[]{:S(2)}, u32[]{:S(2)}) collective-permute-start(bf16[32,2048]{1,0:T(8,128)(2,1)S(1)} %shard_map.86.refs_1_), channel_id=1, source_target_pairs={{0,192},{192,0},{1,193},{193,1},{2,194},{194,2},{3,195},{195,3},{4... | collective-permute-start | bytes 393224 | tf_op jit(solution)/shard_map/ppermute | solution.py:426
  349.0 38.3 %all_to_all.50.rows_ref = bf16[64,1,4,2048]{3,2,1,0:T(4,128)(2,1)S(1)} all-to-all(bf16[64,1,4,2048]{3,2,1,0:T(4,128)(2,1)S(1)} %get-tuple-element.51), channel_id=1, replica_groups=mesh['section'=4,'expert'=64] {'expert'}, dimensions={0} | all-to-all | bytes 2097152 | tf_op jit(solution)/shard_map/all_to_all | solution.py:429
  387.2 6.1 %shard_map.88 = bf16[64,1,4,2048]{3,2,1,0:T(4,128)(2,1)S(1)} custom-call(s32[1]{0:T(128)} %bitcast.section_ref, bf16[64,1,4,2048]{3,2,1,0:T(4,128)(2,1)S(1)} %all_to_all.50.rows_ref, bf16[16128,256]{1,0:T(8,128)(2,1)} %get-tuple-element.41.refs_0_, bf16[2304,256]{1,0:T(8,128)(2,1)S(1)} %get-tuple-element.42.refs_1_, ...), custom_call_target="tpu_custom_call" | custom-call | flops 2415919104 | bytes 11534336 | tf_op jit(solution)/shard_map/pallas_call | solution.py:385
  393.3 34.7 %all_to_all.51.back_ref = bf16[64,1,4,2048]{3,2,1,0:T(4,128)(2,1)S(1)} all-to-all(bf16[64,1,4,2048]{3,2,1,0:T(4,128)(2,1)S(1)} %shard_map.88), channel_id=1, replica_groups=mesh['section'=4,'expert'=64] {'expert'}, dimensions={0} | all-to-all | bytes 2097152 | tf_op jit(solution)/shard_map/all_to_all | solution.py:429
  436.0 34.8 %all_to_all.52.rows_ref = bf16[64,1,4,2048]{3,2,1,0:T(4,128)(2,1)S(1)} all-to-all(bf16[64,1,4,2048]{3,2,1,0:T(4,128)(2,1)S(1)} %get-tuple-element.54), channel_id=1, replica_groups=mesh['section'=4,'expert'=64] {'expert'}, dimensions={0} | all-to-all | bytes 2097152 | tf_op jit(solution)/shard_map/all_to_all | solution.py:429
  470.8 6.1 %shard_map.91 = bf16[64,1,4,2048]{3,2,1,0:T(4,128)(2,1)S(1)} custom-call(s32[1]{0:T(128)} %bitcast.section_ref, bf16[64,1,4,2048]{3,2,1,0:T(4,128)(2,1)S(1)} %all_to_all.52.rows_ref, bf16[16128,256]{1,0:T(8,128)(2,1)} %get-tuple-element.41.refs_0_, bf16[2304,256]{1,0:T(8,128)(2,1)S(1)} %get-tuple-element.42.refs_1_, ...), custom_call_target="tpu_custom_call" | custom-call | flops 2415919104 | bytes 11534336 | tf_op jit(solution)/shard_map/pallas_call | solution.py:385
  476.9 34.5 %all_to_all.53.back_ref = bf16[64,1,4,2048]{3,2,1,0:T(4,128)(2,1)S(1)} all-to-all(bf16[64,1,4,2048]{3,2,1,0:T(4,128)(2,1)S(1)} %shard_map.91), channel_id=1, replica_groups=mesh['section'=4,'expert'=64] {'expert'}, dimensions={0} | all-to-all | bytes 2097152 | tf_op jit(solution)/shard_map/all_to_all | solution.py:429
  (144 shorter events, 104.1 us)
Async XLA Ops:
  0.0 8.3 %collective-permute-start.7 = (bf16[32,2048]{1,0:T(8,128)(2,1)}, bf16[32,2048]{1,0:T(8,128)(2,1)S(1)}, u32[]{:S(2)}, u32[]{:S(2)}) collective-permute-start(bf16[32,2048]{1,0:T(8,128)(2,1)} %bitcast.10), channel_id=1, source_target_pairs={{128,0},{129,1},{130,2},{131,3},{132,4},{133,5},{134,6},{135,7},{1... | collective-permute-start | bytes 393224 | tf_op jit(solution)/shard_map/ppermute | solution.py:426
  1.4 6.9 %collective-permute-start = (f32[1,2048]{1,0:T(1,128)}, f32[1,2048]{1,0:T(1,128)S(1)}, u32[]{:S(2)}, u32[]{:S(2)}) collective-permute-start(f32[1,2048]{1,0:T(1,128)} %refs_0_.3), channel_id=1, source_target_pairs={{64,0},{128,64},{192,128},{0,192},{65,1},{129,65},{193,129},{1,193... | collective-permute-start | bytes 24584 | tf_op jit(solution)/shard_map/ppermute | solution.py:426
  11.6 42.4 %all-to-all-start = ((bf16[64,1,4,2048]{3,2,1,0:T(4,128)(2,1)}), bf16[64,1,4,2048]{3,2,1,0:T(4,128)(2,1)S(1)}, u32[]{:S(2)}, u32[]{:S(2)}) async-start(bf16[64,1,4,2048]{3,2,1,0:T(4,128)(2,1)} %get-tuple-element.39), calls=%async_computation | async-start | bytes 2097152 | tf_op jit(solution)/shard_map/all_to_all | solution.py:429
  25.5 10.9 %collective-permute-start.6 = (bf16[32,2048]{1,0:T(8,128)(2,1)S(1)}, bf16[32,2048]{1,0:T(8,128)(2,1)S(1)}, u32[]{:S(2)}, u32[]{:S(2)}) collective-permute-start(bf16[32,2048]{1,0:T(8,128)(2,1)S(1)} %bitcast.12), channel_id=1, source_target_pairs={{64,0},{65,1},{66,2},{67,3},{68,4},{69,5},{70,6},{71,7},{72,8},{73... | collective-permute-start | bytes 393224 | tf_op jit(solution)/shard_map/ppermute | solution.py:426
  26.8 9.6 %collective-permute-start.1 = (f32[1,2048]{1,0:T(1,128)}, f32[1,2048]{1,0:T(1,128)S(1)}, u32[]{:S(2)}, u32[]{:S(2)}) collective-permute-start(f32[1,2048]{1,0:T(1,128)} %refs_0_.3), channel_id=1, source_target_pairs={{64,128},{128,192},{192,0},{0,64},{65,129},{129,193},{193,1},{1,65... | collective-permute-start | bytes 24584 | tf_op jit(solution)/shard_map/ppermute | solution.py:426
  28.9 4.6 collective-permute-start.3
  31.7 4.6 collective-permute-start.5
  45.6 178.9 %collective-permute-start.11 = (bf16[16128,256]{1,0:T(8,128)(2,1)}, bf16[16128,256]{1,0:T(8,128)(2,1)}, u32[]{:S(2)}, u32[]{:S(2)}) collective-permute-start(bf16[16128,256]{1,0:T(8,128)(2,1)} %get-tuple-element.41.refs_0_), channel_id=1, source_target_pairs={{64,0},{128,64},{192,128},{65,1},{129,65},{193,129},{66,2},{130,66... | collective-permute-start | bytes 24772616 | tf_op jit(solution)/shard_map/ppermute | solution.py:426
  46.9 177.6 %collective-permute-start.12 = (bf16[16128,256]{1,0:T(8,128)(2,1)}, bf16[16128,256]{1,0:T(8,128)(2,1)}, u32[]{:S(2)}, u32[]{:S(2)}) collective-permute-start(bf16[16128,256]{1,0:T(8,128)(2,1)} %get-tuple-element.41.refs_0_), channel_id=1, source_target_pairs={{64,128},{128,192},{65,129},{129,193},{66,130},{130,194},{67,131},... | collective-permute-start | bytes 24772616 | tf_op jit(solution)/shard_map/ppermute | solution.py:426
  61.0 37.8 %all-to-all-start.1 = ((bf16[64,1,4,2048]{3,2,1,0:T(4,128)(2,1)}), bf16[64,1,4,2048]{3,2,1,0:T(4,128)(2,1)}, u32[]{:S(2)}, u32[]{:S(2)}) async-start(bf16[64,1,4,2048]{3,2,1,0:T(4,128)(2,1)} %shard_map.76), calls=%async_computation.1 | async-start | bytes 2097152 | tf_op jit(solution)/shard_map/all_to_all | solution.py:429
  70.4 27.4 %collective-permute-start.8 = (bf16[64,1,4,2048]{3,2,1,0:T(4,128)(2,1)S(1)}, bf16[64,1,4,2048]{3,2,1,0:T(4,128)(2,1)S(1)}, u32[]{:S(2)}, u32[]{:S(2)}) collective-permute-start(bf16[64,1,4,2048]{3,2,1,0:T(4,128)(2,1)S(1)} %all-to-all-done.rows_ref), channel_id=1, source_target_pairs={{192,0},{193,1},{194,2},{195,3},{196,4},{197,5},{198,6},{199,7},{2... | collective-permute-start | bytes 3145736 | tf_op jit(solution)/shard_map/ppermute | solution.py:426
  101.7 7.8 %collective-permute-start.9 = (bf16[32,2048]{1,0:T(8,128)(2,1)S(1)}, bf16[32,2048]{1,0:T(8,128)(2,1)S(1)}, u32[]{:S(2)}, u32[]{:S(2)}) collective-permute-start(bf16[32,2048]{1,0:T(8,128)(2,1)S(1)} %shard_map.77), channel_id=1, source_target_pairs={{0,64},{1,65},{2,66},{3,67},{4,68},{5,69},{6,70},{7,71},{8,72},{9,... | collective-permute-start | bytes 393224 | tf_op jit(solution)/shard_map/ppermute | solution.py:426
  113.2 57.8 %all-to-all-start.2 = ((bf16[64,2,4,2048]{3,2,1,0:T(4,128)(2,1)}), bf16[64,2,4,2048]{3,2,1,0:T(4,128)(2,1)}, u32[]{:S(2)}, u32[]{:S(2)}) async-start(bf16[64,2,4,2048]{3,2,1,0:T(4,128)(2,1)} %copy-done.4), calls=%async_computation.2 | async-start | bytes 4194304 | tf_op jit(solution)/shard_map/all_to_all | solution.py:429
  126.0 23.6 %collective-permute-start.10 = (bf16[64,1,4,2048]{3,2,1,0:T(4,128)(2,1)S(1)}, bf16[64,1,4,2048]{3,2,1,0:T(4,128)(2,1)S(1)}, u32[]{:S(2)}, u32[]{:S(2)}) collective-permute-start(bf16[64,1,4,2048]{3,2,1,0:T(4,128)(2,1)S(1)} %shard_map.79), channel_id=1, source_target_pairs={{0,192},{1,193},{2,194},{3,195},{4,196},{5,197},{6,198},{7,199},{8... | collective-permute-start | bytes 3145736 | tf_op jit(solution)/shard_map/ppermute | solution.py:426
  127.3 207.4 %collective-permute-start.16 = (bf16[16128,256]{1,0:T(8,128)(2,1)}, bf16[16128,256]{1,0:T(8,128)(2,1)}, u32[]{:S(2)}, u32[]{:S(2)}) collective-permute-start(bf16[16128,256]{1,0:T(8,128)(2,1)} %get-tuple-element.41.refs_0_), channel_id=1, source_target_pairs={{192,0},{193,1},{194,2},{195,3},{196,4},{197,5},{198,6},{199,7},{2... | collective-permute-start | bytes 24772616 | tf_op jit(solution)/shard_map/ppermute | solution.py:426
  182.6 57.1 %all-to-all-start.3 = ((bf16[64,2,4,2048]{3,2,1,0:T(4,128)(2,1)}), bf16[64,2,4,2048]{3,2,1,0:T(4,128)(2,1)S(1)}, u32[]{:S(2)}, u32[]{:S(2)}) async-start(bf16[64,2,4,2048]{3,2,1,0:T(4,128)(2,1)} %copy-done.5), calls=%async_computation.3 | async-start | bytes 4194304 | tf_op jit(solution)/shard_map/all_to_all | solution.py:429
  241.3 6.6 %collective-permute-start.13 = (bf16[32,2048]{1,0:T(8,128)(2,1)S(1)}, bf16[32,2048]{1,0:T(8,128)(2,1)S(1)}, u32[]{:S(2)}, u32[]{:S(2)}) collective-permute-start(bf16[32,2048]{1,0:T(8,128)(2,1)S(1)} %get-tuple-element.46), channel_id=1, source_target_pairs={{0,64},{64,192},{192,128},{1,65},{65,193},{193,129},{2,66},{66,194... | collective-permute-start | bytes 393224 | tf_op jit(solution)/shard_map/ppermute | solution.py:426
  250.1 36.7 %all-to-all-start.4 = ((bf16[64,1,4,2048]{3,2,1,0:T(4,128)(2,1)}), bf16[64,1,4,2048]{3,2,1,0:T(4,128)(2,1)}, u32[]{:S(2)}, u32[]{:S(2)}) async-start(bf16[64,1,4,2048]{3,2,1,0:T(4,128)(2,1)} %get-tuple-element.48), calls=%async_computation.4 | async-start | bytes 2097152 | tf_op jit(solution)/shard_map/all_to_all | solution.py:429
  256.8 30.1 %collective-permute-start.14 = (bf16[2304,256]{1,0:T(8,128)(2,1)S(1)}, bf16[2304,256]{1,0:T(8,128)(2,1)S(1)}, u32[]{:S(2)}, u32[]{:S(2)}) collective-permute-start(bf16[2304,256]{1,0:T(8,128)(2,1)S(1)} %get-tuple-element.42.refs_1_), channel_id=1, source_target_pairs={{64,0},{128,64},{192,128},{65,1},{129,65},{193,129},{66,2},{130,66... | collective-permute-start | bytes 3538952 | tf_op jit(solution)/shard_map/ppermute | solution.py:426
  258.1 28.8 %collective-permute-start.15 = (bf16[2304,256]{1,0:T(8,128)(2,1)S(1)}, bf16[2304,256]{1,0:T(8,128)(2,1)S(1)}, u32[]{:S(2)}, u32[]{:S(2)}) collective-permute-start(bf16[2304,256]{1,0:T(8,128)(2,1)S(1)} %get-tuple-element.42.refs_1_), channel_id=1, source_target_pairs={{64,128},{128,192},{65,129},{129,193},{66,130},{130,194},{67,131},... | collective-permute-start | bytes 3538952 | tf_op jit(solution)/shard_map/ppermute | solution.py:426
  258.8 75.9 %collective-permute-start.17 = (bf16[2304,256]{1,0:T(8,128)(2,1)S(1)}, bf16[2304,256]{1,0:T(8,128)(2,1)}, u32[]{:S(2)}, u32[]{:S(2)}) collective-permute-start(bf16[2304,256]{1,0:T(8,128)(2,1)S(1)} %get-tuple-element.42.refs_1_), channel_id=1, source_target_pairs={{192,0},{193,1},{194,2},{195,3},{196,4},{197,5},{198,6},{199,7},{2... | collective-permute-start | bytes 3538952 | tf_op jit(solution)/shard_map/ppermute | solution.py:426
  295.1 39.6 %all-to-all-start.5 = ((bf16[64,1,4,2048]{3,2,1,0:T(4,128)(2,1)}), bf16[64,1,4,2048]{3,2,1,0:T(4,128)(2,1)}, u32[]{:S(2)}, u32[]{:S(2)}) async-start(bf16[64,1,4,2048]{3,2,1,0:T(4,128)(2,1)} %copy-done), calls=%async_computation.5 | async-start | bytes 2097152 | tf_op jit(solution)/shard_map/all_to_all | solution.py:429
  338.1 9.5 %collective-permute-start.18 = (bf16[32,2048]{1,0:T(8,128)(2,1)S(1)}, bf16[32,2048]{1,0:T(8,128)(2,1)S(1)}, u32[]{:S(2)}, u32[]{:S(2)}) collective-permute-start(bf16[32,2048]{1,0:T(8,128)(2,1)S(1)} %shard_map.86.refs_1_), channel_id=1, source_target_pairs={{0,192},{192,0},{1,193},{193,1},{2,194},{194,2},{3,195},{195,3},{4... | collective-permute-start | bytes 393224 | tf_op jit(solution)/shard_map/ppermute | solution.py:426
  428.5 7.0 %collective-permute-start.19 = (bf16[32,2048]{1,0:T(8,128)(2,1)S(1)}, bf16[32,2048]{1,0:T(8,128)(2,1)S(1)}, u32[]{:S(2)}, u32[]{:S(2)}) collective-permute-start(bf16[32,2048]{1,0:T(8,128)(2,1)S(1)} %shard_map.89.refs_1_), channel_id=1, source_target_pairs={{64,0},{0,64},{65,1},{1,65},{66,2},{2,66},{67,3},{3,67},{68,4},{4,... | collective-permute-start | bytes 393224 | tf_op jit(solution)/shard_map/ppermute | solution.py:426
  (47 other events, 449.6 us)
